TPU v7x, 128 devices: a whole 4x4x4 slice. The times are simulated.
128 devices in a mesh: lat: 8 (over z, core), lon: 16 (over x, y).
Axes of the slice: x: 4, y: 4, z: 4, core: 2. Of those that a mesh axis runs over, the one named last changes fastest.
Arguments:
- sea_height: float32 [512, 4096], P('lat', 'lon'), may hold values from -7.5 to 10
- trans_u: float32 [512, 4096], P('lat', 'lon'), may hold values from -3 to 3
- trans_v: float32 [512, 4096], P('lat', 'lon'), may hold values from -3 to 3
- depth: float32 [512, 4096], P('lat', 'lon'), may hold values from 0.2 to 1
- sea_mask: int32 [512, 4096], P('lat', 'lon'), may hold values 0 or 1
- freshwater_flux: float32 [512, 4096], P('lat', 'lon'), may hold values from -2 to 6
- love_factor: float32 [1024], replicated, may hold values from 0.5 to 10.8
Outputs:
- height_out: float32 [512, 4096], P('lat', 'lon')
- trans_u_out: float32 [512, 4096], P('lat', 'lon')
- trans_v_out: float32 [512, 4096], P('lat', 'lon')
- sal_height: float32 [512, 4096], P('lat', 'lon')
All inputs are finite; a program needn't handle non-finite values. No bound on the sum of `sea_mask` on one device may be relied on, other than what follows from the above.
Results may differ from a plain program's by a relative error of at most 0.0003.
Values sent between devices are 32-bit elements; how exact they have to be, the bound alone decides.
No kernel may reach another device: no remote copies, remote signals or barrier semaphores. Data moves between devices by JAX's collectives and lax.ppermute only.
A program may use at most 128 MiB of HBM per device.

v0:
```python
import math

import jax
import jax.numpy as jnp
from jax import lax
from jax.sharding import PartitionSpec as P

ITERS = 4


step_time = 0.5
sal_ratio = 3.0 * 1035.0 / 5517.0
block_steps = 64


def padded_2(block, sides, width):
    for axis, dim in sides:
        count = lax.axis_size(axis)
        forward = [(i, i + 1) for i in range(count - 1)]
        forward.append((count - 1, 0))
        backward = [(target, source) for source, target in forward]
        low = lax.ppermute(
            lax.slice_in_dim(block, block.shape[dim] - width, None, axis=dim), axis, forward
        )
        high = lax.ppermute(lax.slice_in_dim(block, 0, width, axis=dim), axis, backward)
        block = jnp.concatenate([low, block, high], axis=dim)
    return block


def seed_table(degrees):
    order_ids = jnp.arange(degrees, dtype=jnp.int32)
    order_f = order_ids.astype(jnp.float32)
    terms = jnp.where(
        order_ids > 0,
        jnp.log((2.0 * order_f + 1.0) / jnp.maximum(2.0 * order_f, 1.0)),
        0.0 * order_f,
    )
    values = 0.5 * math.log(2.0) + 0.5 * jnp.cumsum(terms)
    return jnp.where(order_ids == 0, 0.0 * order_f, values)


def row_latitudes(first_row, row_count, total_rows, spacing):
    row_ids = first_row + jnp.arange(row_count, dtype=jnp.int32)
    return (row_ids.astype(jnp.float32) + 0.5 - total_rows / 2) * spacing


def row_cosines(first_row, row_count, total_rows, spacing):
    latitude = row_latitudes(first_row, row_count, total_rows, spacing)
    return (jnp.cos(latitude), jnp.cos(latitude + spacing / 2))


def clear_outside(stacked, first_row, total_rows):
    row_ids = first_row + jnp.arange(stacked.shape[1], dtype=jnp.int32)
    inside = ((row_ids >= 0) & (row_ids < total_rows)).astype(jnp.float32)
    return stacked * inside[None, :, None]


def substep(fields, center_cos, north_cos):
    height, flux_u, flux_v, depth, sea_cells, forcing = fields
    inner_cos = center_cos[1:-1, None]
    north_flux = flux_v * north_cos[:, None]
    divergence = (flux_u[1:-1, 1:-1] - flux_u[1:-1, :-2]) / inner_cos + (
        north_flux[1:-1, 1:-1] - north_flux[:-2, 1:-1]
    ) / inner_cos
    height_mid = height[1:-1, 1:-1] - step_time * divergence + step_time * forcing[1:-1, 1:-1]
    depth_mid = depth[1:-1, 1:-1]
    sea_mid = sea_cells[1:-1, 1:-1]
    flux_u_mid = flux_u[1:-1, 1:-1]
    flux_v_mid = flux_v[1:-1, 1:-1]
    core_cos = center_cos[2:-2, None]
    new_u = (
        sea_mid[1:-1, 1:-1]
        * sea_mid[1:-1, 2:]
        * (
            flux_u_mid[1:-1, 1:-1]
            - step_time
            * 0.5
            * (depth_mid[1:-1, 1:-1] + depth_mid[1:-1, 2:])
            * (height_mid[1:-1, 2:] - height_mid[1:-1, 1:-1])
            / core_cos
        )
    )
    new_v = (
        sea_mid[1:-1, 1:-1]
        * sea_mid[2:, 1:-1]
        * (
            flux_v_mid[1:-1, 1:-1]
            - step_time
            * 0.5
            * (depth_mid[1:-1, 1:-1] + depth_mid[2:, 1:-1])
            * (height_mid[2:, 1:-1] - height_mid[1:-1, 1:-1])
        )
    )
    return (
        height_mid[1:-1, 1:-1],
        new_u,
        new_v,
        depth[2:-2, 2:-2],
        sea_cells[2:-2, 2:-2],
        forcing[2:-2, 2:-2],
    )


def tables(row_count, col_count, period):
    products = (
        jnp.arange(row_count, dtype=jnp.int32)[:, None]
        * jnp.arange(col_count, dtype=jnp.int32)[None, :]
        % period
    )
    angles = products.astype(jnp.float32) * (2.0 * math.pi / period)
    return (jnp.cos(angles), jnp.sin(angles))


def product(form, left, right):
    return jnp.einsum(form, left, right, precision=lax.Precision.HIGHEST)


def forward_transform(row_data, degrees):
    row_count, width_lon = row_data.shape
    factor = math.isqrt(width_lon)
    blocks = degrees // factor
    outer_cos, outer_sin = tables(factor, factor, factor)
    twist_cos, twist_sin = tables(factor, factor, width_lon)
    inner_cos, inner_sin = tables(factor, blocks, factor)
    row_grid = row_data.reshape(row_count, factor, factor)
    first_cos = product("rab,am->rmb", row_grid, outer_cos)
    first_sin = product("rab,am->rmb", row_grid, outer_sin)
    turned_cos = first_cos * twist_cos - first_sin * twist_sin
    turned_sin = first_cos * twist_sin + first_sin * twist_cos
    part_cos = product("rmb,bk->rkm", turned_cos, inner_cos) - product(
        "rmb,bk->rkm", turned_sin, inner_sin
    )
    part_sin = product("rmb,bk->rkm", turned_cos, inner_sin) + product(
        "rmb,bk->rkm", turned_sin, inner_cos
    )
    return (part_cos.reshape(row_count, degrees), part_sin.reshape(row_count, degrees))


def inverse_transform(amp_cos, amp_sin, width_lon):
    row_count, degrees = amp_cos.shape
    factor = math.isqrt(width_lon)
    blocks = degrees // factor
    outer_cos, outer_sin = tables(factor, factor, factor)
    twist_cos, twist_sin = tables(factor, factor, width_lon)
    order_cos, order_sin = tables(blocks, factor, factor)
    real_grid = amp_cos.reshape(row_count, blocks, factor)
    imag_grid = -amp_sin.reshape(row_count, blocks, factor)
    summed_re = product("rkm,kb->rmb", real_grid, order_cos) - product(
        "rkm,kb->rmb", imag_grid, order_sin
    )
    summed_im = product("rkm,kb->rmb", real_grid, order_sin) + product(
        "rkm,kb->rmb", imag_grid, order_cos
    )
    turned_re = summed_re * twist_cos - summed_im * twist_sin
    turned_im = summed_re * twist_sin + summed_im * twist_cos
    sal_field = product("rmb,ma->rab", turned_re, outer_cos) - product(
        "rmb,ma->rab", turned_im, outer_sin
    )
    return sal_field.reshape(row_count, width_lon)


def advance(previous, current, orders, sine_lat, degree_next):
    degree_f = orders + degree_next
    factor_a = jnp.sqrt((4.0 * degree_f * degree_f - 1.0) / (degree_f * degree_f - orders * orders))
    below = degree_f - 1.0
    factor_b = jnp.sqrt((below * below - orders * orders) / (4.0 * below * below - 1.0))
    return (current, factor_a * (sine_lat * current - factor_b * previous))


def analysis(orders, sine_lat, seed_values, weighted_cos, weighted_sin, lat_axis, degrees):
    order_list = orders.reshape(-1)
    coef_zero = jnp.zeros((degrees, order_list.shape[0]), jnp.float32)

    def analysis_one_block(block_index, loop_state):
        previous, current, coef_cos, coef_sin = loop_state
        first_degree = block_index * block_steps
        cos_rows = []
        sin_rows = []
        for offset in range(block_steps):
            degree = first_degree + offset
            in_range = (order_list + degree.astype(jnp.float32) <= degrees - 1).astype(jnp.float32)
            cos_rows.append(jnp.sum(weighted_cos * current, axis=lat_axis) * in_range)
            sin_rows.append(jnp.sum(weighted_sin * current, axis=lat_axis) * in_range)
            previous, current = advance(
                previous, current, orders, sine_lat, (degree + 1).astype(jnp.float32)
            )
        coef_cos = lax.dynamic_update_slice_in_dim(coef_cos, jnp.stack(cos_rows), first_degree, 0)
        coef_sin = lax.dynamic_update_slice_in_dim(coef_sin, jnp.stack(sin_rows), first_degree, 0)
        return (previous, current, coef_cos, coef_sin)

    start_state = (jnp.zeros_like(seed_values), seed_values, coef_zero, coef_zero)
    final_state = lax.fori_loop(0, degrees // block_steps, analysis_one_block, start_state)
    return (final_state[2], final_state[3])


def synthesis(orders, sine_lat, seed_values, coef_cos, coef_sin, degree_gain, first_order, degrees):
    order_count = orders.size

    def synthesis_one_block(block_index, loop_state):
        previous, current, amp_cos, amp_sin = loop_state
        first_degree = block_index * block_steps
        cos_block = lax.dynamic_slice_in_dim(coef_cos, first_degree, block_steps, 0)
        sin_block = lax.dynamic_slice_in_dim(coef_sin, first_degree, block_steps, 0)
        for offset in range(block_steps):
            degree = first_degree + offset
            scaled = lax.dynamic_slice_in_dim(degree_gain, first_order + degree, order_count)
            amp_cos = amp_cos + (scaled * cos_block[offset]).reshape(orders.shape) * current
            amp_sin = amp_sin + (scaled * sin_block[offset]).reshape(orders.shape) * current
            previous, current = advance(
                previous, current, orders, sine_lat, (degree + 1).astype(jnp.float32)
            )
        return (previous, current, amp_cos, amp_sin)

    zero_state = jnp.zeros_like(seed_values)
    final_state = lax.fori_loop(
        0,
        degrees // block_steps,
        synthesis_one_block,
        (zero_state, seed_values, zero_state, zero_state),
    )
    return (final_state[2], final_state[3])


def on_device(sea_height, trans_u, trans_v, depth, sea_mask, freshwater_flux, love_factor):
    tile_rows, tile_cols = sea_height.shape
    lat_count = lax.axis_size("lat")
    lon_count = lax.axis_size("lon")
    total_rows = tile_rows * lat_count
    width_lon = tile_cols * lon_count
    spacing = 2.0 * math.pi / width_lon
    sea_cells = sea_mask.astype(jnp.float32)
    lat_index = lax.axis_index("lat")
    lon_index = lax.axis_index("lon")
    first_row = lat_index * tile_rows
    center_cos, north_cos = row_cosines(first_row, tile_rows, total_rows, spacing)
    area_cells = sea_cells * center_cos[:, None]
    flux_sums = lax.psum(
        (jnp.sum(area_cells * freshwater_flux), jnp.sum(area_cells)), ("lat", "lon")
    )
    mean_flux = flux_sums[0] / flux_sums[1]
    forcing = sea_cells * (freshwater_flux - mean_flux)
    stacked = jnp.stack([sea_height, trans_u, trans_v, depth, sea_cells, forcing])
    center_pad, north_pad = row_cosines(first_row - 2, tile_rows + 4, total_rows, spacing)
    fields = tuple((stacked[slot] for slot in range(6)))
    for repeat in range(ITERS):
        padded = padded_2(jnp.stack(fields), (("lat", 1), ("lon", 2)), 2)
        padded = clear_outside(padded, first_row - 2, total_rows)
        fields = substep(tuple((padded[slot] for slot in range(6))), center_pad, north_pad)
    height = fields[0]
    sea_mass = sea_cells * sea_height
    owner_index = lat_index * lon_count + lon_index
    row_data = lax.all_to_all(sea_mass, "lon", split_axis=0, concat_axis=1, tiled=True)
    owner_rows = row_data.shape[0]
    degrees = love_factor.shape[0]
    part_cos, part_sin = forward_transform(row_data, degrees)
    seed_log = seed_table(degrees)
    degree_list = jnp.arange(degrees, dtype=jnp.int32).astype(jnp.float32)
    degree_gain = jnp.concatenate(
        [sal_ratio * love_factor / (2.0 * degree_list + 1.0), jnp.zeros((degrees,), jnp.float32)]
    )
    weight_scale = spacing * spacing / (4.0 * math.pi)
    orders = degree_list[None, :]
    latitude = row_latitudes(owner_index * owner_rows, owner_rows, total_rows, spacing)[:, None]
    cosines = jnp.cos(latitude)
    sine_lat = jnp.sin(latitude)
    seed_values = jnp.exp(seed_log[None, :] + orders * jnp.log(cosines))
    weights = cosines * weight_scale
    coef_cos, coef_sin = analysis(
        orders, sine_lat, seed_values, part_cos * weights, part_sin * weights, 0, degrees
    )
    coef_cos, coef_sin = lax.psum((coef_cos, coef_sin), ("lat", "lon"))
    amp_cos, amp_sin = synthesis(
        orders, sine_lat, seed_values, coef_cos, coef_sin, degree_gain, 0, degrees
    )
    sal_rows = inverse_transform(amp_cos, amp_sin, width_lon)
    sal_height = (
        lax.all_to_all(sal_rows, "lon", split_axis=1, concat_axis=0, tiled=True) * sea_cells
    )
    return (height, fields[1], fields[2], sal_height)


def solution(mesh):
    return jax.shard_map(
        on_device,
        mesh=mesh,
        in_specs=(
            P("lat", "lon"),
            P("lat", "lon"),
            P("lat", "lon"),
            P("lat", "lon"),
            P("lat", "lon"),
            P("lat", "lon"),
            P(),
        ),
        out_specs=(P("lat", "lon"), P("lat", "lon"), P("lat", "lon"), P("lat", "lon")),
        check_vma=False,
    )
```

profile of v0, /device:TPU:1, one launch (start us, length us, event | category | flops | bytes accessed | tf_op | source)
XLA Modules:
  0.0 722.5 jit_solution(9715157770581792007)
XLA Ops:
  8.7 7.6 %all-to-all-start = ((f32[16,4,256]{2,1,0:T(4,128)}), f32[16,4,256]{2,1,0:T(4,128)S(1)}, u32[]{:S(2)}, u32[]{:S(2)}) async-start(f32[16,4,256]{2,1,0:T(4,128)} %all_to_all.26), calls=%async_computation | async-start | bytes 131072 | tf_op jit(solution)/shard_map/all_to_all | solution.py:252
  17.6 5.2 all-to-all-done
  25.8 2.5 broadcast_in_dim.2
  28.3 2.5 broadcast_in_dim.2.clone
  30.8 122.5 %while.48 = (s32[]{:T(128)}, f32[4,1024]{1,0:T(4,128)S(1)}, f32[4,1024]{1,0:T(4,128)S(1)}, f32[1024,1024]{1,0:T(8,128)}, f32[1024,1024]{1,0:T(8,128)}, /*index=5...) while((s32[]{:T(128)}, f32[4,1024]{1,0:T(4,128)S(1)}, ...), condition=%wide.region_135.136_spmd.clone.clone, body=%wide.region_6.135_spmd.clone.clone.sunk | while | flops 3479704 | bytes 7527245 | solution.py:192
  154.3 161.2 %all-reduce.5.cloned.1.call-done = (f32[1024,1024]{1,0:T(8,128)}, f32[1024,1024]{1,0:T(8,128)}) async-done(((f32[1024,1024]{1,0:T(8,128)}, f32[1024,1024]{1,0:T(8,128)}), (f32[1024,1024]{1,0:T(8,128)}, f32[1024,1024]{1,0:T(8,128)})) %all-reduce.5.cloned.1.call-update) | async-done | bytes 8388624 | tf_op jit(solution)/shard_map/psum | solution.py:271
  315.4 256.5 %while.49 = (s32[]{:T(128)}, f32[4,1024]{1,0:T(4,128)S(1)}, f32[4,1024]{1,0:T(4,128)S(1)}, f32[4,1024]{1,0:T(4,128)S(1)}, f32[4,1024]{1,0:T(4,128)S(1)}, /*index...) while((s32[]{:T(128)}, f32[4,1024]{1,0:T(4,128)S(1)}, ...), condition=%wide.region_139.140_spmd.clone.clone, body=%wide.region_138.139_spmd.clone.clone.sunk | while | flops 4016533 | bytes 5983261 | solution.py:215
  322.3 1.6 constant_dynamic-slice_fusion.140
  332.8 1.4 constant_dynamic-slice_fusion.138
  334.2 1.4 constant_dynamic-slice_fusion.141
  348.8 1.4 constant_dynamic-slice_fusion.138
  350.2 1.4 constant_dynamic-slice_fusion.141
  363.3 1.5 constant_dynamic-slice_fusion.137
  364.8 1.4 constant_dynamic-slice_fusion.138
  366.2 1.4 constant_dynamic-slice_fusion.141
  367.6 1.4 constant_dynamic-slice_fusion.136
  399.4 1.4 constant_dynamic-slice_fusion.136
  412.7 1.4 constant_dynamic-slice_fusion.138
  415.5 1.4 constant_dynamic-slice_fusion.136
  427.3 1.4 constant_dynamic-slice_fusion.137
  428.7 1.4 constant_dynamic-slice_fusion.138
  430.1 1.4 constant_dynamic-slice_fusion.141
  431.5 1.4 constant_dynamic-slice_fusion.136
  443.3 1.4 constant_dynamic-slice_fusion.137
  447.5 1.5 constant_dynamic-slice_fusion.136
  452.0 1.4 constant_dynamic-slice_fusion.139
  459.4 1.4 constant_dynamic-slice_fusion.137
  460.9 1.4 constant_dynamic-slice_fusion.138
  463.7 1.4 constant_dynamic-slice_fusion.136
  475.4 1.4 constant_dynamic-slice_fusion.137
  476.8 1.4 constant_dynamic-slice_fusion.138
  478.2 1.4 constant_dynamic-slice_fusion.141
  479.7 1.4 constant_dynamic-slice_fusion.136
  491.5 1.4 constant_dynamic-slice_fusion.137
  492.9 1.4 constant_dynamic-slice_fusion.138
  494.4 1.4 constant_dynamic-slice_fusion.141
  495.8 1.4 constant_dynamic-slice_fusion.136
  500.1 1.4 constant_dynamic-slice_fusion.139
  509.0 1.4 constant_dynamic-slice_fusion.138
  511.8 1.4 constant_dynamic-slice_fusion.136
  514.7 1.4 constant_dynamic-slice_fusion.140
  525.1 1.4 constant_dynamic-slice_fusion.138
  527.9 1.4 constant_dynamic-slice_fusion.136
  539.6 1.4 constant_dynamic-slice_fusion.137
  542.4 1.4 constant_dynamic-slice_fusion.141
  555.5 1.5 constant_dynamic-slice_fusion.137
  557.0 1.5 constant_dynamic-slice_fusion.138
  559.8 1.6 constant_dynamic-slice_fusion.136
  575.4 5.0 all-to-all-start.1
  580.5 6.5 all-to-all-done.1
  588.3 64.4 %all-reduce.1 = (f32[]{:T(128)}, f32[]{:T(128)}) all-reduce(f32[]{:T(128)} %get-tuple-element.3797, f32[]{:T(128)} %get-tuple-element.3796), channel_id=1, replica_groups=mesh['lat'=8,'lon'=16] {'lat','lon'}, use_global_device_ids=true, to_apply=%region_1.0 | all-reduce | flops 2 | bytes 16 | tf_op jit(solution)/shard_map/psum | solution.py:237
  655.6 1.7 collective-permute-done.1
  658.5 3.8 collective-permute-start.3
  662.5 3.2 collective-permute-done.2
  667.2 2.5 collective-permute-start.4
  671.0 1.8 collective-permute-done.5
  673.0 5.4 collective-permute-start.7
  678.5 4.1 collective-permute-done.6
  688.5 5.4 collective-permute-start.11
  693.9 3.2 collective-permute-done.10
  698.6 2.2 collective-permute-start.12
  702.4 1.5 collective-permute-done.13
  704.2 5.4 collective-permute-start.15
  709.5 3.7 collective-permute-done.14
  (4981 shorter events, 301.8 us)
Async XLA Ops:
  8.7 14.1 %all-to-all-start = ((f32[16,4,256]{2,1,0:T(4,128)}), f32[16,4,256]{2,1,0:T(4,128)S(1)}, u32[]{:S(2)}, u32[]{:S(2)}) async-start(f32[16,4,256]{2,1,0:T(4,128)} %all_to_all.26), calls=%async_computation | async-start | bytes 131072 | tf_op jit(solution)/shard_map/all_to_all | solution.py:252
  16.3 299.1 %all-reduce.5.cloned.1.call-start = ((), (), s32[]{:S(2)}) async-start(), calls=%async_computation.2 | async-start | bytes 16777216 | tf_op jit(solution)/shard_map/psum | solution.py:271
  153.3 0.7 copy-start.7
  153.3 0.9 copy-start.2
  153.3 0.9 copy-start.4
  153.3 0.9 copy-start.5
  153.3 0.9 copy-start.6
  153.3 0.9 copy-start
  315.4 271.6 %copy-start.3 = (f32[64,256]{1,0:T(8,128)S(1)}, f32[64,256]{1,0:T(8,128)}, u32[]{:S(2)}) copy-start(f32[64,256]{1,0:T(8,128)} %param.16) | copy-start | bytes 196612
  575.4 11.6 %all-to-all-start.1 = ((f32[4,16,256]{2,0,1:T(4,128)}), f32[4,16,256]{2,0,1:T(4,128)S(1)}, u32[]{:S(2)}, u32[]{:S(2)}) async-start(f32[4,16,256]{2,0,1:T(4,128)} %copy.28), calls=%async_computation.1 | async-start | bytes 131072 | tf_op jit(solution)/shard_map/all_to_all | solution.py:277
  654.1 1.5 collective-permute-start
  654.2 3.1 collective-permute-start.1
  657.5 8.2 %collective-permute-start.2 = (f32[6,68,2]{2,1,0:T(8,128)S(1)}, f32[6,68,2]{2,1,0:T(8,128)S(1)}, u32[]{:S(2)}, u32[]{:S(2)}) collective-permute-start(f32[6,68,2]{2,1,0:T(8,128)S(1)} %get-tuple-element.4715), channel_id=1, source_target_pairs={{0,1},{1,2},{2,3},{3,4},{4,5},{5,6},{6,7},{7,8},{8,9},{9,10},{10,1... | collective-permute-start | bytes 9800 | tf_op jit(solution)/shard_map/ppermute | solution.py:22
  658.5 7.1 collective-permute-start.3
  667.2 3.8 collective-permute-start.4
  669.7 3.1 collective-permute-start.5
  673.0 9.6 %collective-permute-start.6 = (f32[6,68,2]{2,1,0:T(8,128)S(1)}, f32[6,68,2]{2,1,0:T(8,128)S(1)}, u32[]{:S(2)}, u32[]{:S(2)}) collective-permute-start(f32[6,68,2]{2,1,0:T(8,128)S(1)} %get-tuple-element.4713), channel_id=1, source_target_pairs={{0,1},{1,2},{2,3},{3,4},{4,5},{5,6},{6,7},{7,8},{8,9},{9,10},{10,1... | collective-permute-start | bytes 9800 | tf_op jit(solution)/shard_map/ppermute | solution.py:22
  673.0 9.5 %collective-permute-start.7 = (f32[6,68,2]{2,1,0:T(8,128)S(1)}, f32[6,68,2]{2,1,0:T(8,128)S(1)}, u32[]{:S(2)}, u32[]{:S(2)}) collective-permute-start(f32[6,68,2]{2,1,0:T(8,128)S(1)} %get-tuple-element.4714), channel_id=1, source_target_pairs={{1,0},{2,1},{3,2},{4,3},{5,4},{6,5},{7,6},{8,7},{9,8},{10,9},{11,1... | collective-permute-start | bytes 9800 | tf_op jit(solution)/shard_map/ppermute | solution.py:25
  684.1 2.9 collective-permute-start.8
  685.1 3.1 collective-permute-start.9
  688.4 8.7 %collective-permute-start.10 = (f32[6,68,2]{2,1,0:T(8,128)S(1)}, f32[6,68,2]{2,1,0:T(8,128)S(1)}, u32[]{:S(2)}, u32[]{:S(2)}) collective-permute-start(f32[6,68,2]{2,1,0:T(8,128)S(1)} %get-tuple-element.4711), channel_id=1, source_target_pairs={{0,1},{1,2},{2,3},{3,4},{4,5},{5,6},{6,7},{7,8},{8,9},{9,10},{10,1... | collective-permute-start | bytes 9800 | tf_op jit(solution)/shard_map/ppermute | solution.py:22
  688.5 8.6 %collective-permute-start.11 = (f32[6,68,2]{2,1,0:T(8,128)S(1)}, f32[6,68,2]{2,1,0:T(8,128)S(1)}, u32[]{:S(2)}, u32[]{:S(2)}) collective-permute-start(f32[6,68,2]{2,1,0:T(8,128)S(1)} %get-tuple-element.4712), channel_id=1, source_target_pairs={{1,0},{2,1},{3,2},{4,3},{5,4},{6,5},{7,6},{8,7},{9,8},{10,9},{11,1... | collective-permute-start | bytes 9800 | tf_op jit(solution)/shard_map/ppermute | solution.py:25
  698.6 3.8 collective-permute-start.12
  700.8 3.1 collective-permute-start.13
  704.1 9.2 %collective-permute-start.14 = (f32[6,68,2]{2,1,0:T(8,128)S(1)}, f32[6,68,2]{2,1,0:T(8,128)S(1)}, u32[]{:S(2)}, u32[]{:S(2)}) collective-permute-start(f32[6,68,2]{2,1,0:T(8,128)S(1)} %get-tuple-element.4709), channel_id=1, source_target_pairs={{0,1},{1,2},{2,3},{3,4},{4,5},{5,6},{6,7},{7,8},{8,9},{9,10},{10,1... | collective-permute-start | bytes 9800 | tf_op jit(solution)/shard_map/ppermute | solution.py:22
  704.2 9.1 %collective-permute-start.15 = (f32[6,68,2]{2,1,0:T(8,128)S(1)}, f32[6,68,2]{2,1,0:T(8,128)S(1)}, u32[]{:S(2)}, u32[]{:S(2)}) collective-permute-start(f32[6,68,2]{2,1,0:T(8,128)S(1)} %get-tuple-element.4710), channel_id=1, source_target_pairs={{1,0},{2,1},{3,2},{4,3},{5,4},{6,5},{7,6},{8,7},{9,8},{10,9},{11,1... | collective-permute-start | bytes 9800 | tf_op jit(solution)/shard_map/ppermute | solution.py:25
  714.8 0.8 copy-start.1
Sparse Core Ops, SparseCore 0:
  153.5 161.9 all-reduce.4
where the time goes:
time: 736 us; the launch traced here: 723 us
  waiting for transfers between devices  196 us (27%)
  local copies, waits for them, and re-layouts  192 us (26%)
  other arithmetic  159 us (22%)
  blocking collectives  64.4 us (9%)
  loops' own time  47.3 us (6%)
  starting transfers between devices  43.2 us (6%)
  between operations  16 us (2%)
    psum x1, waiting for transfers between devices, on_device(): coef_cos, coef_sin = lax.psum((coef_cos, coef_sin), ('lat', 'lon'))  161 us
    slice x64, local copies, waits for them, and re-layouts, synthesis_one_block(): sin_block[offset]  87 us
    slice x48, local copies, waits for them, and re-layouts, synthesis_one_block(): cos_block[offset]  65.9 us
    psum x1, blocking collectives, on_device(): lax.psum((jnp.sum(area_cells * freshwater_flux), jnp.sum(area_cells)), ('...  64.4 us
    another operation x1, loops' own time, analysis(): lax.fori_loop(0, degrees // block_steps, analysis_one_block, start_state)  27.8 us
    mul x224, other arithmetic, synthesis_one_block(): scaled * cos_block[offset]  27.5 us
    reduce_sum x64, other arithmetic, analysis_one_block(): sin_rows.append(jnp.sum(weighted_sin * current, axis=lat_axis) * in_range)  24.5 us
    ppermute x8, starting transfers between devices, padded_2(): lax.ppermute(lax.slice_in_dim(block, 0, width, axis=dim), axis, backward)  23.6 us

commit v1 on v0

v1 whole, which is shorter than its diff:
```python
import math

import jax
import jax.numpy as jnp
import ml_dtypes
import numpy as np
from jax import lax
from jax.experimental import pallas as pl
from jax.experimental.pallas import tpu as pltpu
from jax.sharding import PartitionSpec as P

ITERS = 4
NLON = 4096
NLAT = 512
DEG = 1024
LATS = 8
LONS = 16
DEVS = LATS * LONS
ROWS = NLAT // LATS
COLS = NLON // LONS
HALF = NLAT // 2
ORDERS = DEG // DEVS
WIDE = 4
FIELDS = 6
PAD_ROWS = ROWS + 2 * WIDE
PAD_COLS = COLS + 128
STRIP = FIELDS * WIDE
CHUNK = 128
CHUNKS = DEG // CHUNK

step_time = 0.5
sal_ratio = 3.0 * 1035.0 / 5517.0
spacing = 2.0 * math.pi / NLON

f32 = jnp.float32
bf16 = jnp.bfloat16


def split_table(values):
    high = values.astype(ml_dtypes.bfloat16)
    low = (values - high.astype(np.float64)).astype(ml_dtypes.bfloat16)
    return high, low


def wave_tables():
    order = (np.arange(DEVS)[:, None] + DEVS * np.arange(ORDERS)[None, :]).reshape(-1)
    angle = (order[:, None] * np.arange(COLS)[None, :] % NLON) * (2.0 * math.pi / NLON)
    cos_high, cos_low = split_table(np.cos(angle))
    sin_high, sin_low = split_table(np.sin(angle))
    return np.stack([cos_high, sin_high, cos_low, sin_low])


def phase_tables():
    angle = np.arange(LONS) * (2.0 * math.pi / LONS)
    return np.stack([np.cos(angle), np.sin(angle)]).astype(np.float32)


def latitude_of(rows):
    return (rows + 0.5 - NLAT / 2) * spacing


def row_tables():
    local = np.concatenate([np.arange(ROWS + WIDE), np.arange(-WIDE, 0)])
    latitude = latitude_of(np.arange(LATS)[:, None] * ROWS + local[None, :])
    both = np.stack([1.0 / np.cos(latitude), np.cos(latitude + spacing / 2)], axis=1)
    return np.broadcast_to(both[..., None], both.shape + (128,)).astype(np.float32)


def area_table():
    latitude = latitude_of(np.arange(NLAT)).reshape(LATS, ROWS, 1)
    return np.broadcast_to(np.cos(latitude), (LATS, ROWS, 128)).astype(np.float32)


def north_tables():
    latitude = latitude_of(np.arange(HALF, NLAT))
    weight = np.cos(latitude) * spacing * spacing / (4.0 * math.pi)
    table = np.stack([np.sin(latitude), np.log(np.cos(latitude)), weight])
    return np.broadcast_to(table[:, None, :], (3, 8, HALF)).astype(np.float32)


def seed_table():
    order = np.arange(1, DEG)
    grown = 0.5 * math.log(2.0) + 0.5 * np.cumsum(np.log((2.0 * order + 1.0) / (2.0 * order)))
    return np.concatenate([[0.0], grown]).reshape(ORDERS, DEVS).astype(np.float32)


def iota(shape, dim):
    return lax.broadcasted_iota(jnp.int32, shape, dim)


def halves(values):
    high = values.astype(bf16)
    low = (values - high.astype(f32)).astype(bf16)
    return high, low


def dot_nt(left, right):
    return lax.dot_general(left, right, (((1,), (1,)), ((), ())), preferred_element_type=f32)


def dot_nn(left, right):
    return lax.dot_general(left, right, (((1,), (0,)), ((), ())), preferred_element_type=f32)


def row_order(lat_index):
    row = iota((ROWS, ROWS), 0)
    col = iota((ROWS, ROWS), 1)
    south = lat_index < LATS // 2
    return jnp.where(south, (row + col == ROWS - 1).astype(f32), (row == col).astype(f32))


def reorder(matrix, values):
    return lax.dot_general(
        matrix,
        values,
        (((1,), (0,)), ((), ())),
        precision=lax.Precision.HIGHEST,
        preferred_element_type=f32,
    )


def forward_kernel(
    height, flux_u, flux_v, depth, mask, flux, wave, phase, area, message, strip_north, strip_south
):
    lat_index = lax.axis_index("lat")
    lon_index = lax.axis_index("lon")
    sea = mask[...].astype(f32)
    for slot, ref in enumerate((height, flux_u, flux_v, depth, None, flux)):
        values = sea if ref is None else ref[...]
        strip_north[slot * WIDE : (slot + 1) * WIDE, :] = values[ROWS - WIDE :, :]
        strip_south[slot * WIDE : (slot + 1) * WIDE, :] = values[:WIDE, :]

    mass = reorder(row_order(lat_index), sea * height[...])
    mass_high, mass_low = halves(mass)
    zero = jnp.zeros_like(mass_high)

    def sides(part):
        return (
            jnp.concatenate([part, zero, zero, part], axis=0),
            jnp.concatenate([zero, part, -part, zero], axis=0),
        )

    high_cos, high_sin = sides(mass_high)
    low_cos, low_sin = sides(mass_low)
    spectrum = (
        dot_nt(wave[0], high_cos)
        + dot_nt(wave[1], high_sin)
        + dot_nt(wave[0], low_cos)
        + dot_nt(wave[1], low_sin)
        + dot_nt(wave[2], high_cos)
        + dot_nt(wave[3], high_sin)
    )
    for device in range(DEVS):
        turn = (device % LONS) * lon_index % LONS
        part = spectrum[device * ORDERS : (device + 1) * ORDERS, :]
        message[device] = phase[0, turn] * part[:, :128] + phase[1, turn] * part[:, 128:]

    band = area[lat_index]
    area_cells = sea * jnp.concatenate([band, band], axis=1)
    flux_sum = jnp.sum(area_cells * flux[...])
    area_sum = jnp.sum(area_cells)
    row = iota((8, 128), 0)
    lane = iota((8, 128), 1)
    first = message[0]
    first = jnp.where((row == 0) & (lane >= 64), area_sum, first)
    message[0] = jnp.where((row == 0) & (lane == 64), flux_sum, first)


def table_kernel(north, seeds, high, low):
    device = lax.axis_index("lat") * LONS + lax.axis_index("lon")
    lane = iota((8, CHUNK), 1)
    row = iota((8, CHUNK), 0)
    seed_log = jnp.sum(jnp.where(lane == device, seeds[...], 0.0), axis=1, keepdims=True)
    order = (device + DEVS * row).astype(f32)
    sine = north[0]
    current = jnp.exp(seed_log + order[:, :1] * north[1])

    def one_chunk(chunk, state):
        previous, current = state
        step = (chunk * CHUNK + lane).astype(f32)
        below = order + step
        degree = below + 1.0
        factor_a = jnp.sqrt(
            (4.0 * degree * degree - 1.0) / ((step + 1.0) * (2.0 * order + step + 1.0))
        )
        factor_b = jnp.sqrt(
            step * (2.0 * order + step) / jnp.maximum(4.0 * below * below - 1.0, 1.0)
        )
        factor_c = factor_a * factor_b
        for pair in range(CHUNK // 2):
            kept = []
            for offset in range(2 * pair, 2 * pair + 2):
                kept.append(current)
                scaled = factor_a[:, offset : offset + 1] * sine
                behind = factor_c[:, offset : offset + 1] * previous
                previous, current = current, scaled * current - behind
            table_high, table_low = halves(jnp.concatenate(kept, axis=0))
            place = pl.ds(pl.multiple_of(chunk * (CHUNK * ORDERS) + 16 * pair, 16), 16)
            high[place, :] = table_high
            low[place, :] = table_low
        return previous, current

    lax.fori_loop(0, CHUNKS, one_chunk, (jnp.zeros_like(current), current))


def legendre_kernel(received, high, low, love, north, message, rows_scratch, gain_scratch, total):
    chunk = pl.program_id(0)
    device = lax.axis_index("lat") * LONS + lax.axis_index("lon")
    lane = iota((8, 128), 1)
    row = iota((8, 128), 0)
    left = lane < 64
    span = CHUNK * ORDERS

    @pl.when(chunk == 0)
    def _():
        bands = []
        for lat in range(LATS):
            band = received[lat * LONS]
            for lon in range(1, LONS):
                band = band + received[lat * LONS + lon]
            bands.append(band)
        whole = bands[0]
        for band in bands[1:]:
            whole = whole + band
        total[32:40, 0:128] = whole
        even = [bands[4 + part] + bands[3 - part] for part in range(4)]
        odd = [bands[4 + part] - bands[3 - part] for part in range(4)]

        def arrange(parts):
            cos_parts = []
            sin_parts = []
            for first, second in ((parts[0], parts[1]), (parts[2], parts[3])):
                cos_parts.append(jnp.where(left, first, pltpu.roll(second, 64, 1)))
                sin_parts.append(jnp.where(left, pltpu.roll(first, 64, 1), second))
            weight = north[2]
            return [
                jnp.concatenate(cos_parts, axis=1) * weight,
                jnp.concatenate(sin_parts, axis=1) * weight,
            ]

        rows = jnp.concatenate(arrange(even) + arrange(odd), axis=0)
        rows_high, rows_low = halves(rows)
        rows_scratch[0:32, :] = rows_high
        rows_scratch[32:64, :] = rows_low
        total[0:32, :] = jnp.zeros((32, HALF), f32)

        degree = (128 * row + lane).astype(f32)
        gain = sal_ratio * love[...] / (2.0 * degree + 1.0)
        turned = pltpu.roll(gain, (128 - device) % 128, 1)
        above = jnp.concatenate([turned[1:], jnp.zeros((1, 128), f32)], axis=0)
        shifted = jnp.where(lane + device < 128, turned, above)
        padded = jnp.concatenate([shifted, jnp.zeros((8, 128), f32)], axis=0)
        blocks = jnp.concatenate([padded[c : c + 8] for c in range(CHUNKS)], axis=0)
        blocks_high, blocks_low = halves(blocks)
        spread = (iota((CHUNK, span), 1) // ORDERS == iota((CHUNK, span), 0)).astype(f32).astype(bf16)
        wide = dot_nn(blocks_high, spread) + dot_nn(blocks_low, spread)
        gain_scratch[...] = wide.reshape(CHUNKS, ORDERS, span)

    rows_high = rows_scratch[0:32, :]
    both = dot_nt(rows_scratch[...], high[...])
    coefs = both[:32] + both[32:] + dot_nt(rows_high, low[...])
    gain = gain_scratch[chunk]
    column = iota((ORDERS, span), 1)
    gain = jnp.where(column % ORDERS == iota((ORDERS, span), 0), gain, 0.0)
    is_even = (column // ORDERS) % 2 == 0
    gain_even = jnp.where(is_even, gain, 0.0)
    gain_odd = gain - gain_even
    coefs = coefs * jnp.concatenate([gain_even, gain_even, gain_odd, gain_odd], axis=0)
    coefs_high, coefs_low = halves(coefs)
    both = dot_nn(jnp.concatenate([coefs_high, coefs_low], axis=0), high[...])
    total[0:32, :] += both[:32] + both[32:] + dot_nn(coefs_high, low[...])

    @pl.when(chunk == CHUNKS - 1)
    def _():
        sums = total[32:40, 0:128]
        flux_sum = jnp.sum(jnp.where((row == 0) & (lane == 64), sums, 0.0))
        area_sum = jnp.sum(jnp.where((row == 0) & (lane == 65), sums, 0.0))
        mean = jnp.full((8, 128), flux_sum, f32) / jnp.full((8, 128), area_sum, f32)
        slot = (device == 0) & (row == 0) & (lane >= 64)
        cos_even, sin_even = total[0:8, :], total[8:16, :]
        cos_odd, sin_odd = total[16:24, :], total[24:32, :]
        for north_side in (True, False):
            if north_side:
                cos_all, sin_all = cos_even + cos_odd, sin_even + sin_odd
            else:
                cos_all, sin_all = cos_even - cos_odd, sin_even - sin_odd
            for part in range(4):
                block = slice(128 * (part // 2), 128 * (part // 2) + 128)
                cos_part, sin_part = cos_all[:, block], sin_all[:, block]
                if part % 2 == 0:
                    sent = jnp.where(left, cos_part, pltpu.roll(sin_part, 64, 1))
                else:
                    sent = jnp.where(left, pltpu.roll(cos_part, 64, 1), sin_part)
                sent = jnp.where(slot, mean, sent)
                lat = 4 + part if north_side else 3 - part
                for lon in range(LONS):
                    message[lat * LONS + lon] = sent


def inverse_kernel(received, mask, wave, phase, sal_height, turned_scratch):
    lat_index = lax.axis_index("lat")
    lon_index = lax.axis_index("lon")
    sign = jnp.where(iota((8, 128), 1) < 64, 1.0, -1.0)
    for device in range(DEVS):
        turn = (device % LONS) * lon_index % LONS
        part = received[device]
        crossed = pltpu.roll(part, 64, 1) * sign
        turned_scratch[device * ORDERS : (device + 1) * ORDERS, :] = (
            phase[0, turn] * part + phase[1, turn] * crossed
        )
    turned = turned_scratch[...].T
    high, low = halves(turned)
    cos_both = jnp.concatenate([high[:64], low[:64]], axis=0)
    sin_both = jnp.concatenate([high[64:], low[64:]], axis=0)
    both = dot_nn(cos_both, wave[0]) + dot_nn(sin_both, wave[1])
    field = both[:64] + both[64:] + dot_nn(high[:64], wave[2]) + dot_nn(high[64:], wave[3])
    sal_height[...] = reorder(row_order(lat_index), field) * mask[...].astype(f32)


def column_kernel(
    height, flux_u, flux_v, depth, mask, flux, from_south, from_north, to_west, to_east, block
):
    lane = iota((128, 128), 1)
    west = jnp.zeros((128, 128), f32)
    east = jnp.zeros((128, 128), f32)
    block[PAD_ROWS:, :] = jnp.zeros((128 - PAD_ROWS, COLS), f32)
    for slot, ref in enumerate((height, flux_u, flux_v, depth, mask, flux)):
        block[0:ROWS, :] = ref[...].astype(f32)
        block[ROWS : ROWS + WIDE, :] = from_north[slot * WIDE : (slot + 1) * WIDE, :]
        block[ROWS + WIDE : PAD_ROWS, :] = from_south[slot * WIDE : (slot + 1) * WIDE, :]
        here = (lane >= slot * WIDE) & (lane < (slot + 1) * WIDE)
        west_part = block[:, 0:128]
        east_part = pltpu.roll(block[:, COLS - 128 : COLS], (WIDE + slot * WIDE) % 128, 1)
        if slot:
            west_part = pltpu.roll(west_part, slot * WIDE, 1)
        west = jnp.where(here, west_part, west)
        east = jnp.where(here, east_part, east)
    to_west[...] = west.T[:STRIP, :]
    to_east[...] = east.T[:STRIP, :]


def substep_kernel(
    height,
    flux_u,
    flux_v,
    depth,
    mask,
    flux,
    from_south,
    from_north,
    from_west,
    from_east,
    first_part,
    bands,
    height_out,
    u_out,
    v_out,
    block,
):
    lat_index = lax.axis_index("lat")
    row = iota((8, 128), 0)
    spot = iota((8, 128), 1)
    mean = jnp.sum(jnp.where((row == 0) & (spot == 64), first_part[0], 0.0))
    lane = iota((PAD_ROWS, 128), 1)
    fill = jnp.zeros((128 - STRIP, 128), f32)
    west = jnp.concatenate([from_west[...], fill], axis=0).T[:PAD_ROWS, :]
    east = jnp.concatenate([from_east[...], fill], axis=0).T[:PAD_ROWS, :]
    padded = []
    for slot, ref in enumerate((height, flux_u, flux_v, depth, mask, flux)):
        block[slot, 0:ROWS, 0:COLS] = ref[...].astype(f32)
        block[slot, ROWS : ROWS + WIDE, 0:COLS] = from_north[slot * WIDE : (slot + 1) * WIDE, :]
        block[slot, ROWS + WIDE : PAD_ROWS, 0:COLS] = from_south[slot * WIDE : (slot + 1) * WIDE, :]
        high_side = pltpu.roll(east, 128 - slot * WIDE, 1) if slot else east
        low_side = pltpu.roll(west, 128 - WIDE - slot * WIDE, 1)
        block[slot, :, COLS:] = jnp.where(
            lane < WIDE, high_side, jnp.where(lane >= 128 - WIDE, low_side, 0.0)
        )
        padded.append(block[slot])

    def eastward(values):
        return pltpu.roll(values, PAD_COLS - 1, 1)

    def northward(values):
        return pltpu.roll(values, PAD_ROWS - 1, 0)

    height_now, u_now, v_now, depth_all, sea, flux_all = padded
    inverse_cos = jnp.concatenate([bands[lat_index, 0]] * 3, axis=1)
    north_cos = jnp.concatenate([bands[lat_index, 1]] * 3, axis=1)
    forcing = step_time * sea * (flux_all - mean)
    open_u = sea * eastward(sea)
    open_v = sea * northward(sea)
    pull_u = open_u * (0.5 * step_time) * (depth_all + eastward(depth_all)) * inverse_cos
    pull_v = open_v * (0.5 * step_time) * (depth_all + northward(depth_all))
    scale = step_time * inverse_cos
    for repeat in range(ITERS):
        north_flux = v_now * north_cos
        divergence = u_now - pltpu.roll(u_now, 1, 1) + (north_flux - pltpu.roll(north_flux, 1, 0))
        height_now = height_now - scale * divergence + forcing
        u_now = open_u * u_now - pull_u * (eastward(height_now) - height_now)
        v_now = open_v * v_now - pull_v * (northward(height_now) - height_now)
    height_out[...] = height_now[:ROWS, :COLS]
    u_out[...] = u_now[:ROWS, :COLS]
    v_out[...] = v_now[:ROWS, :COLS]


def whole(space=pltpu.VMEM):
    return pl.BlockSpec(memory_space=space)


def shaped(*shape, kind=f32):
    return jax.ShapeDtypeStruct(shape, kind)


def cost(flops, moved):
    return pl.CostEstimate(flops=flops, bytes_accessed=moved, transcendentals=0)


def params(mebibytes=40):
    return pltpu.CompilerParams(vmem_limit_bytes=mebibytes << 20)


def on_device(sea_height, trans_u, trans_v, depth, sea_mask, freshwater_flux, love_factor):
    both_axes = ("lat", "lon")
    wave = jnp.asarray(wave_tables())
    phase = jnp.asarray(phase_tables())
    north = jnp.asarray(north_tables())
    fields = (sea_height, trans_u, trans_v, depth, sea_mask, freshwater_flux)

    message, strip_north, strip_south = pl.pallas_call(
        forward_kernel,
        out_shape=(shaped(DEVS, 8, 128), shaped(STRIP, COLS), shaped(STRIP, COLS)),
        in_specs=[whole()] * 7 + [whole(pltpu.SMEM), whole()],
        out_specs=(whole(),) * 3,
        compiler_params=params(),
        cost_estimate=cost(6 * 2 * 1024 * 256 * 256, 3 << 20),
        name="forward",
    )(*fields, wave, phase, jnp.asarray(area_table()))
    received = lax.all_to_all(message, both_axes, split_axis=0, concat_axis=0, tiled=True)

    upward = [(i, i + 1) for i in range(LATS - 1)]
    downward = [(i + 1, i) for i in range(LATS - 1)]
    from_south = lax.ppermute(strip_north, "lat", upward)
    from_north = lax.ppermute(strip_south, "lat", downward)
    to_west, to_east = pl.pallas_call(
        column_kernel,
        out_shape=(shaped(STRIP, 128), shaped(STRIP, 128)),
        in_specs=[whole()] * 8,
        out_specs=(whole(),) * 2,
        scratch_shapes=[pltpu.VMEM((128, COLS), f32)],
        compiler_params=params(),
        name="columns",
    )(*fields, from_south, from_north)
    from_west = lax.ppermute(to_east, "lon", [(i, (i + 1) % LONS) for i in range(LONS)])
    from_east = lax.ppermute(to_west, "lon", [((i + 1) % LONS, i) for i in range(LONS)])

    table_shape = shaped(DEG * ORDERS, HALF, kind=bf16)
    high, low = pl.pallas_call(
        table_kernel,
        out_shape=(table_shape, table_shape),
        in_specs=[whole()] * 2,
        out_specs=(whole(),) * 2,
        compiler_params=params(),
        cost_estimate=cost(DEG * ORDERS * HALF * 16, 8 << 20),
        name="table",
    )(north, jnp.asarray(seed_table()))

    span = CHUNK * ORDERS
    reply = pl.pallas_call(
        legendre_kernel,
        grid=(CHUNKS,),
        out_shape=shaped(DEVS, 8, 128),
        in_specs=[
            whole(),
            pl.BlockSpec((span, HALF), lambda chunk: (chunk, 0)),
            pl.BlockSpec((span, HALF), lambda chunk: (chunk, 0)),
            whole(),
            whole(),
        ],
        out_specs=whole(),
        scratch_shapes=[
            pltpu.VMEM((64, HALF), bf16),
            pltpu.VMEM((CHUNKS, ORDERS, span), f32),
            pltpu.VMEM((40, HALF), f32),
        ],
        compiler_params=params(),
        cost_estimate=cost(6 * 2 * 64 * 8192 * 256, 9 << 20),
        name="legendre",
    )(received, high, low, love_factor.reshape(8, 128), north)
    answer = lax.all_to_all(reply, both_axes, split_axis=0, concat_axis=0, tiled=True)

    tile = shaped(ROWS, COLS)
    height_out, u_out, v_out = pl.pallas_call(
        substep_kernel,
        grid=(1,),
        out_shape=(tile, tile, tile),
        in_specs=[whole()] * 10 + [pl.BlockSpec((1, 8, 128), lambda step: (0, 0, 0)), whole()],
        out_specs=(whole(),) * 3,
        scratch_shapes=[pltpu.VMEM((FIELDS, PAD_ROWS, PAD_COLS), f32)],
        compiler_params=params(),
        name="substeps",
    )(
        *fields,
        from_south,
        from_north,
        from_west,
        from_east,
        answer,
        jnp.asarray(row_tables()),
    )
    sal_height = pl.pallas_call(
        inverse_kernel,
        out_shape=tile,
        in_specs=[whole()] * 3 + [whole(pltpu.SMEM)],
        out_specs=whole(),
        scratch_shapes=[pltpu.VMEM((DEG, 128), f32)],
        compiler_params=params(),
        name="inverse",
    )(answer, sea_mask, wave, phase)
    return height_out, u_out, v_out, sal_height


def solution(mesh):
    tiles = P("lat", "lon")
    return jax.shard_map(
        on_device,
        mesh=mesh,
        in_specs=(tiles,) * 6 + (P(),),
        out_specs=(tiles,) * 4,
        check_vma=False,
    )
```

time: 736 us -> 81.5 us (0.11); the launches traced: 723 us -> 80.4 us
  waiting for transfers between devices: 196 us -> 7.87 us
  local copies, waits for them, and re-layouts: 192 us -> 23.9 us
  other arithmetic: 159 us -> 0 us
  blocking collectives: 64.4 us -> 0 us
  loops' own time: 47.3 us -> 0 us
  Pallas kernels: 0 us -> 19.9 us
  starting transfers between devices: 43.2 us -> 27.9 us
  between operations: 16 us -> 0.81 us
    psum x1 -> x0, waiting for transfers between devices: 161 us -> none  [on_device(): coef_cos, coef_sin = lax.psum((coef_cos, coef_sin), ('lat', 'lon'))]
    slice x122 -> x0, local copies, waits for them, and re-layouts: 154 us -> none  [the longest x64 87 us: synthesis_one_block(): sin_block[offset]]
    psum x1 -> x0, blocking collectives: 64.4 us -> none  [on_device(): lax.psum((jnp.sum(area_cells * freshwater_flux), jnp.sum(area_cells)), ('...]
    mul x2445 -> x0, other arithmetic: 60.5 us -> none  [the longest x224 27.5 us: synthesis_one_block(): scaled * cos_block[offset]]
    add x2084 -> x0, other arithmetic: 56.6 us -> none  [the longest x16 20.1 us: synthesis_one_block(): amp_sin + (scaled * sin_block[offset]).reshape(orders.shape) * current]
    another operation x2 -> x0, loops' own time: 47.3 us -> none  [the longest x1 27.8 us: analysis(): lax.fori_loop(0, degrees // block_steps, analysis_one_block, start_state)]
    reduce_sum x65 -> x0, other arithmetic: 25.7 us -> none  [the longest x64 24.5 us: analysis_one_block(): sin_rows.append(jnp.sum(weighted_sin * current, axis=lat_axis) * in_range)]
    unnamed x30 -> x66, local copies, waits for them, and re-layouts: 1.65 us -> 23.9 us
where the time goes in v1:
time: 81.5 us; the launch traced here: 80.4 us
  starting transfers between devices  27.9 us (34%)
  local copies, waits for them, and re-layouts  23.9 us (29%)
  Pallas kernels  19.9 us (24%)
  waiting for transfers between devices  7.87 us (10%)
    unnamed x66, local copies, waits for them, and re-layouts  23.9 us
    all_to_all x1, starting transfers between devices, on_device(): lax.all_to_all(message, both_axes, split_axis=0, concat_axis=0, tiled=True)  11.5 us
    pallas_call x1, Pallas kernels, on_device(): pl.pallas_call(legendre_kernel, grid=(CHUNKS,), out_shape=shaped(DEVS, 8,...  7.82 us
    all_to_all x1, starting transfers between devices, on_device(): lax.all_to_all(reply, both_axes, split_axis=0, concat_axis=0, tiled=True)  6.07 us
    pallas_call x1, Pallas kernels, on_device(): pl.pallas_call(table_kernel, out_shape=(table_shape, table_shape), in_spe...  4.21 us
    ppermute x1, waiting for transfers between devices, on_device(): from_north = lax.ppermute(strip_south, 'lat', downward)  4.16 us
    all_to_all x1, waiting for transfers between devices, on_device(): lax.all_to_all(message, both_axes, split_axis=0, concat_axis=0, tiled=True)  3.7 us
    ppermute x1, starting transfers between devices, on_device(): from_south = lax.ppermute(strip_north, 'lat', upward)  3.66 us
  transfers between devices with their start and end apart: 6, of which 2 were waited for; matrix products, arithmetic and copies ran while one was open for 0% of the time, Pallas kernels for 9%

profile of v1, /device:TPU:1, one launch (start us, length us, event | category | flops | bytes accessed | tf_op | source)
XLA Modules:
  0.0 80.4 jit_solution(14289337523425450201)
XLA Ops:
  0.6 0.0 copy-start.4
  0.6 1.6 %copy-done.4 = bf16[4,1024,256]{2,1,0:T(8,128)(2,1)S(1)} copy-done((bf16[4,1024,256]{2,1,0:T(8,128)(2,1)S(1)}, bf16[4,1024,256]{2,1,0:T(8,128)(2,1)}, u32[]{:S(2)}) %copy-start.4) | copy-done | bytes 2097176
  2.2 0.0 copy-start.7
  2.2 0.8 %copy-done.7 = s32[64,256]{1,0:T(8,128)S(1)} copy-done((s32[64,256]{1,0:T(8,128)S(1)}, s32[64,256]{1,0:T(8,128)}, u32[]{:S(2)}) %copy-start.7) | copy-done | bytes 65560
  3.1 0.0 copy-start.9
  3.1 0.8 %copy-done.9 = f32[64,256]{1,0:T(8,128)S(1)} copy-done((f32[64,256]{1,0:T(8,128)S(1)}, f32[64,256]{1,0:T(8,128)}, u32[]{:S(2)}) %copy-start.9) | copy-done | bytes 65560
  3.9 0.0 copy-start.11
  3.9 0.8 %copy-done.11 = f32[64,256]{1,0:T(8,128)S(1)} copy-done((f32[64,256]{1,0:T(8,128)S(1)}, f32[64,256]{1,0:T(8,128)}, u32[]{:S(2)}) %copy-start.11) | copy-done | bytes 65560
  4.7 0.0 copy-start.13
  4.7 0.8 %copy-done.13 = f32[64,256]{1,0:T(8,128)S(1)} copy-done((f32[64,256]{1,0:T(8,128)S(1)}, f32[64,256]{1,0:T(8,128)}, u32[]{:S(2)}) %copy-start.13) | copy-done | bytes 65560
  5.6 0.8 %copy-done.15 = f32[64,256]{1,0:T(8,128)S(1)} copy-done((f32[64,256]{1,0:T(8,128)S(1)}, f32[64,256]{1,0:T(8,128)}, u32[]{:S(2)}) %copy-start.15) | copy-done | bytes 65560
  6.4 0.8 %copy-done.17 = f32[64,256]{1,0:T(8,128)S(1)} copy-done((f32[64,256]{1,0:T(8,128)S(1)}, f32[64,256]{1,0:T(8,128)}, u32[]{:S(2)}) %copy-start.17) | copy-done | bytes 65560
  7.3 0.7 copy-done.27
  7.9 0.9 %copy-done.31 = f32[8,64,128]{2,1,0:T(8,128)S(1)} copy-done((f32[8,64,128]{2,1,0:T(8,128)S(1)}, f32[8,64,128]{2,1,0:T(8,128)}, u32[]{:S(2)}) %copy-start.31) | copy-done | bytes 262168
  8.9 2.6 %forward.1 = (f32[128,8,128]{2,1,0:T(8,128)}, f32[24,256]{1,0:T(8,128)S(1)}, f32[24,256]{1,0:T(8,128)S(1)}) custom-call(f32[64,256]{1,0:T(8,128)S(1)} %copy-done.9, f32[64,256]{1,0:T(8,128)S(1)} %copy-done.11, f32[64,256]{1,0:T(8,128)S(1)} %copy-done.13, f32[64,256]{1,0:T(8,128)S(1)} %copy-done.15, s32[64,256]{1,0:T(8,128)S(1)} %copy-done.7, ...), custom_call_target="tpu_custom_call" | custom-call | flops 805306368 | bytes 3145728 | tf_op jit(solution)/shard_map/forward/pallas_call | solution.py:429
  11.5 0.6 copy-done.29
  12.1 0.6 copy-done.30
  12.7 11.5 %all-to-all-start = ((f32[128,8,128]{2,1,0:T(8,128)}), f32[128,8,128]{2,1,0:T(8,128)S(1)}, u32[]{:S(2)}, u32[]{:S(2)}) async-start(f32[128,8,128]{2,1,0:T(8,128)} %get-tuple-element.18), calls=%async_computation | async-start | bytes 1048576 | tf_op jit(solution)/shard_map/all_to_all | solution.py:438
  24.2 0.0 copy-start.24
  24.3 0.7 copy-done.24
  25.0 0.7 copy-done.32
  25.7 4.2 %table.1 = (bf16[8192,256]{1,0:T(8,128)(2,1)S(1)}, bf16[8192,256]{1,0:T(8,128)(2,1)S(1)}) custom-call(f32[3,8,256]{2,1,0:T(8,128)S(1)} %copy-done.24, f32[8,128]{1,0:T(8,128)S(1)} %copy-done.32), custom_call_target="tpu_custom_call" | custom-call | flops 33554432 | bytes 8388608 | tf_op jit(solution)/shard_map/table/pallas_call | solution.py:457
  29.9 0.0 copy-start
  29.9 2.0 %copy-done = bf16[8192,256]{1,0:T(8,128)(2,1)} copy-done((bf16[8192,256]{1,0:T(8,128)(2,1)}, bf16[8192,256]{1,0:T(8,128)(2,1)S(1)}, u32[]{:S(2)}) %copy-start) | copy-done | bytes 4194328
  31.9 2.0 %copy-done.2 = bf16[8192,256]{1,0:T(8,128)(2,1)} copy-done((bf16[8192,256]{1,0:T(8,128)(2,1)}, bf16[8192,256]{1,0:T(8,128)(2,1)S(1)}, u32[]{:S(2)}) %copy-start.2) | copy-done | bytes 4194328
  33.9 3.7 %all-to-all-done.received = f32[128,8,128]{2,1,0:T(8,128)S(1)} async-done(((f32[128,8,128]{2,1,0:T(8,128)}), f32[128,8,128]{2,1,0:T(8,128)S(1)}, u32[]{:S(2)}, u32[]{:S(2)}) %all-to-all-start) | async-done | bytes 524320 | tf_op jit(solution)/shard_map/all_to_all | solution.py:438
  37.6 2.2 %copy-done.1 = bf16[8192,256]{1,0:T(8,128)(2,1)S(1)} copy-done((bf16[8192,256]{1,0:T(8,128)(2,1)S(1)}, bf16[8192,256]{1,0:T(8,128)(2,1)}, u32[]{:S(2)}) %copy-start.1) | copy-done | bytes 4194328
  39.8 2.2 %copy-done.3 = bf16[8192,256]{1,0:T(8,128)(2,1)S(1)} copy-done((bf16[8192,256]{1,0:T(8,128)(2,1)S(1)}, bf16[8192,256]{1,0:T(8,128)(2,1)}, u32[]{:S(2)}) %copy-start.3) | copy-done | bytes 4194328
  42.0 0.7 copy-done.25
  42.7 0.7 copy-done.26
  43.4 0.0 copy-start.16
  43.4 0.0 copy-start.5
  43.4 0.0 copy-start.28
  43.4 7.8 %legendre.1 = f32[128,8,128]{2,1,0:T(8,128)} custom-call(f32[128,8,128]{2,1,0:T(8,128)S(1)} %all-to-all-done.received, bf16[8192,256]{1,0:T(8,128)(2,1)S(1)} %copy-done.1, bf16[8192,256]{1,0:T(8,128)(2,1)S(1)} %copy-done.3, f32[8,128]{1,0:T(8,128)S(1)} %bitcast.1, f32[3,8,256]{2,1,0:T(8,128)S(1)} %copy-done.25), custom_call_target="tpu_custom_call" | custom-call | flops 1610612736 | bytes 9437184 | tf_op jit(solution)/shard_map/legendre/pallas_call | solution.py:468
  51.3 6.1 %all-to-all-start.1 = ((f32[128,8,128]{2,1,0:T(8,128)}), f32[128,8,128]{2,1,0:T(8,128)S(1)}, u32[]{:S(2)}, u32[]{:S(2)}) async-start(f32[128,8,128]{2,1,0:T(8,128)} %legendre.1), calls=%async_computation.1 | async-start | bytes 1048576 | tf_op jit(solution)/shard_map/all_to_all | solution.py:489
  57.3 3.7 %collective-permute-start = (f32[24,256]{1,0:T(8,128)}, f32[24,256]{1,0:T(8,128)S(1)}, u32[]{:S(2)}, u32[]{:S(2)}) collective-permute-start(f32[24,256]{1,0:T(8,128)} %copy-done.30), channel_id=1, source_target_pairs={{0,16},{16,32},{32,48},{48,64},{64,80},{80,96},{96,112},{1,17},{17... | collective-permute-start | bytes 73736 | tf_op jit(solution)/shard_map/ppermute | solution.py:442
  61.0 1.9 %collective-permute-start.1 = (f32[24,256]{1,0:T(8,128)}, f32[24,256]{1,0:T(8,128)S(1)}, u32[]{:S(2)}, u32[]{:S(2)}) collective-permute-start(f32[24,256]{1,0:T(8,128)} %copy-done.29), channel_id=1, source_target_pairs={{16,0},{32,16},{48,32},{64,48},{80,64},{96,80},{112,96},{17,1},{33... | collective-permute-start | bytes 73736 | tf_op jit(solution)/shard_map/ppermute | solution.py:443
  62.9 0.0 collective-permute-done.from_south
  62.9 0.0 copy-start.20
  63.0 4.2 %collective-permute-done.1.from_north = f32[24,256]{1,0:T(8,128)S(1)} collective-permute-done((f32[24,256]{1,0:T(8,128)}, f32[24,256]{1,0:T(8,128)S(1)}, u32[]{:S(2)}, u32[]{:S(2)}) %collective-permute-start.1) | collective-permute-done | bytes 24608 | tf_op jit(solution)/shard_map/ppermute | solution.py:443
  67.1 0.0 copy-done.8
  67.1 0.0 copy-done.10
  67.1 0.0 copy-done.12
  67.1 0.0 copy-done.14
  67.1 0.0 copy-done.16
  67.1 0.0 copy-start.18
  67.2 0.8 %copy-done.18 = f32[64,256]{1,0:T(8,128)S(1)} copy-done((f32[64,256]{1,0:T(8,128)S(1)}, f32[64,256]{1,0:T(8,128)}, u32[]{:S(2)}) %copy-start.18) | copy-done | bytes 65560
  68.0 0.9 %columns.1 = (f32[24,128]{1,0:T(8,128)}, f32[24,128]{1,0:T(8,128)}) custom-call(f32[64,256]{1,0:T(8,128)S(1)} %copy-done.10, f32[64,256]{1,0:T(8,128)S(1)} %copy-done.12, f32[64,256]{1,0:T(8,128)S(1)} %copy-done.14, f32[64,256]{1,0:T(8,128)S(1)} %copy-done.16, s32[64,256]{1,0:T(8,128)S(1)} %copy-done.8, f32[64,256]{1,0:T(8,128)S(1)} %copy-done.18, ...), custom_call_target="tpu_custom_call" | custom-call | tf_op jit(solution)/shard_map/columns/pallas_call | solution.py:444
  68.9 1.2 %collective-permute-start.2 = (f32[24,128]{1,0:T(8,128)}, f32[24,128]{1,0:T(8,128)S(1)}, u32[]{:S(2)}, u32[]{:S(2)}) collective-permute-start(f32[24,128]{1,0:T(8,128)} %get-tuple-element.16), channel_id=1, source_target_pairs={{0,1},{1,2},{2,3},{3,4},{4,5},{5,6},{6,7},{7,8},{8,9},{9,10},{10,1... | collective-permute-start | bytes 36872 | tf_op jit(solution)/shard_map/ppermute | solution.py:453
  70.0 0.0 copy-done.20
  70.0 0.0 copy-done.22
  70.0 3.6 %collective-permute-start.3 = (f32[24,128]{1,0:T(8,128)}, f32[24,128]{1,0:T(8,128)}, u32[]{:S(2)}, u32[]{:S(2)}) collective-permute-start(f32[24,128]{1,0:T(8,128)} %get-tuple-element.17), channel_id=1, source_target_pairs={{1,0},{2,1},{3,2},{4,3},{5,4},{6,5},{7,6},{8,7},{9,8},{10,9},{11,1... | collective-permute-start | bytes 36872 | tf_op jit(solution)/shard_map/ppermute | solution.py:454
  73.7 0.0 all-to-all-done.1.first_part.received
  73.7 0.0 copy-done.5
  73.7 0.0 copy-done.28
  73.7 2.2 %inverse.1 = f32[64,256]{1,0:T(8,128)} custom-call(f32[128,8,128]{2,1,0:T(8,128)S(1)} %all-to-all-done.1.first_part.received, s32[64,256]{1,0:T(8,128)S(1)} %copy-done.8, bf16[4,1024,256]{2,1,0:T(8,128)(2,1)S(1)} %copy-done.5, f32[2,16]{1,0:T(2,128)S(1)} %copy-done.28), custom_call_target="tpu_custom_call" | custom-call | tf_op jit(solution)/shard_map/inverse/pallas_call | solution.py:510
  75.8 0.0 collective-permute-done.2.from_west
  75.8 0.0 collective-permute-done.3.from_east
  75.8 0.0 copy-done.6
  75.8 0.0 copy-start.19
  75.9 0.8 %copy-done.19 = f32[64,256]{1,0:T(8,128)S(1)} copy-done((f32[64,256]{1,0:T(8,128)S(1)}, f32[64,256]{1,0:T(8,128)}, u32[]{:S(2)}) %copy-start.19) | copy-done | bytes 65560
  76.7 0.7 copy-done.21
  77.4 0.7 copy-done.23
  78.2 2.2 %substeps.1 = (f32[64,256]{1,0:T(8,128)}, f32[64,256]{1,0:T(8,128)}, f32[64,256]{1,0:T(8,128)}) custom-call(f32[64,256]{1,0:T(8,128)S(1)} %copy-done.10, f32[64,256]{1,0:T(8,128)S(1)} %copy-done.12, f32[64,256]{1,0:T(8,128)S(1)} %copy-done.14, f32[64,256]{1,0:T(8,128)S(1)} %copy-done.16, s32[64,256]{1,0:T(8,128)S(1)} %copy-done.8, f32[64,256]{1,0:T(8,128)S(1)} %copy-done.19, ...), custom_call_target="tpu_custom_call" | custom-call | tf_op jit(solution)/shard_map/substeps/pallas_call | solution.py:492
  (20 shorter events, 0.0 us)
Async XLA Ops:
  0.6 1.6 %copy-start.4 = (bf16[4,1024,256]{2,1,0:T(8,128)(2,1)S(1)}, bf16[4,1024,256]{2,1,0:T(8,128)(2,1)}, u32[]{:S(2)}) copy-start(bf16[4,1024,256]{2,1,0:T(8,128)(2,1)} %constant.12.clone.wave) | copy-start | bytes 6291460
  2.2 0.8 %copy-start.7 = (s32[64,256]{1,0:T(8,128)S(1)}, s32[64,256]{1,0:T(8,128)}, u32[]{:S(2)}) copy-start(s32[64,256]{1,0:T(8,128)} %mask.7) | copy-start | bytes 196612
  3.1 0.8 %copy-start.9 = (f32[64,256]{1,0:T(8,128)S(1)}, f32[64,256]{1,0:T(8,128)}, u32[]{:S(2)}) copy-start(f32[64,256]{1,0:T(8,128)} %height.5) | copy-start | bytes 196612
  3.9 0.8 %copy-start.11 = (f32[64,256]{1,0:T(8,128)S(1)}, f32[64,256]{1,0:T(8,128)}, u32[]{:S(2)}) copy-start(f32[64,256]{1,0:T(8,128)} %flux_u.5) | copy-start | bytes 196612
  4.7 0.8 %copy-start.13 = (f32[64,256]{1,0:T(8,128)S(1)}, f32[64,256]{1,0:T(8,128)}, u32[]{:S(2)}) copy-start(f32[64,256]{1,0:T(8,128)} %flux_v.5) | copy-start | bytes 196612
  5.6 0.8 %copy-start.15 = (f32[64,256]{1,0:T(8,128)S(1)}, f32[64,256]{1,0:T(8,128)}, u32[]{:S(2)}) copy-start(f32[64,256]{1,0:T(8,128)} %depth.5) | copy-start | bytes 196612
  6.4 0.8 %copy-start.17 = (f32[64,256]{1,0:T(8,128)S(1)}, f32[64,256]{1,0:T(8,128)}, u32[]{:S(2)}) copy-start(f32[64,256]{1,0:T(8,128)} %flux.5) | copy-start | bytes 196612
  7.3 0.7 copy-start.27
  7.9 0.9 %copy-start.31 = (f32[8,64,128]{2,1,0:T(8,128)S(1)}, f32[8,64,128]{2,1,0:T(8,128)}, u32[]{:S(2)}) copy-start(f32[8,64,128]{2,1,0:T(8,128)} %constant.15.clone.area) | copy-start | bytes 786436
  11.5 0.6 copy-start.29
  12.1 0.6 copy-start.30
  12.7 24.8 %all-to-all-start = ((f32[128,8,128]{2,1,0:T(8,128)}), f32[128,8,128]{2,1,0:T(8,128)S(1)}, u32[]{:S(2)}, u32[]{:S(2)}) async-start(f32[128,8,128]{2,1,0:T(8,128)} %get-tuple-element.18), calls=%async_computation | async-start | bytes 1048576 | tf_op jit(solution)/shard_map/all_to_all | solution.py:438
  24.2 0.7 copy-start.24
  25.0 0.7 copy-start.32
  29.9 2.0 %copy-start = (bf16[8192,256]{1,0:T(8,128)(2,1)}, bf16[8192,256]{1,0:T(8,128)(2,1)S(1)}, u32[]{:S(2)}) copy-start(bf16[8192,256]{1,0:T(8,128)(2,1)S(1)} %get-tuple-element.19.high) | copy-start | bytes 12582916
  31.9 2.0 %copy-start.2 = (bf16[8192,256]{1,0:T(8,128)(2,1)}, bf16[8192,256]{1,0:T(8,128)(2,1)S(1)}, u32[]{:S(2)}) copy-start(bf16[8192,256]{1,0:T(8,128)(2,1)S(1)} %get-tuple-element.20.low) | copy-start | bytes 12582916
  37.6 2.2 %copy-start.1 = (bf16[8192,256]{1,0:T(8,128)(2,1)S(1)}, bf16[8192,256]{1,0:T(8,128)(2,1)}, u32[]{:S(2)}) copy-start(bf16[8192,256]{1,0:T(8,128)(2,1)} %copy-done) | copy-start | bytes 12582916
  39.8 2.2 %copy-start.3 = (bf16[8192,256]{1,0:T(8,128)(2,1)S(1)}, bf16[8192,256]{1,0:T(8,128)(2,1)}, u32[]{:S(2)}) copy-start(bf16[8192,256]{1,0:T(8,128)(2,1)} %copy-done.2) | copy-start | bytes 12582916
  42.0 0.7 copy-start.25
  42.7 0.7 copy-start.26
  43.4 23.7 %copy-start.8 = (s32[64,256]{1,0:T(8,128)S(1)}, s32[64,256]{1,0:T(8,128)}, u32[]{:S(2)}) copy-start(s32[64,256]{1,0:T(8,128)} %mask.7) | copy-start | bytes 196612
  43.4 23.7 %copy-start.10 = (f32[64,256]{1,0:T(8,128)S(1)}, f32[64,256]{1,0:T(8,128)}, u32[]{:S(2)}) copy-start(f32[64,256]{1,0:T(8,128)} %height.5) | copy-start | bytes 196612
  43.4 23.7 %copy-start.12 = (f32[64,256]{1,0:T(8,128)S(1)}, f32[64,256]{1,0:T(8,128)}, u32[]{:S(2)}) copy-start(f32[64,256]{1,0:T(8,128)} %flux_u.5) | copy-start | bytes 196612
  43.4 23.7 %copy-start.14 = (f32[64,256]{1,0:T(8,128)S(1)}, f32[64,256]{1,0:T(8,128)}, u32[]{:S(2)}) copy-start(f32[64,256]{1,0:T(8,128)} %flux_v.5) | copy-start | bytes 196612
  43.4 23.7 %copy-start.16 = (f32[64,256]{1,0:T(8,128)S(1)}, f32[64,256]{1,0:T(8,128)}, u32[]{:S(2)}) copy-start(f32[64,256]{1,0:T(8,128)} %depth.5) | copy-start | bytes 196612
  43.4 30.3 %copy-start.5 = (bf16[4,1024,256]{2,1,0:T(8,128)(2,1)S(1)}, bf16[4,1024,256]{2,1,0:T(8,128)(2,1)}, u32[]{:S(2)}) copy-start(bf16[4,1024,256]{2,1,0:T(8,128)(2,1)} %constant.12.clone.wave) | copy-start | bytes 6291460
  43.4 30.3 %copy-start.28 = (f32[2,16]{1,0:T(2,128)S(1)}, f32[2,16]{1,0:T(2,128)}, u32[]{:S(2)}) copy-start(f32[2,16]{1,0:T(2,128)} %constant.13.clone.phase) | copy-start | bytes 388
  51.3 24.6 %copy-start.6 = (f32[8,2,72,128]{3,2,1,0:T(8,128)S(1)}, f32[8,2,72,128]{3,2,1,0:T(8,128)}, u32[]{:S(2)}) copy-start(f32[8,2,72,128]{3,2,1,0:T(8,128)} %constant.17.clone.bands) | copy-start | bytes 1769476
  51.3 22.4 %all-to-all-start.1 = ((f32[128,8,128]{2,1,0:T(8,128)}), f32[128,8,128]{2,1,0:T(8,128)S(1)}, u32[]{:S(2)}, u32[]{:S(2)}) async-start(f32[128,8,128]{2,1,0:T(8,128)} %legendre.1), calls=%async_computation.1 | async-start | bytes 1048576 | tf_op jit(solution)/shard_map/all_to_all | solution.py:489
  57.3 5.6 %collective-permute-start = (f32[24,256]{1,0:T(8,128)}, f32[24,256]{1,0:T(8,128)S(1)}, u32[]{:S(2)}, u32[]{:S(2)}) collective-permute-start(f32[24,256]{1,0:T(8,128)} %copy-done.30), channel_id=1, source_target_pairs={{0,16},{16,32},{32,48},{48,64},{64,80},{80,96},{96,112},{1,17},{17... | collective-permute-start | bytes 73736 | tf_op jit(solution)/shard_map/ppermute | solution.py:442
  61.0 6.1 %collective-permute-start.1 = (f32[24,256]{1,0:T(8,128)}, f32[24,256]{1,0:T(8,128)S(1)}, u32[]{:S(2)}, u32[]{:S(2)}) collective-permute-start(f32[24,256]{1,0:T(8,128)} %copy-done.29), channel_id=1, source_target_pairs={{16,0},{32,16},{48,32},{64,48},{80,64},{96,80},{112,96},{17,1},{33... | collective-permute-start | bytes 73736 | tf_op jit(solution)/shard_map/ppermute | solution.py:443
  62.9 7.1 %copy-start.20 = (f32[24,256]{1,0:T(8,128)}, f32[24,256]{1,0:T(8,128)S(1)}, u32[]{:S(2)}) copy-start(f32[24,256]{1,0:T(8,128)S(1)} %collective-permute-done.from_south) | copy-start | bytes 73732
  67.1 0.8 %copy-start.18 = (f32[64,256]{1,0:T(8,128)S(1)}, f32[64,256]{1,0:T(8,128)}, u32[]{:S(2)}) copy-start(f32[64,256]{1,0:T(8,128)} %flux.5) | copy-start | bytes 196612
  68.0 2.1 %copy-start.22 = (f32[24,256]{1,0:T(8,128)}, f32[24,256]{1,0:T(8,128)S(1)}, u32[]{:S(2)}) copy-start(f32[24,256]{1,0:T(8,128)S(1)} %collective-permute-done.1.from_north) | copy-start | bytes 73732
  68.9 7.0 %collective-permute-start.2 = (f32[24,128]{1,0:T(8,128)}, f32[24,128]{1,0:T(8,128)S(1)}, u32[]{:S(2)}, u32[]{:S(2)}) collective-permute-start(f32[24,128]{1,0:T(8,128)} %get-tuple-element.16), channel_id=1, source_target_pairs={{0,1},{1,2},{2,3},{3,4},{4,5},{5,6},{6,7},{7,8},{8,9},{9,10},{10,1... | collective-permute-start | bytes 36872 | tf_op jit(solution)/shard_map/ppermute | solution.py:453
  70.0 5.8 %collective-permute-start.3 = (f32[24,128]{1,0:T(8,128)}, f32[24,128]{1,0:T(8,128)}, u32[]{:S(2)}, u32[]{:S(2)}) collective-permute-start(f32[24,128]{1,0:T(8,128)} %get-tuple-element.17), channel_id=1, source_target_pairs={{1,0},{2,1},{3,2},{4,3},{5,4},{6,5},{7,6},{8,7},{9,8},{10,9},{11,1... | collective-permute-start | bytes 36872 | tf_op jit(solution)/shard_map/ppermute | solution.py:454
  75.8 0.8 %copy-start.19 = (f32[64,256]{1,0:T(8,128)S(1)}, f32[64,256]{1,0:T(8,128)}, u32[]{:S(2)}) copy-start(f32[64,256]{1,0:T(8,128)} %flux.5) | copy-start | bytes 196612
  76.7 0.7 copy-start.21
  77.4 0.7 copy-start.23

commit v2 on v1

v2 whole, which is shorter than its diff:
```python
import math

import jax
import jax.numpy as jnp
import ml_dtypes
import numpy as np
from jax import lax
from jax.experimental import pallas as pl
from jax.experimental.pallas import tpu as pltpu
from jax.sharding import PartitionSpec as P

ITERS = 4
NLON = 4096
NLAT = 512
DEG = 1024
LATS = 8
LONS = 16
DEVS = LATS * LONS
ROWS = NLAT // LATS
COLS = NLON // LONS
HALF = NLAT // 2
ORDERS = DEG // DEVS
WIDE = 4
FIELDS = 6
PAD_ROWS = ROWS + 2 * WIDE
PAD_COLS = COLS + 128
STRIP = FIELDS * WIDE
CHUNK = 128
CHUNKS = DEG // CHUNK
TILE = 256

step_time = 0.5
sal_ratio = 3.0 * 1035.0 / 5517.0
spacing = 2.0 * math.pi / NLON

f32 = jnp.float32
bf16 = jnp.bfloat16


def split_table(values):
    high = values.astype(ml_dtypes.bfloat16)
    low = (values - high.astype(np.float64)).astype(ml_dtypes.bfloat16)
    return high, low


def wave_tables():
    order = (np.arange(DEVS)[:, None] + DEVS * np.arange(ORDERS)[None, :]).reshape(-1)
    angle = (order[:, None] * np.arange(COLS)[None, :] % NLON) * (2.0 * math.pi / NLON)
    cos_high, cos_low = split_table(np.cos(angle))
    sin_high, sin_low = split_table(np.sin(angle))
    return np.stack([cos_high, sin_high, cos_low, sin_low])


def phase_tables():
    angle = np.arange(LONS)[:, None] * np.arange(LONS)[None, :] % LONS * (2.0 * math.pi / LONS)
    both = np.concatenate([np.cos(angle), np.sin(angle)], axis=1)
    return np.broadcast_to(both[..., None], both.shape + (128,)).astype(np.float32)


def balance_table():
    order = np.arange(DEG, dtype=np.float64)
    scale = np.ones(DEG)
    squares = []
    for step in range(DEG):
        squares.append(scale * scale)
        degree = order + step + 1.0
        factor = np.sqrt((4.0 * degree * degree - 1.0) / (degree * degree - order * order))
        scale = factor / scale
    return np.stack(squares, axis=1).reshape(ORDERS, DEVS, DEG).transpose(1, 0, 2).astype(np.float32)


def latitude_of(rows):
    return (rows + 0.5 - NLAT / 2) * spacing


def row_tables():
    local = np.concatenate([np.arange(ROWS + WIDE), np.arange(-WIDE, 0)])
    latitude = latitude_of(np.arange(LATS)[:, None] * ROWS + local[None, :])
    both = np.stack([1.0 / np.cos(latitude), np.cos(latitude + spacing / 2)], axis=1)
    return np.broadcast_to(both[..., None], both.shape + (128,)).astype(np.float32)


def area_table():
    latitude = latitude_of(np.arange(NLAT)).reshape(LATS, ROWS, 1)
    return np.broadcast_to(np.cos(latitude), (LATS, ROWS, 128)).astype(np.float32)


def north_tables():
    latitude = latitude_of(np.arange(HALF, NLAT))
    weight = np.cos(latitude) * spacing * spacing / (4.0 * math.pi)
    table = np.stack([np.sin(latitude), np.log(np.cos(latitude)), weight])
    return np.broadcast_to(table[:, None, :], (3, 8, HALF)).astype(np.float32)


def seed_table():
    order = np.arange(1, DEG)
    grown = 0.5 * math.log(2.0) + 0.5 * np.cumsum(np.log((2.0 * order + 1.0) / (2.0 * order)))
    return np.concatenate([[0.0], grown]).reshape(ORDERS, DEVS).astype(np.float32)


def iota(shape, dim):
    return lax.broadcasted_iota(jnp.int32, shape, dim)


def halves(values):
    high = values.astype(bf16)
    low = (values - high.astype(f32)).astype(bf16)
    return high, low


def dot_nt(left, right):
    return lax.dot_general(left, right, (((1,), (1,)), ((), ())), preferred_element_type=f32)


def dot_nn(left, right):
    return lax.dot_general(left, right, (((1,), (0,)), ((), ())), preferred_element_type=f32)


def fetch(pairs, sems):
    copies = [pltpu.make_async_copy(a, b, sems.at[slot]) for slot, (a, b) in enumerate(pairs)]
    for copy in copies:
        copy.start()
    return copies


def row_order(lat_index):
    row = iota((ROWS, ROWS), 0)
    col = iota((ROWS, ROWS), 1)
    south = lat_index < LATS // 2
    return jnp.where(south, (row + col == ROWS - 1).astype(f32), (row == col).astype(f32))


def forward_kernel(
    height_in,
    flux_u_in,
    flux_v_in,
    depth_in,
    mask_in,
    flux_in,
    wave_in,
    phase_in,
    area_in,
    message_out,
    north_out,
    south_out,
    tiles,
    mask,
    wave,
    phase,
    area,
    message,
    strips,
    sems,
    send_sem,
    strip_sems,
):
    lat_index = lax.axis_index("lat")
    lon_index = lax.axis_index("lon")
    loads = fetch(
        (
            (mask_in, mask),
            (height_in, tiles.at[0]),
            (wave_in, wave),
            (phase_in.at[lon_index], phase),
            (flux_in, tiles.at[4]),
            (area_in.at[lat_index], area),
            (flux_u_in, tiles.at[1]),
            (flux_v_in, tiles.at[2]),
            (depth_in, tiles.at[3]),
        ),
        sems,
    )
    loads[0].wait()
    loads[1].wait()
    sea = mask[...].astype(f32)
    mass_high, mass_low = halves(sea * tiles[0])
    both = jnp.concatenate([mass_high, mass_low], axis=1)
    both = dot_nn(row_order(lat_index).astype(bf16), both).astype(bf16)
    mass_high, mass_low = both[:, :COLS], both[:, COLS:]
    zero = jnp.zeros_like(mass_high)

    def sides(part):
        return (
            jnp.concatenate([part, zero, zero, part], axis=0),
            jnp.concatenate([zero, part, -part, zero], axis=0),
        )

    high_cos, high_sin = sides(mass_high)
    low_cos, low_sin = sides(mass_low)
    loads[2].wait()
    spectrum = (
        dot_nt(wave[0], high_cos)
        + dot_nt(wave[1], high_sin)
        + dot_nt(wave[0], low_cos)
        + dot_nt(wave[1], low_sin)
        + dot_nt(wave[2], high_cos)
        + dot_nt(wave[3], high_sin)
    )
    loads[3].wait()
    for device in range(DEVS):
        turn = device % LONS
        part = spectrum[device * ORDERS : (device + 1) * ORDERS, :]
        cos_turn, sin_turn = phase[turn : turn + 1, :], phase[LONS + turn : LONS + turn + 1, :]
        message[device] = cos_turn * part[:, :128] + sin_turn * part[:, 128:]

    loads[4].wait()
    loads[5].wait()
    band = area[...]
    area_cells = sea * jnp.concatenate([band, band], axis=1)
    flux_sum = jnp.sum(area_cells * tiles[4])
    area_sum = jnp.sum(area_cells)
    row = iota((8, 128), 0)
    lane = iota((8, 128), 1)
    first = message[0]
    first = jnp.where((row == 0) & (lane >= 64), area_sum, first)
    message[0] = jnp.where((row == 0) & (lane == 64), flux_sum, first)
    send = pltpu.make_async_copy(message, message_out, send_sem)
    send.start()

    for load in loads[6:]:
        load.wait()
    for slot, values in enumerate((tiles[0], tiles[1], tiles[2], tiles[3], sea, tiles[4])):
        strips[0, slot * WIDE : (slot + 1) * WIDE, :] = values[ROWS - WIDE :, :]
        strips[1, slot * WIDE : (slot + 1) * WIDE, :] = values[:WIDE, :]
    sends = fetch(((strips.at[0], north_out), (strips.at[1], south_out)), strip_sems)
    for copy in [send] + sends:
        copy.wait()


def tiles_of():
    found = []
    for chunk in range(CHUNKS):
        kept = 8 if chunk < 4 else 4 if chunk < 6 else 2
        steps = TILE // kept
        found += [(chunk, first, steps, kept) for first in range(0, CHUNK, steps)]
    return found


TILES = tiles_of()


def gain_kernel(love_in, balance_in, gains_out, love, balance, gains, sems, out_sem):
    device = lax.axis_index("lat") * LONS + lax.axis_index("lon")
    loads = fetch(((love_in, love), (balance_in.at[device], balance)), sems)
    for load in loads:
        load.wait()
    lane = iota((8, 128), 1)
    row = iota((8, 128), 0)
    degree = (128 * row + lane).astype(f32)
    gain = sal_ratio * love[...] / (2.0 * degree + 1.0)
    turned = pltpu.roll(gain, (128 - device) % 128, 1)
    above = jnp.concatenate([turned[1:], jnp.zeros((1, 128), f32)], axis=0)
    shifted = jnp.where(lane + device < 128, turned, above)
    padded = jnp.concatenate([shifted, jnp.zeros((8, 128), f32)], axis=0)
    blocks = jnp.concatenate(
        [padded[c : c + 8] * balance[:, c * CHUNK : (c + 1) * CHUNK] for c in range(CHUNKS)], axis=0
    )
    high, low = halves(blocks)
    column = iota((ORDERS, TILE), 1)
    for slot, (chunk, first, steps, kept) in enumerate(TILES):
        same = iota((CHUNK, TILE), 1) // kept + first == iota((CHUNK, TILE), 0)
        spread = same.astype(f32).astype(bf16)
        place = slice(chunk * ORDERS, (chunk + 1) * ORDERS)
        wide = dot_nn(high, spread)[place] + dot_nn(low, spread)[place]
        wide = jnp.where(column % kept == iota((ORDERS, TILE), 0), wide, 0.0)
        even = jnp.where((column // kept) % 2 == 0, wide, 0.0)
        gains[slot, 0:8, :] = even
        gains[slot, 8:16, :] = wide - even
    copy = pltpu.make_async_copy(gains, gains_out, out_sem)
    copy.start()
    copy.wait()


def legendre_kernel(
    received,
    gains_in,
    balance_in,
    seeds_in,
    north_in,
    message_out,
    gains,
    balance,
    seeds,
    north,
    high,
    low,
    message,
    sems,
    out_sems,
):
    device = lax.axis_index("lat") * LONS + lax.axis_index("lon")
    loads = fetch(
        (
            (north_in, north),
            (seeds_in, seeds),
            (balance_in.at[device], balance),
            (gains_in, gains),
        ),
        sems,
    )
    lane = iota((8, 128), 1)
    row = iota((8, 128), 0)
    left = lane < 64

    bands = []
    for lat in range(LATS):
        band = received[lat * LONS]
        for lon in range(1, LONS):
            band = band + received[lat * LONS + lon]
        bands.append(band)
    sums = bands[0]
    for band in bands[1:]:
        sums = sums + band
    even = [bands[4 + part] + bands[3 - part] for part in range(4)]
    odd = [bands[4 + part] - bands[3 - part] for part in range(4)]

    for load in loads[:3]:
        load.wait()

    def arrange(parts):
        cos_parts = []
        sin_parts = []
        for first, second in ((parts[0], parts[1]), (parts[2], parts[3])):
            cos_parts.append(jnp.where(left, first, pltpu.roll(second, 64, 1)))
            sin_parts.append(jnp.where(left, pltpu.roll(first, 64, 1), second))
        weight = north[2]
        return [
            jnp.concatenate(cos_parts, axis=1) * weight,
            jnp.concatenate(sin_parts, axis=1) * weight,
        ]

    rows_high, rows_low = halves(jnp.concatenate(arrange(even) + arrange(odd), axis=0))
    rows_both = jnp.concatenate([rows_high, rows_low], axis=0)

    sine = north[0]
    seed_log = jnp.sum(jnp.where(lane == device, seeds[...], 0.0), axis=1, keepdims=True)
    order = (device + DEVS * row).astype(f32)[:, :1]
    state = [jnp.zeros((ORDERS, HALF), f32), jnp.exp(seed_log + order * north[1])]
    wide_row = iota((ORDERS, HALF), 0)

    def extend(slot):
        chunk, first, steps, kept = TILES[slot]
        share = ORDERS // kept
        packed = []
        for step in range(first, first + steps, share):
            block = None
            for part in range(share):
                previous, current = state
                spot = chunk * CHUNK + step + part
                if part == 0:
                    block = current
                else:
                    moved = pltpu.roll(current, part * kept, 0)
                    block = jnp.where(wide_row < part * kept, block, moved)
                turn = balance[:, spot : spot + 1] * sine
                state[0], state[1] = current, turn * current - previous
            packed.append(block)
            if len(packed) == 2:
                place = slice(slot * TILE + (step - first) // share * 8 - 8, None)
                place = slice(place.start, place.start + 16)
                high[place, :], low[place, :] = halves(jnp.concatenate(packed, axis=0))
                packed = []

    def analyse(slot):
        place = slice(slot * TILE, (slot + 1) * TILE)
        both = dot_nt(rows_both, high[place, :])
        coefs = both[:32] + both[32:] + dot_nt(rows_high, low[place, :])
        even, odd = gains[slot, 0:8, :], gains[slot, 8:16, :]
        coefs_high, coefs_low = halves(coefs * jnp.concatenate([even, even, odd, odd], axis=0))
        return jnp.concatenate([coefs_high, coefs_low], axis=0)

    def synthesise(slot, coefs):
        place = slice(slot * TILE, (slot + 1) * TILE)
        return dot_nn(coefs, high[place, :]), dot_nn(coefs[:32], low[place, :])

    count = len(TILES)
    total_high = jnp.zeros((64, HALF), f32)
    total_low = jnp.zeros((32, HALF), f32)
    coefs = {}
    for turn in range(count + 2):
        if turn < count:
            extend(turn)
        if turn == 1:
            loads[3].wait()
        if 1 <= turn <= count:
            coefs[turn - 1] = analyse(turn - 1)
        if turn >= 2:
            more_high, more_low = synthesise(turn - 2, coefs.pop(turn - 2))
            total_high = total_high + more_high
            total_low = total_low + more_low
    total = total_high[:32] + total_high[32:] + total_low

    flux_sum = jnp.sum(jnp.where((row == 0) & (lane == 64), sums, 0.0))
    area_sum = jnp.sum(jnp.where((row == 0) & (lane == 65), sums, 0.0))
    mean = jnp.full((8, 128), flux_sum, f32) / jnp.full((8, 128), area_sum, f32)
    slot = (device == 0) & (row == 0) & (lane >= 64)
    cos_even, sin_even = total[0:8, :], total[8:16, :]
    cos_odd, sin_odd = total[16:24, :], total[24:32, :]
    copies = []
    for north_side in (True, False):
        if north_side:
            cos_all, sin_all = cos_even + cos_odd, sin_even + sin_odd
        else:
            cos_all, sin_all = cos_even - cos_odd, sin_even - sin_odd
        for part in range(4):
            block = slice(128 * (part // 2), 128 * (part // 2) + 128)
            cos_part, sin_part = cos_all[:, block], sin_all[:, block]
            if part % 2 == 0:
                sent = jnp.where(left, cos_part, pltpu.roll(sin_part, 64, 1))
            else:
                sent = jnp.where(left, pltpu.roll(cos_part, 64, 1), sin_part)
            sent = jnp.where(slot, mean, sent)
            lat = 4 + part if north_side else 3 - part
            for lon in range(LONS):
                message[lat * LONS + lon] = sent
            part_place = pl.ds(lat * LONS, LONS)
            copies += fetch(((message.at[part_place], message_out.at[part_place]),), out_sems.at[pl.ds(lat, 1)])
    for copy in copies:
        copy.wait()


def inverse_kernel(
    received,
    mask_in,
    wave_in,
    phase_in,
    plain_in,
    response_in,
    sal_out,
    height_out,
    u_out,
    v_out,
    mask,
    wave,
    phase,
    plain,
    response,
    turned_scratch,
    results,
    sems,
    out_sems,
    sal_sem,
):
    lat_index = lax.axis_index("lat")
    lon_index = lax.axis_index("lon")
    loads = fetch(
        (
            (phase_in.at[lon_index], phase),
            (wave_in, wave),
            (plain_in, plain),
            (response_in, response),
            (mask_in, mask),
        ),
        sems,
    )
    loads[0].wait()
    lane = iota((8, 128), 1)
    sign = jnp.where(lane[:1] < 64, 1.0, -1.0)
    for device in range(DEVS):
        turn = device % LONS
        part = received[device]
        cos_turn, sin_turn = phase[turn : turn + 1, :], phase[LONS + turn : LONS + turn + 1, :] * sign
        turned_scratch[device * ORDERS : (device + 1) * ORDERS, :] = (
            cos_turn * part + sin_turn * pltpu.roll(part, 64, 1)
        )
    turned = turned_scratch[...].T
    high, low = halves(turned)
    cos_both = jnp.concatenate([high[:64], low[:64]], axis=0)
    sin_both = jnp.concatenate([high[64:], low[64:]], axis=0)
    loads[1].wait()
    both = dot_nn(cos_both, wave[0]) + dot_nn(sin_both, wave[1])
    field = both[:64] + both[64:] + dot_nn(high[:64], wave[2]) + dot_nn(high[64:], wave[3])
    for load in loads[2:]:
        load.wait()
    mean = jnp.sum(jnp.where((iota((8, 128), 0) == 0) & (lane == 64), received[0], 0.0))
    for slot in range(3):
        results[slot] = plain[slot] - mean * response[slot]
    sends = fetch(zip((results.at[0], results.at[1], results.at[2]), (height_out, u_out, v_out)), out_sems)
    field_high, field_low = halves(field)
    order = row_order(lat_index).astype(bf16)
    field = dot_nn(order, field_high) + dot_nn(order, field_low)
    results[3] = field * mask[...].astype(f32)
    send = pltpu.make_async_copy(results.at[3], sal_out, sal_sem)
    send.start()
    for copy in sends + [send]:
        copy.wait()


def column_kernel(
    height_in,
    flux_u_in,
    flux_v_in,
    depth_in,
    mask_in,
    flux_in,
    south_in,
    north_in,
    west_out,
    east_out,
    tiles,
    mask,
    strips,
    sides,
    block,
    sems,
    out_sems,
):
    loads = fetch(
        (
            (south_in, strips.at[0]),
            (north_in, strips.at[1]),
            (height_in, tiles.at[0]),
            (flux_u_in, tiles.at[1]),
            (flux_v_in, tiles.at[2]),
            (depth_in, tiles.at[3]),
            (mask_in, mask),
            (flux_in, tiles.at[5]),
        ),
        sems,
    )
    lane = iota((128, 128), 1)
    west = jnp.zeros((128, 128), f32)
    east = jnp.zeros((128, 128), f32)
    block[PAD_ROWS:, :] = jnp.zeros((128 - PAD_ROWS, COLS), f32)
    for load in loads:
        load.wait()
    for slot in range(FIELDS):
        block[0:ROWS, :] = mask[...].astype(f32) if slot == 4 else tiles[slot]
        block[ROWS : ROWS + WIDE, :] = strips[1, slot * WIDE : (slot + 1) * WIDE, :]
        block[ROWS + WIDE : PAD_ROWS, :] = strips[0, slot * WIDE : (slot + 1) * WIDE, :]
        here = (lane >= slot * WIDE) & (lane < (slot + 1) * WIDE)
        west_part = block[:, 0:128]
        east_part = pltpu.roll(block[:, COLS - 128 : COLS], (WIDE + slot * WIDE) % 128, 1)
        if slot:
            west_part = pltpu.roll(west_part, slot * WIDE, 1)
        west = jnp.where(here, west_part, west)
        east = jnp.where(here, east_part, east)
    sides[0] = west.T[:STRIP, :]
    sides[1] = east.T[:STRIP, :]
    for copy in fetch(((sides.at[0], west_out), (sides.at[1], east_out)), out_sems):
        copy.wait()


def substep_kernel(
    height_in,
    flux_u_in,
    flux_v_in,
    depth_in,
    mask_in,
    flux_in,
    south_in,
    north_in,
    west_in,
    east_in,
    bands_in,
    plain_out,
    response_out,
    tiles,
    mask,
    strips,
    sides,
    bands,
    block,
    plain,
    response,
    sems,
    out_sems,
):
    lat_index = lax.axis_index("lat")
    loads = fetch(
        (
            (south_in, strips.at[0]),
            (north_in, strips.at[1]),
            (west_in, sides.at[0]),
            (east_in, sides.at[1]),
            (height_in, tiles.at[0]),
            (flux_u_in, tiles.at[1]),
            (flux_v_in, tiles.at[2]),
            (depth_in, tiles.at[3]),
            (mask_in, mask),
            (flux_in, tiles.at[5]),
            (bands_in.at[lat_index], bands),
        ),
        sems,
    )
    for load in loads:
        load.wait()
    lane = iota((PAD_ROWS, 128), 1)
    fill = jnp.zeros((128 - STRIP, 128), f32)
    west = jnp.concatenate([sides[0], fill], axis=0).T[:PAD_ROWS, :]
    east = jnp.concatenate([sides[1], fill], axis=0).T[:PAD_ROWS, :]
    padded = []
    for slot in range(FIELDS):
        block[slot, 0:ROWS, 0:COLS] = mask[...].astype(f32) if slot == 4 else tiles[slot]
        block[slot, ROWS : ROWS + WIDE, 0:COLS] = strips[1, slot * WIDE : (slot + 1) * WIDE, :]
        block[slot, ROWS + WIDE : PAD_ROWS, 0:COLS] = strips[0, slot * WIDE : (slot + 1) * WIDE, :]
        high_side = pltpu.roll(east, 128 - slot * WIDE, 1) if slot else east
        low_side = pltpu.roll(west, 128 - WIDE - slot * WIDE, 1)
        block[slot, :, COLS:] = jnp.where(
            lane < WIDE, high_side, jnp.where(lane >= 128 - WIDE, low_side, 0.0)
        )
        padded.append(block[slot])

    def eastward(values):
        return pltpu.roll(values, PAD_COLS - 1, 1)

    def northward(values):
        return pltpu.roll(values, PAD_ROWS - 1, 0)

    height_now, u_now, v_now, depth_all, sea, flux_all = padded
    inverse_cos = jnp.concatenate([bands[0]] * 3, axis=1)
    north_cos = jnp.concatenate([bands[1]] * 3, axis=1)
    open_u = sea * eastward(sea)
    open_v = sea * northward(sea)
    pull_u = open_u * (0.5 * step_time) * (depth_all + eastward(depth_all)) * inverse_cos
    pull_v = open_v * (0.5 * step_time) * (depth_all + northward(depth_all))
    scale = step_time * inverse_cos

    def advance(state, forcing):
        height_now, u_now, v_now = state
        north_flux = v_now * north_cos
        divergence = u_now - pltpu.roll(u_now, 1, 1) + (north_flux - pltpu.roll(north_flux, 1, 0))
        height_now = height_now - scale * divergence + forcing
        u_now = open_u * u_now - pull_u * (eastward(height_now) - height_now)
        v_now = open_v * v_now - pull_v * (northward(height_now) - height_now)
        return height_now, u_now, v_now

    own = step_time * sea
    with_flux = (height_now, u_now, v_now)
    with_one = (jnp.zeros_like(sea),) * 3
    for repeat in range(ITERS):
        with_flux = advance(with_flux, own * flux_all)
        with_one = advance(with_one, own)
    for slot in range(3):
        plain[slot] = with_flux[slot][:ROWS, :COLS]
        response[slot] = with_one[slot][:ROWS, :COLS]
    for copy in fetch(((plain, plain_out), (response, response_out)), out_sems):
        copy.wait()


def far_call(kernel, name, operands, results, scratch, work=None, here=()):
    placed = []
    specs = []
    for slot, operand in enumerate(operands):
        if slot in here:
            space = pltpu.VMEM
        else:
            space = pltpu.HBM
            operand = pltpu.with_memory_space_constraint(operand, pltpu.HBM)
        placed.append(operand)
        specs.append(pl.BlockSpec(memory_space=space))
    return pl.pallas_call(
        kernel,
        out_shape=tuple(pltpu.HBM(shape, kind) for shape, kind in results),
        in_specs=specs,
        out_specs=(pl.BlockSpec(memory_space=pltpu.HBM),) * len(results),
        scratch_shapes=scratch,
        compiler_params=pltpu.CompilerParams(vmem_limit_bytes=32 << 20),
        cost_estimate=work,
        name=name,
    )(*placed)


def cost(flops, moved):
    return pl.CostEstimate(flops=flops, bytes_accessed=moved, transcendentals=0)


def on_device(sea_height, trans_u, trans_v, depth, sea_mask, freshwater_flux, love_factor):
    both_axes = ("lat", "lon")
    wave = jnp.asarray(wave_tables())
    phase = jnp.asarray(phase_tables())
    north = jnp.asarray(north_tables())
    fields = (sea_height, trans_u, trans_v, depth, sea_mask, freshwater_flux)
    vmem = pltpu.VMEM
    copies = pltpu.SemaphoreType.DMA
    tile = ((ROWS, COLS), f32)
    strip = ((STRIP, COLS), f32)
    side = ((STRIP, 128), f32)
    messages = ((DEVS, 8, 128), f32)
    tiles = vmem((FIELDS, ROWS, COLS), f32)
    mask_tile = vmem((ROWS, COLS), jnp.int32)

    message, strip_north, strip_south = far_call(
        forward_kernel,
        "forward",
        fields + (wave, phase, jnp.asarray(area_table())),
        (messages, strip, strip),
        [
            tiles,
            mask_tile,
            vmem((4, DEG, COLS), bf16),
            vmem((2 * LONS, 128), f32),
            vmem((ROWS, 128), f32),
            vmem(*messages),
            vmem((2, STRIP, COLS), f32),
            copies((9,)),
            copies,
            copies((2,)),
        ],
        work=cost(6 * 2 * 1024 * 256 * 256, 3 << 20),
    )
    received = lax.all_to_all(message, both_axes, split_axis=0, concat_axis=0, tiled=True)

    upward = [(i, i + 1) for i in range(LATS - 1)]
    downward = [(i + 1, i) for i in range(LATS - 1)]
    from_south = lax.ppermute(strip_north, "lat", upward)
    from_north = lax.ppermute(strip_south, "lat", downward)

    balance = jnp.asarray(balance_table())
    gain_tiles = ((len(TILES), 16, TILE), f32)
    (gains,) = far_call(
        gain_kernel,
        "gains",
        (love_factor.reshape(8, 128), balance),
        (gain_tiles,),
        [
            vmem((8, 128), f32),
            vmem((ORDERS, DEG), f32),
            vmem(*gain_tiles),
            copies((2,)),
            copies,
        ],
        work=cost(2 << 20, 1 << 20),
    )
    received, from_south, from_north = lax.optimization_barrier((received, from_south, from_north))
    table = ((len(TILES) * TILE, HALF), bf16)
    (reply,) = far_call(
        legendre_kernel,
        "legendre",
        (received, gains, balance, jnp.asarray(seed_table()), north),
        (messages,),
        [
            vmem(*gain_tiles),
            vmem((ORDERS, DEG), f32),
            vmem((ORDERS, DEVS), f32),
            vmem((3, 8, HALF), f32),
            vmem(*table),
            vmem(*table),
            vmem(*messages),
            copies((4,)),
            copies((LATS,)),
        ],
        work=cost(6 * 2 * 64 * 8192 * 256, 9 << 20),
        here=(0,),
    )
    answer = lax.all_to_all(reply, both_axes, split_axis=0, concat_axis=0, tiled=True)

    to_west, to_east = far_call(
        column_kernel,
        "columns",
        fields + (from_south, from_north),
        (side, side),
        [
            tiles,
            mask_tile,
            vmem((2, STRIP, COLS), f32),
            vmem((2, STRIP, 128), f32),
            vmem((128, COLS), f32),
            copies((8,)),
            copies((2,)),
        ],
    )
    from_west = lax.ppermute(to_east, "lon", [(i, (i + 1) % LONS) for i in range(LONS)])
    from_east = lax.ppermute(to_west, "lon", [((i + 1) % LONS, i) for i in range(LONS)])

    three = ((3, ROWS, COLS), f32)
    plain, response = far_call(
        substep_kernel,
        "substeps",
        fields + (from_south, from_north, from_west, from_east, jnp.asarray(row_tables())),
        (three, three),
        [
            tiles,
            mask_tile,
            vmem((2, STRIP, COLS), f32),
            vmem((2, STRIP, 128), f32),
            vmem((2, PAD_ROWS, 128), f32),
            vmem((FIELDS, PAD_ROWS, PAD_COLS), f32),
            vmem(*three),
            vmem(*three),
            copies((11,)),
            copies((2,)),
        ],
    )
    sal_height, height_out, u_out, v_out = far_call(
        inverse_kernel,
        "inverse",
        (answer, sea_mask, wave, phase, plain, response),
        (tile,) * 4,
        [
            mask_tile,
            vmem((4, DEG, COLS), bf16),
            vmem((2 * LONS, 128), f32),
            vmem(*three),
            vmem(*three),
            vmem((DEG, 128), f32),
            vmem((4, ROWS, COLS), f32),
            copies((5,)),
            copies((3,)),
            copies,
        ],
        here=(0,),
    )
    return height_out, u_out, v_out, sal_height


def solution(mesh):
    tiles = P("lat", "lon")
    return jax.shard_map(
        on_device,
        mesh=mesh,
        in_specs=(tiles,) * 6 + (P(),),
        out_specs=(tiles,) * 4,
        check_vma=False,
    )
```

time: 81.5 us -> 57.7 us (0.71)
  local copies, waits for them, and re-layouts: 23.9 us -> 1.2 us
  waiting for transfers between devices: 7.87 us -> 9.43 us
  Pallas kernels: 19.9 us -> 18.9 us
  starting transfers between devices: 27.9 us -> 26.9 us
    unnamed x66 -> x8, local copies, waits for them, and re-layouts: 23.9 us -> 1.2 us
    ppermute x1, waiting for transfers between devices: 0.01 us -> 3.6 us  [on_device(): lax.ppermute(to_east, 'lon', [(i, (i + 1) % LONS) for i in range(LONS)])]
    ppermute x1, waiting for transfers between devices: 4.16 us -> 2.27 us  [on_device(): from_north = lax.ppermute(strip_south, 'lat', downward)]
    all_to_all x1, starting transfers between devices: 6.07 us -> 4.88 us  [on_device(): lax.all_to_all(reply, both_axes, split_axis=0, concat_axis=0, tiled=True)]
    pallas_call x6, Pallas kernels: 19.9 us -> 18.9 us  [far_call(): pl.pallas_call(kernel, out_shape=tuple((pltpu.HBM(shape, kind) for shape,...]
  transfers between devices with their start and end apart: 6 -> 6, of which waited for: 2 -> 3; matrix products, arithmetic and copies ran while one was open for 0% -> 0% of each run, Pallas kernels for 9% -> 13%
where the time goes in v2:
time: 57.7 us; the launch traced here: 57.2 us
  starting transfers between devices  26.9 us (47%)
  Pallas kernels  18.9 us (33%)
  waiting for transfers between devices  9.43 us (16%)
  local copies, waits for them, and re-layouts  1.2 us (2%)
  between operations  0.75 us (1%)
    pallas_call x6, Pallas kernels, far_call(): pl.pallas_call(kernel, out_shape=tuple((pltpu.HBM(shape, kind) for shape,...  18.9 us
    all_to_all x1, starting transfers between devices, on_device(): lax.all_to_all(message, both_axes, split_axis=0, concat_axis=0, tiled=True)  11.5 us
    all_to_all x1, starting transfers between devices, on_device(): lax.all_to_all(reply, both_axes, split_axis=0, concat_axis=0, tiled=True)  4.88 us
    ppermute x1, starting transfers between devices, on_device(): from_south = lax.ppermute(strip_north, 'lat', upward)  3.66 us
    ppermute x1, waiting for transfers between devices, on_device(): lax.ppermute(to_east, 'lon', [(i, (i + 1) % LONS) for i in range(LONS)])  3.6 us
    all_to_all x1, waiting for transfers between devices, on_device(): lax.all_to_all(message, both_axes, split_axis=0, concat_axis=0, tiled=True)  3.55 us
    ppermute x1, starting transfers between devices, on_device(): lax.ppermute(to_west, 'lon', [((i + 1) % LONS, i) for i in range(LONS)])  3.52 us
    ppermute x1, waiting for transfers between devices, on_device(): from_north = lax.ppermute(strip_south, 'lat', downward)  2.27 us
  transfers between devices with their start and end apart: 6, of which 3 were waited for; matrix products, arithmetic and copies ran while one was open for 0% of the time, Pallas kernels for 13%

profile of v2, /device:TPU:1, one launch (start us, length us, event | category | flops | bytes accessed | tf_op | source)
XLA Modules:
  0.0 57.2 jit_solution(7713555343353870342)
XLA Ops:
  0.6 3.8 %forward.1 = (f32[128,8,128]{2,1,0:T(8,128)}, f32[24,256]{1,0:T(8,128)}, f32[24,256]{1,0:T(8,128)}) custom-call(f32[64,256]{1,0:T(8,128)} %height_in.5, f32[64,256]{1,0:T(8,128)} %flux_u_in.5, f32[64,256]{1,0:T(8,128)} %flux_v_in.5, f32[64,256]{1,0:T(8,128)} %depth_in.5, s32[64,256]{1,0:T(8,128)} %mask_in.7, f32[64,256]{1,0:T(8,128)} %flux_in.5, ...), custom_call_target="tpu_custom_call" | custom-call | flops 805306368 | bytes 3145728 | tf_op jit(solution)/shard_map/forward/pallas_call | solution.py:652
  4.4 11.5 %all-to-all-start = ((f32[128,8,128]{2,1,0:T(8,128)}), f32[128,8,128]{2,1,0:T(8,128)S(1)}, u32[]{:S(2)}, u32[]{:S(2)}) async-start(f32[128,8,128]{2,1,0:T(8,128)} %get-tuple-element.18), calls=%async_computation | async-start | bytes 1048576 | tf_op jit(solution)/shard_map/all_to_all | solution.py:702
  15.9 3.7 %collective-permute-start = (f32[24,256]{1,0:T(8,128)}, f32[24,256]{1,0:T(8,128)S(1)}, u32[]{:S(2)}, u32[]{:S(2)}) collective-permute-start(f32[24,256]{1,0:T(8,128)} %get-tuple-element.19), channel_id=1, source_target_pairs={{0,16},{16,32},{32,48},{48,64},{64,80},{80,96},{96,112},{1,17},{17... | collective-permute-start | bytes 73736 | tf_op jit(solution)/shard_map/ppermute | solution.py:706
  19.6 1.9 %collective-permute-start.1 = (f32[24,256]{1,0:T(8,128)}, f32[24,256]{1,0:T(8,128)S(1)}, u32[]{:S(2)}, u32[]{:S(2)}) collective-permute-start(f32[24,256]{1,0:T(8,128)} %get-tuple-element.20), channel_id=1, source_target_pairs={{16,0},{32,16},{48,32},{64,48},{80,64},{96,80},{112,96},{17,1},{33... | collective-permute-start | bytes 73736 | tf_op jit(solution)/shard_map/ppermute | solution.py:707
  21.5 1.9 %gains.1.gains_in = f32[22,16,256]{2,1,0:T(8,128)} custom-call(f32[8,128]{1,0:T(8,128)} %bitcast.1, f32[128,8,1024]{2,1,0:T(8,128)} %constant.18.clone.balance_in), custom_call_target="tpu_custom_call" | custom-call | flops 2097152 | bytes 1048576 | tf_op jit(solution)/shard_map/gains/pallas_call | solution.py:652
  23.4 0.0 collective-permute-done.south_in
  23.4 0.0 copy-start
  23.4 2.3 %collective-permute-done.1.north_in = f32[24,256]{1,0:T(8,128)S(1)} collective-permute-done((f32[24,256]{1,0:T(8,128)}, f32[24,256]{1,0:T(8,128)S(1)}, u32[]{:S(2)}, u32[]{:S(2)}) %collective-permute-start.1) | collective-permute-done | bytes 24608 | tf_op jit(solution)/shard_map/ppermute | solution.py:707
  25.7 0.0 copy-start.1
  25.7 3.5 %all-to-all-done.received = f32[128,8,128]{2,1,0:T(8,128)S(1)} async-done(((f32[128,8,128]{2,1,0:T(8,128)}), f32[128,8,128]{2,1,0:T(8,128)S(1)}, u32[]{:S(2)}, u32[]{:S(2)}) %all-to-all-start) | async-done | bytes 524320 | tf_op jit(solution)/shard_map/all_to_all | solution.py:702
  29.3 4.9 %legendre.1 = f32[128,8,128]{2,1,0:T(8,128)} custom-call(f32[128,8,128]{2,1,0:T(8,128)S(1)} %all-to-all-done.received, f32[22,16,256]{2,1,0:T(8,128)} %gains.1.gains_in, f32[128,8,1024]{2,1,0:T(8,128)} %constant.18.clone.balance_in, f32[8,128]{1,0:T(8,128)} %constant.19.clone.seeds_in, f32[3,8,256]{2,1,0:T(8,128)} %constant.16.clone.north_in), custom_call_target="tpu_custom_call" | custom-call | flops 1610612736 | bytes 9437184 | tf_op jit(solution)/shard_map/legendre/pallas_call | solution.py:652
  34.1 4.9 %all-to-all-start.1 = ((f32[128,8,128]{2,1,0:T(8,128)}), f32[128,8,128]{2,1,0:T(8,128)S(1)}, u32[]{:S(2)}, u32[]{:S(2)}) async-start(f32[128,8,128]{2,1,0:T(8,128)} %legendre.1), calls=%async_computation.1 | async-start | bytes 1048576 | tf_op jit(solution)/shard_map/all_to_all | solution.py:746
  39.0 0.0 copy-done
  39.0 0.0 copy-done.1
  39.1 2.0 %columns.1 = (f32[24,128]{1,0:T(8,128)}, f32[24,128]{1,0:T(8,128)}) custom-call(f32[64,256]{1,0:T(8,128)} %height_in.5, f32[64,256]{1,0:T(8,128)} %flux_u_in.5, f32[64,256]{1,0:T(8,128)} %flux_v_in.5, f32[64,256]{1,0:T(8,128)} %depth_in.5, s32[64,256]{1,0:T(8,128)} %mask_in.7, f32[64,256]{1,0:T(8,128)} %flux_in.5, f32[24,256]{1,0:T(8,128)} %copy-done, ...), custom_call_target="tpu_custom_call" | custom-call | tf_op jit(solution)/shard_map/columns/pallas_call | solution.py:652
  41.1 1.5 %collective-permute-start.2 = (f32[24,128]{1,0:T(8,128)}, f32[24,128]{1,0:T(8,128)S(1)}, u32[]{:S(2)}, u32[]{:S(2)}) collective-permute-start(f32[24,128]{1,0:T(8,128)} %get-tuple-element.24), channel_id=1, source_target_pairs={{0,1},{1,2},{2,3},{3,4},{4,5},{5,6},{6,7},{7,8},{8,9},{9,10},{10,1... | collective-permute-start | bytes 36872 | tf_op jit(solution)/shard_map/ppermute | solution.py:763
  42.5 3.5 %collective-permute-start.3 = (f32[24,128]{1,0:T(8,128)}, f32[24,128]{1,0:T(8,128)S(1)}, u32[]{:S(2)}, u32[]{:S(2)}) collective-permute-start(f32[24,128]{1,0:T(8,128)} %get-tuple-element.25), channel_id=1, source_target_pairs={{1,0},{2,1},{3,2},{4,3},{5,4},{6,5},{7,6},{8,7},{9,8},{10,9},{11,1... | collective-permute-start | bytes 36872 | tf_op jit(solution)/shard_map/ppermute | solution.py:764
  46.1 3.6 %collective-permute-done.2.west_in = f32[24,128]{1,0:T(8,128)S(1)} collective-permute-done((f32[24,128]{1,0:T(8,128)}, f32[24,128]{1,0:T(8,128)S(1)}, u32[]{:S(2)}, u32[]{:S(2)}) %collective-permute-start.2) | collective-permute-done | bytes 12320 | tf_op jit(solution)/shard_map/ppermute | solution.py:763
  49.7 0.0 copy-start.2
  49.7 0.0 collective-permute-done.3.east_in
  49.7 0.6 %copy-done.2 = f32[24,128]{1,0:T(8,128)} copy-done((f32[24,128]{1,0:T(8,128)}, f32[24,128]{1,0:T(8,128)S(1)}, u32[]{:S(2)}) %copy-start.2) | copy-done | bytes 12312
  50.3 0.0 copy-start.3
  50.3 0.6 %copy-done.3 = f32[24,128]{1,0:T(8,128)} copy-done((f32[24,128]{1,0:T(8,128)}, f32[24,128]{1,0:T(8,128)S(1)}, u32[]{:S(2)}) %copy-start.3) | copy-done | bytes 12312
  50.9 3.3 %substeps.1 = (f32[3,64,256]{2,1,0:T(8,128)}, f32[3,64,256]{2,1,0:T(8,128)}) custom-call(f32[64,256]{1,0:T(8,128)} %height_in.5, f32[64,256]{1,0:T(8,128)} %flux_u_in.5, f32[64,256]{1,0:T(8,128)} %flux_v_in.5, f32[64,256]{1,0:T(8,128)} %depth_in.5, s32[64,256]{1,0:T(8,128)} %mask_in.7, f32[64,256]{1,0:T(8,128)} %flux_in.5, f32[24,256]{1,0:T(8,128)} %copy-done, ...), custom_call_target="tpu_custom_call" | custom-call | tf_op jit(solution)/shard_map/substeps/pallas_call | solution.py:652
  54.2 0.0 all-to-all-done.1.received
  54.2 3.0 %inverse.1 = (f32[64,256]{1,0:T(8,128)}, f32[64,256]{1,0:T(8,128)}, f32[64,256]{1,0:T(8,128)}, f32[64,256]{1,0:T(8,128)}) custom-call(f32[128,8,128]{2,1,0:T(8,128)S(1)} %all-to-all-done.1.received, s32[64,256]{1,0:T(8,128)} %mask_in.7, bf16[4,1024,256]{2,1,0:T(8,128)(2,1)} %constant.14.clone.wave_in, f32[16,32,128]{2,1,0:T(8,128)} %constant.15.clone.phase_in, ...), custom_call_target="tpu_custom_call" | custom-call | tf_op jit(solution)/shard_map/inverse/pallas_call | solution.py:652
Async XLA Ops:
  4.4 24.9 %all-to-all-start = ((f32[128,8,128]{2,1,0:T(8,128)}), f32[128,8,128]{2,1,0:T(8,128)S(1)}, u32[]{:S(2)}, u32[]{:S(2)}) async-start(f32[128,8,128]{2,1,0:T(8,128)} %get-tuple-element.18), calls=%async_computation | async-start | bytes 1048576 | tf_op jit(solution)/shard_map/all_to_all | solution.py:702
  15.9 7.5 %collective-permute-start = (f32[24,256]{1,0:T(8,128)}, f32[24,256]{1,0:T(8,128)S(1)}, u32[]{:S(2)}, u32[]{:S(2)}) collective-permute-start(f32[24,256]{1,0:T(8,128)} %get-tuple-element.19), channel_id=1, source_target_pairs={{0,16},{16,32},{32,48},{48,64},{64,80},{80,96},{96,112},{1,17},{17... | collective-permute-start | bytes 73736 | tf_op jit(solution)/shard_map/ppermute | solution.py:706
  19.6 6.1 %collective-permute-start.1 = (f32[24,256]{1,0:T(8,128)}, f32[24,256]{1,0:T(8,128)S(1)}, u32[]{:S(2)}, u32[]{:S(2)}) collective-permute-start(f32[24,256]{1,0:T(8,128)} %get-tuple-element.20), channel_id=1, source_target_pairs={{16,0},{32,16},{48,32},{64,48},{80,64},{96,80},{112,96},{17,1},{33... | collective-permute-start | bytes 73736 | tf_op jit(solution)/shard_map/ppermute | solution.py:707
  23.4 15.6 %copy-start = (f32[24,256]{1,0:T(8,128)}, f32[24,256]{1,0:T(8,128)S(1)}, u32[]{:S(2)}) copy-start(f32[24,256]{1,0:T(8,128)S(1)} %collective-permute-done.south_in) | copy-start | bytes 73732
  25.7 13.3 %copy-start.1 = (f32[24,256]{1,0:T(8,128)}, f32[24,256]{1,0:T(8,128)S(1)}, u32[]{:S(2)}) copy-start(f32[24,256]{1,0:T(8,128)S(1)} %collective-permute-done.1.north_in) | copy-start | bytes 73732
  34.1 20.0 %all-to-all-start.1 = ((f32[128,8,128]{2,1,0:T(8,128)}), f32[128,8,128]{2,1,0:T(8,128)S(1)}, u32[]{:S(2)}, u32[]{:S(2)}) async-start(f32[128,8,128]{2,1,0:T(8,128)} %legendre.1), calls=%async_computation.1 | async-start | bytes 1048576 | tf_op jit(solution)/shard_map/all_to_all | solution.py:746
  41.1 8.6 %collective-permute-start.2 = (f32[24,128]{1,0:T(8,128)}, f32[24,128]{1,0:T(8,128)S(1)}, u32[]{:S(2)}, u32[]{:S(2)}) collective-permute-start(f32[24,128]{1,0:T(8,128)} %get-tuple-element.24), channel_id=1, source_target_pairs={{0,1},{1,2},{2,3},{3,4},{4,5},{5,6},{6,7},{7,8},{8,9},{9,10},{10,1... | collective-permute-start | bytes 36872 | tf_op jit(solution)/shard_map/ppermute | solution.py:763
  42.5 7.1 %collective-permute-start.3 = (f32[24,128]{1,0:T(8,128)}, f32[24,128]{1,0:T(8,128)S(1)}, u32[]{:S(2)}, u32[]{:S(2)}) collective-permute-start(f32[24,128]{1,0:T(8,128)} %get-tuple-element.25), channel_id=1, source_target_pairs={{1,0},{2,1},{3,2},{4,3},{5,4},{6,5},{7,6},{8,7},{9,8},{10,9},{11,1... | collective-permute-start | bytes 36872 | tf_op jit(solution)/shard_map/ppermute | solution.py:764
  49.7 0.6 %copy-start.2 = (f32[24,128]{1,0:T(8,128)}, f32[24,128]{1,0:T(8,128)S(1)}, u32[]{:S(2)}) copy-start(f32[24,128]{1,0:T(8,128)S(1)} %collective-permute-done.2.west_in) | copy-start | bytes 36868
  50.3 0.6 %copy-start.3 = (f32[24,128]{1,0:T(8,128)}, f32[24,128]{1,0:T(8,128)S(1)}, u32[]{:S(2)}) copy-start(f32[24,128]{1,0:T(8,128)S(1)} %collective-permute-done.3.east_in) | copy-start | bytes 36868

commit v3 on v2

v3 whole, which is shorter than its diff:
```python
import math

import jax
import jax.numpy as jnp
import ml_dtypes
import numpy as np
from jax import lax
from jax.experimental import pallas as pl
from jax.experimental.pallas import tpu as pltpu
from jax.sharding import PartitionSpec as P

ITERS = 4
NLON = 4096
NLAT = 512
DEG = 1024
LATS = 8
LONS = 16
DEVS = LATS * LONS
ROWS = NLAT // LATS
COLS = NLON // LONS
HALF = NLAT // 2
ORDERS = DEG // DEVS
WIDE = 4
FIELDS = 6
PAD_ROWS = ROWS + 2 * WIDE
PAD_COLS = COLS + 128
STRIP = FIELDS * WIDE
CHUNK = 128
CHUNKS = DEG // CHUNK
TILE = 256

step_time = 0.5
sal_ratio = 3.0 * 1035.0 / 5517.0
spacing = 2.0 * math.pi / NLON

f32 = jnp.float32
bf16 = jnp.bfloat16


def split_table(values):
    high = values.astype(ml_dtypes.bfloat16)
    low = (values - high.astype(np.float64)).astype(ml_dtypes.bfloat16)
    return high, low


def wave_tables():
    order = (np.arange(DEVS)[:, None] + DEVS * np.arange(ORDERS)[None, :]).reshape(-1)
    angle = (order[:, None] * np.arange(COLS)[None, :] % NLON) * (2.0 * math.pi / NLON)
    cos_high, cos_low = split_table(np.cos(angle))
    sin_high, sin_low = split_table(np.sin(angle))
    return np.stack([cos_high, sin_high, cos_low, sin_low])


def phase_tables():
    angle = np.arange(LONS)[:, None] * np.arange(LONS)[None, :] % LONS * (2.0 * math.pi / LONS)
    left = np.broadcast_to(np.array([np.cos(angle), -np.sin(angle)])[..., None], (2, LONS, LONS, 64))
    right = np.broadcast_to(np.array([np.sin(angle), np.cos(angle)])[..., None], (2, LONS, LONS, 64))
    both = np.concatenate([left, right], axis=-1).transpose(1, 0, 2, 3)
    return both.reshape(LONS, 2 * LONS, 128).astype(np.float32)


def balance_table():
    order = np.arange(DEG, dtype=np.float64)
    scale = np.ones(DEG)
    squares = []
    for step in range(DEG):
        squares.append(scale * scale)
        degree = order + step + 1.0
        factor = np.sqrt((4.0 * degree * degree - 1.0) / (degree * degree - order * order))
        scale = factor / scale
    return np.stack(squares, axis=1).reshape(ORDERS, DEVS, DEG).transpose(1, 0, 2).astype(np.float32)


def latitude_of(rows):
    return (rows + 0.5 - NLAT / 2) * spacing


def row_tables():
    local = np.concatenate([np.arange(ROWS + WIDE), np.arange(-WIDE, 0)])
    latitude = latitude_of(np.arange(LATS)[:, None] * ROWS + local[None, :])
    both = np.stack([1.0 / np.cos(latitude), np.cos(latitude + spacing / 2)], axis=1)
    return np.broadcast_to(both[..., None], both.shape + (128,)).astype(np.float32)


def area_table():
    latitude = latitude_of(np.arange(NLAT)).reshape(LATS, ROWS, 1)
    return np.broadcast_to(np.cos(latitude), (LATS, ROWS, 128)).astype(np.float32)


def north_tables():
    latitude = latitude_of(np.arange(HALF, NLAT))
    weight = np.cos(latitude) * spacing * spacing / (4.0 * math.pi)
    table = np.stack([np.sin(latitude), np.log(np.cos(latitude)), weight])
    return np.broadcast_to(table[:, None, :], (3, 8, HALF)).astype(np.float32)


def seed_table():
    order = np.arange(1, DEG)
    grown = 0.5 * math.log(2.0) + 0.5 * np.cumsum(np.log((2.0 * order + 1.0) / (2.0 * order)))
    return np.concatenate([[0.0], grown]).reshape(ORDERS, DEVS).astype(np.float32)


def iota(shape, dim):
    return lax.broadcasted_iota(jnp.int32, shape, dim)


def halves(values):
    high = values.astype(bf16)
    low = (values - high.astype(f32)).astype(bf16)
    return high, low


def dot_nt(left, right):
    return lax.dot_general(left, right, (((1,), (1,)), ((), ())), preferred_element_type=f32)


def dot_nn(left, right):
    return lax.dot_general(left, right, (((1,), (0,)), ((), ())), preferred_element_type=f32)


def fetch(pairs, sems):
    copies = [pltpu.make_async_copy(a, b, sems.at[slot]) for slot, (a, b) in enumerate(pairs)]
    for copy in copies:
        copy.start()
    return copies


def row_order(lat_index):
    row = iota((ROWS, ROWS), 0)
    col = iota((ROWS, ROWS), 1)
    south = lat_index < LATS // 2
    return jnp.where(south, (row + col == ROWS - 1).astype(f32), (row == col).astype(f32))


def forward_kernel(
    height_in,
    flux_u_in,
    flux_v_in,
    depth_in,
    mask_in,
    flux_in,
    wave_in,
    phase_in,
    area_in,
    message_out,
    north_out,
    south_out,
    tiles,
    mask,
    wave,
    phase,
    area,
    message,
    strips,
    sems,
    send_sems,
    strip_sems,
):
    lat_index = lax.axis_index("lat")
    lon_index = lax.axis_index("lon")
    loads = fetch(
        (
            (mask_in, mask),
            (height_in, tiles.at[0]),
            (wave_in, wave),
            (phase_in.at[lon_index], phase),
            (flux_in, tiles.at[4]),
            (area_in.at[lat_index], area),
            (flux_u_in, tiles.at[1]),
            (flux_v_in, tiles.at[2]),
            (depth_in, tiles.at[3]),
        ),
        sems,
    )
    loads[0].wait()
    loads[1].wait()
    sea = mask[...].astype(f32)
    mass_high, mass_low = halves(sea * tiles[0])
    both = jnp.concatenate([mass_high, mass_low], axis=1)
    both = dot_nn(row_order(lat_index).astype(bf16), both).astype(bf16)
    mass_high, mass_low = both[:, :COLS], both[:, COLS:]
    twice = jnp.concatenate([mass_high, mass_high], axis=0)
    all_parts = jnp.concatenate([twice, mass_low, mass_low], axis=0)

    for load in loads[3:6]:
        load.wait()
    band = area[...]
    area_cells = sea * jnp.concatenate([band, band], axis=1)
    flux_sum = jnp.sum(area_cells * tiles[4])
    area_sum = jnp.sum(area_cells)
    row = iota((8, 128), 0)
    lane = iota((8, 128), 1)

    loads[2].wait()
    sends = []
    share = DEVS // 4
    for quarter in range(4):
        place = slice(quarter * share * ORDERS, (quarter + 1) * share * ORDERS)
        cos_parts = dot_nt(wave[0, place], all_parts)
        sin_parts = dot_nt(wave[1, place], all_parts)
        cos_sums = cos_parts[:, :128] + cos_parts[:, 128:] + dot_nt(wave[2, place], twice)
        sin_sums = sin_parts[:, :128] + sin_parts[:, 128:] + dot_nt(wave[3, place], twice)
        for spot in range(share):
            device = quarter * share + spot
            turn = device % LONS
            rows = slice(spot * ORDERS, (spot + 1) * ORDERS)
            sent = (
                phase[turn : turn + 1, :] * cos_sums[rows]
                + phase[LONS + turn : LONS + turn + 1, :] * sin_sums[rows]
            )
            if device == 0:
                sent = jnp.where((row == 0) & (lane >= 64), area_sum, sent)
                sent = jnp.where((row == 0) & (lane == 64), flux_sum, sent)
            message[device] = sent
        place = pl.ds(quarter * share, share)
        pair = (message.at[place], message_out.at[place])
        sends += fetch((pair,), send_sems.at[pl.ds(quarter, 1)])

    for load in loads[6:]:
        load.wait()
    for slot, values in enumerate((tiles[0], tiles[1], tiles[2], tiles[3], sea, tiles[4])):
        strips[0, slot * WIDE : (slot + 1) * WIDE, :] = values[ROWS - WIDE :, :]
        strips[1, slot * WIDE : (slot + 1) * WIDE, :] = values[:WIDE, :]
    sends += fetch(((strips.at[0], north_out), (strips.at[1], south_out)), strip_sems)
    for copy in sends:
        copy.wait()


def tiles_of():
    found = []
    for chunk in range(CHUNKS):
        kept = 8 if chunk < 4 else 4 if chunk < 6 else 2
        steps = TILE // kept
        found += [(chunk, first, steps, kept) for first in range(0, CHUNK, steps)]
    return found


TILES = tiles_of()


def make_gains(love, balance, device, gains):
    lane = iota((8, 128), 1)
    degree = (128 * iota((8, 128), 0) + lane).astype(f32)
    gain = sal_ratio * love[...] / (2.0 * degree + 1.0)
    turned = pltpu.roll(gain, (128 - device) % 128, 1)
    above = jnp.concatenate([turned[1:], jnp.zeros((1, 128), f32)], axis=0)
    shifted = jnp.where(lane + device < 128, turned, above)
    padded = jnp.concatenate([shifted, jnp.zeros((8, 128), f32)], axis=0)
    column = iota((ORDERS, TILE), 1)
    for kept in sorted({kept for _, _, _, kept in TILES}):
        slots = [slot for slot in range(len(TILES)) if TILES[slot][3] == kept]
        chunks = sorted({TILES[slot][0] for slot in slots})
        blocks = [padded[c : c + 8] * balance[:, c * CHUNK : (c + 1) * CHUNK] for c in chunks]
        parts = jnp.concatenate(halves(jnp.concatenate(blocks, axis=0)), axis=0)
        half = len(chunks) * ORDERS
        same = column % kept == iota((ORDERS, TILE), 0)
        even_step = (column // kept) % 2 == 0
        for begin in sorted({TILES[slot][1] for slot in slots}):
            spread = iota((CHUNK, TILE), 1) // kept + begin == iota((CHUNK, TILE), 0)
            wide = dot_nn(parts, spread.astype(f32).astype(bf16))
            wide = wide[:half] + wide[half:]
            for spot, chunk in enumerate(chunks):
                slot = [slot for slot in slots if TILES[slot][:2] == (chunk, begin)][0]
                here = jnp.where(same, wide[spot * ORDERS : (spot + 1) * ORDERS], 0.0)
                even = jnp.where(even_step, here, 0.0)
                gains[slot, 0:8, :] = even
                gains[slot, 8:16, :] = here - even


def setup_kernel(
    love_in,
    balance_in,
    seeds_in,
    north_in,
    phase_in,
    gains,
    balance,
    start,
    phase,
    love,
    seeds,
    north,
    sems,
):
    device = lax.axis_index("lat") * LONS + lax.axis_index("lon")
    loads = fetch(
        (
            (seeds_in, seeds),
            (north_in, north),
            (balance_in.at[device], balance),
            (love_in, love),
            (phase_in.at[lax.axis_index("lon")], phase),
        ),
        sems,
    )
    for load in loads:
        load.wait()
    lane = iota((8, 128), 1)
    seed_log = jnp.sum(jnp.where(lane == device, seeds[...], 0.0), axis=1, keepdims=True)
    order = (device + DEVS * iota((8, 128), 0)).astype(f32)[:, :1]
    start[...] = jnp.exp(seed_log + order * north[1])
    make_gains(love, balance, device, gains)


def legendre_kernel(
    received, gains, balance, start, north, message_out, high, low, message, out_sems
):
    device = lax.axis_index("lat") * LONS + lax.axis_index("lon")
    lane = iota((8, 128), 1)
    row = iota((8, 128), 0)
    left = lane < 64

    bands = []
    for lat in range(LATS):
        band = received[lat * LONS]
        for lon in range(1, LONS):
            band = band + received[lat * LONS + lon]
        bands.append(band)
    sums = bands[0]
    for band in bands[1:]:
        sums = sums + band
    even = [bands[4 + part] + bands[3 - part] for part in range(4)]
    odd = [bands[4 + part] - bands[3 - part] for part in range(4)]

    def arrange(parts):
        cos_parts = []
        sin_parts = []
        for first, second in ((parts[0], parts[1]), (parts[2], parts[3])):
            cos_parts.append(jnp.where(left, first, pltpu.roll(second, 64, 1)))
            sin_parts.append(jnp.where(left, pltpu.roll(first, 64, 1), second))
        weight = north[2]
        return [
            jnp.concatenate(cos_parts, axis=1) * weight,
            jnp.concatenate(sin_parts, axis=1) * weight,
        ]

    rows_high, rows_low = halves(jnp.concatenate(arrange(even) + arrange(odd), axis=0))
    rows_both = jnp.concatenate([rows_high, rows_low], axis=0)

    sine = north[0]
    state = [jnp.zeros((ORDERS, HALF), f32), start[...]]
    wide_row = iota((ORDERS, HALF), 0)

    def extend(slot):
        chunk, first, steps, kept = TILES[slot]
        share = ORDERS // kept
        packed = []
        for step in range(first, first + steps, share):
            block = None
            for part in range(share):
                previous, current = state
                spot = chunk * CHUNK + step + part
                if part == 0:
                    block = current
                else:
                    moved = pltpu.roll(current, part * kept, 0)
                    block = jnp.where(wide_row < part * kept, block, moved)
                turn = balance[:, spot : spot + 1] * sine
                state[0], state[1] = current, turn * current - previous
            packed.append(block)
            if len(packed) == 2:
                place = slice(slot * TILE + (step - first) // share * 8 - 8, None)
                place = slice(place.start, place.start + 16)
                high[place, :], low[place, :] = halves(jnp.concatenate(packed, axis=0))
                packed = []

    def analyse(slot):
        place = slice(slot * TILE, (slot + 1) * TILE)
        both = dot_nt(rows_both, high[place, :])
        coefs = both[:32] + both[32:] + dot_nt(rows_high, low[place, :])
        even, odd = gains[slot, 0:8, :], gains[slot, 8:16, :]
        coefs_high, coefs_low = halves(coefs * jnp.concatenate([even, even, odd, odd], axis=0))
        return jnp.concatenate([coefs_high, coefs_low], axis=0)

    def synthesise(slot, coefs):
        place = slice(slot * TILE, (slot + 1) * TILE)
        return dot_nn(coefs, high[place, :]), dot_nn(coefs[:32], low[place, :])

    count = len(TILES)
    total_high = jnp.zeros((64, HALF), f32)
    total_low = jnp.zeros((32, HALF), f32)
    coefs = {}
    for turn in range(count + 2):
        if turn < count:
            extend(turn)
        if 1 <= turn <= count:
            coefs[turn - 1] = analyse(turn - 1)
        if turn >= 2:
            more_high, more_low = synthesise(turn - 2, coefs.pop(turn - 2))
            total_high = total_high + more_high
            total_low = total_low + more_low
    total = total_high[:32] + total_high[32:] + total_low

    flux_sum = jnp.sum(jnp.where((row == 0) & (lane == 64), sums, 0.0))
    area_sum = jnp.sum(jnp.where((row == 0) & (lane == 65), sums, 0.0))
    mean = jnp.full((8, 128), flux_sum, f32) / jnp.full((8, 128), area_sum, f32)
    slot = (device == 0) & (row == 0) & (lane >= 64)
    cos_even, sin_even = total[0:8, :], total[8:16, :]
    cos_odd, sin_odd = total[16:24, :], total[24:32, :]
    copies = []
    for north_side in (True, False):
        if north_side:
            cos_all, sin_all = cos_even + cos_odd, sin_even + sin_odd
        else:
            cos_all, sin_all = cos_even - cos_odd, sin_even - sin_odd
        for part in range(4):
            block = slice(128 * (part // 2), 128 * (part // 2) + 128)
            cos_part, sin_part = cos_all[:, block], sin_all[:, block]
            if part % 2 == 0:
                sent = jnp.where(left, cos_part, pltpu.roll(sin_part, 64, 1))
            else:
                sent = jnp.where(left, pltpu.roll(cos_part, 64, 1), sin_part)
            sent = jnp.where(slot, mean, sent)
            lat = 4 + part if north_side else 3 - part
            for lon in range(LONS):
                message[lat * LONS + lon] = sent
            part_place = pl.ds(lat * LONS, LONS)
            copies += fetch(((message.at[part_place], message_out.at[part_place]),), out_sems.at[pl.ds(lat, 1)])
    for copy in copies:
        copy.wait()


def finish_kernel(
    received,
    phase,
    west_in,
    east_in,
    wave,
    blocks_in,
    bands_in,
    height_out,
    u_out,
    v_out,
    sal_out,
    blocks,
    bands,
    turned_scratch,
    results,
    sems,
    out_sems,
):
    lat_index = lax.axis_index("lat")
    loads = fetch(
        (
            (blocks_in, blocks.at[:, :, pl.ds(0, COLS)]),
            (bands_in.at[lat_index], bands),
        ),
        sems,
    )
    lane = iota((8, 128), 1)
    left = lane < 64
    for device in range(DEVS):
        turn = device % LONS
        part = received[device]
        first, second = phase[turn : turn + 1, :], phase[LONS + turn : LONS + turn + 1, :]
        cos_turn = jnp.where(left[:1], first, second)
        sin_turn = -jnp.where(left[:1], second, first)
        turned_scratch[device * ORDERS : (device + 1) * ORDERS, :] = (
            cos_turn * part + sin_turn * pltpu.roll(part, 64, 1)
        )
    mean = jnp.sum(jnp.where((iota((8, 128), 0) == 0) & (lane == 64), received[0], 0.0))
    turned = turned_scratch[...].T
    high, low = halves(turned)
    cos_both = jnp.concatenate([high[:64], low[:64]], axis=0)
    sin_both = jnp.concatenate([high[64:], low[64:]], axis=0)

    wide_lane = iota((PAD_ROWS, 128), 1)
    fill = jnp.zeros((128 - STRIP, 128), f32)
    west = jnp.concatenate([west_in[...], fill], axis=0).T[:PAD_ROWS, :]
    east = jnp.concatenate([east_in[...], fill], axis=0).T[:PAD_ROWS, :]
    for slot in range(FIELDS):
        high_side = pltpu.roll(east, 128 - slot * WIDE, 1) if slot else east
        low_side = pltpu.roll(west, 128 - WIDE - slot * WIDE, 1)
        blocks[slot, :, COLS:] = jnp.where(
            wide_lane < WIDE, high_side, jnp.where(wide_lane >= 128 - WIDE, low_side, 0.0)
        )
    for load in loads:
        load.wait()

    both = dot_nn(cos_both, wave[0]) + dot_nn(sin_both, wave[1])
    field = both[:64] + both[64:] + dot_nn(high[:64], wave[2]) + dot_nn(high[64:], wave[3])
    field_high, field_low = halves(field)
    order = row_order(lat_index).astype(bf16)
    field = dot_nn(order, field_high) + dot_nn(order, field_low)

    def eastward(values):
        return pltpu.roll(values, PAD_COLS - 1, 1)

    def northward(values):
        return pltpu.roll(values, PAD_ROWS - 1, 0)

    height_now, u_now, v_now, depth_all, sea, flux_all = [blocks[slot] for slot in range(FIELDS)]
    inverse_cos = jnp.concatenate([bands[0]] * 3, axis=1)
    north_cos = jnp.concatenate([bands[1]] * 3, axis=1)
    open_u = sea * eastward(sea)
    open_v = sea * northward(sea)
    pull_u = open_u * (0.5 * step_time) * (depth_all + eastward(depth_all)) * inverse_cos
    pull_v = open_v * (0.5 * step_time) * (depth_all + northward(depth_all))
    scale = step_time * inverse_cos
    forcing = step_time * sea * (flux_all - mean)
    for repeat in range(ITERS):
        north_flux = v_now * north_cos
        divergence = u_now - pltpu.roll(u_now, 1, 1) + (north_flux - pltpu.roll(north_flux, 1, 0))
        height_now = height_now - scale * divergence + forcing
        u_now = open_u * u_now - pull_u * (eastward(height_now) - height_now)
        v_now = open_v * v_now - pull_v * (northward(height_now) - height_now)
    for slot, values in enumerate((height_now, u_now, v_now)):
        results[slot] = values[:ROWS, :COLS]
    results[3] = field * sea[:ROWS, :COLS]
    outs = (height_out, u_out, v_out, sal_out)
    for copy in fetch([(results.at[slot], out) for slot, out in enumerate(outs)], out_sems):
        copy.wait()


def column_kernel(
    height_in,
    flux_u_in,
    flux_v_in,
    depth_in,
    mask_in,
    flux_in,
    south_in,
    north_in,
    west_out,
    east_out,
    blocks_out,
    mask,
    strips,
    sides,
    blocks,
    sems,
    out_sems,
):
    own = pl.ds(0, ROWS)
    loads = fetch(
        (
            (south_in, strips.at[0]),
            (north_in, strips.at[1]),
            (height_in, blocks.at[0, own]),
            (flux_u_in, blocks.at[1, own]),
            (flux_v_in, blocks.at[2, own]),
            (depth_in, blocks.at[3, own]),
            (mask_in, mask),
            (flux_in, blocks.at[5, own]),
        ),
        sems,
    )
    lane = iota((PAD_ROWS, 128), 1)
    west = jnp.zeros((PAD_ROWS, 128), f32)
    east = jnp.zeros((PAD_ROWS, 128), f32)
    for load in loads:
        load.wait()
    blocks[4, 0:ROWS, :] = mask[...].astype(f32)
    for slot in range(FIELDS):
        blocks[slot, ROWS : ROWS + WIDE, :] = strips[1, slot * WIDE : (slot + 1) * WIDE, :]
        blocks[slot, ROWS + WIDE : PAD_ROWS, :] = strips[0, slot * WIDE : (slot + 1) * WIDE, :]
        here = (lane >= slot * WIDE) & (lane < (slot + 1) * WIDE)
        west_part = blocks[slot, :, 0:128]
        east_part = pltpu.roll(blocks[slot, :, COLS - 128 : COLS], (WIDE + slot * WIDE) % 128, 1)
        if slot:
            west_part = pltpu.roll(west_part, slot * WIDE, 1)
        west = jnp.where(here, west_part, west)
        east = jnp.where(here, east_part, east)
    fill = jnp.zeros((128 - PAD_ROWS, 128), f32)
    sides[0] = jnp.concatenate([west, fill], axis=0).T[:STRIP, :]
    sides[1] = jnp.concatenate([east, fill], axis=0).T[:STRIP, :]
    pairs = ((sides.at[0], west_out), (sides.at[1], east_out), (blocks, blocks_out))
    for copy in fetch(pairs, out_sems):
        copy.wait()


def far_call(kernel, name, operands, results, scratch, work=None, here=(), near=(), near_out=False):
    placed = []
    specs = []
    out_space = pltpu.VMEM if near_out else pltpu.HBM
    for slot, operand in enumerate(operands):
        if slot in here:
            space = pltpu.VMEM
        elif slot in near:
            space = pltpu.VMEM
            operand = pltpu.with_memory_space_constraint(operand, pltpu.VMEM)
        else:
            space = pltpu.HBM
            operand = pltpu.with_memory_space_constraint(operand, pltpu.HBM)
        placed.append(operand)
        specs.append(pl.BlockSpec(memory_space=space))
    return pl.pallas_call(
        kernel,
        out_shape=tuple(out_space(shape, kind) for shape, kind in results),
        in_specs=specs,
        out_specs=(pl.BlockSpec(memory_space=out_space),) * len(results),
        scratch_shapes=scratch,
        compiler_params=pltpu.CompilerParams(vmem_limit_bytes=32 << 20),
        cost_estimate=work,
        name=name,
    )(*placed)


def cost(flops, moved):
    return pl.CostEstimate(flops=flops, bytes_accessed=moved, transcendentals=0)


def on_device(sea_height, trans_u, trans_v, depth, sea_mask, freshwater_flux, love_factor):
    both_axes = ("lat", "lon")
    wave = jnp.asarray(wave_tables())
    phase = jnp.asarray(phase_tables())
    north = jnp.asarray(north_tables())
    fields = (sea_height, trans_u, trans_v, depth, sea_mask, freshwater_flux)
    vmem = pltpu.VMEM
    copies = pltpu.SemaphoreType.DMA
    tile = ((ROWS, COLS), f32)
    strip = ((STRIP, COLS), f32)
    side = ((STRIP, 128), f32)
    messages = ((DEVS, 8, 128), f32)
    tiles = vmem((FIELDS, ROWS, COLS), f32)
    mask_tile = vmem((ROWS, COLS), jnp.int32)

    message, strip_north, strip_south = far_call(
        forward_kernel,
        "forward",
        fields + (wave, phase, jnp.asarray(area_table())),
        (messages, strip, strip),
        [
            tiles,
            mask_tile,
            vmem((4, DEG, COLS), bf16),
            vmem((2 * LONS, 128), f32),
            vmem((ROWS, 128), f32),
            vmem(*messages),
            vmem((2, STRIP, COLS), f32),
            copies((9,)),
            copies((4,)),
            copies((2,)),
        ],
        work=cost(6 * 2 * 1024 * 256 * 256, 3 << 20),
    )
    received = lax.all_to_all(message, both_axes, split_axis=0, concat_axis=0, tiled=True)

    upward = [(i, i + 1) for i in range(LATS - 1)]
    downward = [(i + 1, i) for i in range(LATS - 1)]
    from_south = lax.ppermute(strip_north, "lat", upward)
    from_north = lax.ppermute(strip_south, "lat", downward)

    gain_tiles = ((len(TILES), 16, TILE), f32)
    squares = ((ORDERS, DEG), f32)
    first_rows = ((ORDERS, HALF), f32)
    turns = ((2 * LONS, 128), f32)
    gains, balance, start, phase_here = far_call(
        setup_kernel,
        "setup",
        (
            love_factor.reshape(8, 128),
            jnp.asarray(balance_table()),
            jnp.asarray(seed_table()),
            north,
            phase,
        ),
        (gain_tiles, squares, first_rows, turns),
        [
            vmem((8, 128), f32),
            vmem((ORDERS, DEVS), f32),
            vmem((3, 8, HALF), f32),
            copies((5,)),
        ],
        work=cost(2 << 20, 1 << 20),
        near_out=True,
    )
    received, from_south, from_north = lax.optimization_barrier((received, from_south, from_north))
    table = ((len(TILES) * TILE, HALF), bf16)
    (reply,) = far_call(
        legendre_kernel,
        "legendre",
        (received, gains, balance, start, north),
        (messages,),
        [vmem(*table), vmem(*table), vmem(*messages), copies((LATS,))],
        work=cost(6 * 2 * 64 * 8192 * 256, 9 << 20),
        here=(0, 4),
        near=(1, 2, 3),
    )
    answer = lax.all_to_all(reply, both_axes, split_axis=0, concat_axis=0, tiled=True)

    padded = ((FIELDS, PAD_ROWS, COLS), f32)
    to_west, to_east, blocks = far_call(
        column_kernel,
        "columns",
        fields + (from_south, from_north),
        (side, side, padded),
        [
            mask_tile,
            vmem((2, STRIP, COLS), f32),
            vmem((2, STRIP, 128), f32),
            vmem(*padded),
            copies((8,)),
            copies((3,)),
        ],
    )
    from_west = lax.ppermute(to_east, "lon", [(i, (i + 1) % LONS) for i in range(LONS)])
    from_east = lax.ppermute(to_west, "lon", [((i + 1) % LONS, i) for i in range(LONS)])

    return far_call(
        finish_kernel,
        "finish",
        (answer, phase_here, from_west, from_east, wave, blocks, jnp.asarray(row_tables())),
        (tile,) * 4,
        [
            vmem((FIELDS, PAD_ROWS, PAD_COLS), f32),
            vmem((2, PAD_ROWS, 128), f32),
            vmem((DEG, 128), f32),
            vmem((4, ROWS, COLS), f32),
            copies((2,)),
            copies((4,)),
        ],
        here=(0, 2, 3, 4),
        near=(1,),
    )


def solution(mesh):
    tiles = P("lat", "lon")
    return jax.shard_map(
        on_device,
        mesh=mesh,
        in_specs=(tiles,) * 6 + (P(),),
        out_specs=(tiles,) * 4,
        check_vma=False,
    )
```

time: 57.7 us -> 54.3 us (0.941)
  Pallas kernels: 18.9 us -> 13.4 us
  waiting for transfers between devices: 9.43 us -> 12.8 us
  local copies, waits for them, and re-layouts: 1.2 us -> 0.02 us
    pallas_call x6 -> x5, Pallas kernels: 18.9 us -> 13.4 us  [far_call(): pl.pallas_call(kernel, out_shape=tuple((out_space(shape, kind) for shape,...]
    all_to_all x1, waiting for transfers between devices: 0.01 us -> 2.72 us  [on_device(): lax.all_to_all(reply, both_axes, split_axis=0, concat_axis=0, tiled=True)]
    unnamed x8, local copies, waits for them, and re-layouts: 1.2 us -> 0.02 us
    ppermute x1, waiting for transfers between devices: 2.27 us -> 3.02 us  [on_device(): from_north = lax.ppermute(strip_south, 'lat', downward)]
  transfers between devices with their start and end apart: 6 -> 6, of which waited for: 3 -> 4; matrix products, arithmetic and copies ran while one was open for 0% -> 0% of each run, Pallas kernels for 13% -> 6%
where the time goes in v3:
time: 54.3 us; the launch traced here: 53.9 us
  starting transfers between devices  26.9 us (50%)
  Pallas kernels  13.4 us (25%)
  waiting for transfers between devices  12.8 us (24%)
  between operations  0.75 us (1%)
    pallas_call x5, Pallas kernels, far_call(): pl.pallas_call(kernel, out_shape=tuple((out_space(shape, kind) for shape,...  13.4 us
    all_to_all x1, starting transfers between devices, on_device(): lax.all_to_all(message, both_axes, split_axis=0, concat_axis=0, tiled=True)  11.5 us
    all_to_all x1, starting transfers between devices, on_device(): lax.all_to_all(reply, both_axes, split_axis=0, concat_axis=0, tiled=True)  4.87 us
    ppermute x1, starting transfers between devices, on_device(): from_south = lax.ppermute(strip_north, 'lat', upward)  3.66 us
    all_to_all x1, waiting for transfers between devices, on_device(): lax.all_to_all(message, both_axes, split_axis=0, concat_axis=0, tiled=True)  3.55 us
    ppermute x1, starting transfers between devices, on_device(): lax.ppermute(to_west, 'lon', [((i + 1) % LONS, i) for i in range(LONS)])  3.53 us
    ppermute x1, waiting for transfers between devices, on_device(): lax.ppermute(to_east, 'lon', [(i, (i + 1) % LONS) for i in range(LONS)])  3.51 us
    ppermute x1, waiting for transfers between devices, on_device(): from_north = lax.ppermute(strip_south, 'lat', downward)  3.02 us
  transfers between devices with their start and end apart: 6, of which 4 were waited for; matrix products, arithmetic and copies ran while one was open for 0% of the time, Pallas kernels for 6%

profile of v3, /device:TPU:1, one launch (start us, length us, event | category | flops | bytes accessed | tf_op | source)
XLA Modules:
  0.0 53.9 jit_solution(1393916210954078351)
XLA Ops:
  0.6 0.0 copy-start.1
  0.6 3.2 %forward.1 = (f32[128,8,128]{2,1,0:T(8,128)}, f32[24,256]{1,0:T(8,128)}, f32[24,256]{1,0:T(8,128)}) custom-call(f32[64,256]{1,0:T(8,128)} %height_in.3, f32[64,256]{1,0:T(8,128)} %flux_u_in.3, f32[64,256]{1,0:T(8,128)} %flux_v_in.3, f32[64,256]{1,0:T(8,128)} %depth_in.3, s32[64,256]{1,0:T(8,128)} %mask_in.3, f32[64,256]{1,0:T(8,128)} %flux_in.3, ...), custom_call_target="tpu_custom_call" | custom-call | flops 805306368 | bytes 3145728 | tf_op jit(solution)/shard_map/forward/pallas_call | solution.py:587
  3.9 11.5 %all-to-all-start = ((f32[128,8,128]{2,1,0:T(8,128)}), f32[128,8,128]{2,1,0:T(8,128)S(1)}, u32[]{:S(2)}, u32[]{:S(2)}) async-start(f32[128,8,128]{2,1,0:T(8,128)} %get-tuple-element.17), calls=%async_computation | async-start | bytes 1048576 | tf_op jit(solution)/shard_map/all_to_all | solution.py:637
  15.4 3.7 %collective-permute-start = (f32[24,256]{1,0:T(8,128)}, f32[24,256]{1,0:T(8,128)S(1)}, u32[]{:S(2)}, u32[]{:S(2)}) collective-permute-start(f32[24,256]{1,0:T(8,128)} %get-tuple-element.18), channel_id=1, source_target_pairs={{0,16},{16,32},{32,48},{48,64},{64,80},{80,96},{96,112},{1,17},{17... | collective-permute-start | bytes 73736 | tf_op jit(solution)/shard_map/ppermute | solution.py:641
  19.1 1.9 %collective-permute-start.1 = (f32[24,256]{1,0:T(8,128)}, f32[24,256]{1,0:T(8,128)S(1)}, u32[]{:S(2)}, u32[]{:S(2)}) collective-permute-start(f32[24,256]{1,0:T(8,128)} %get-tuple-element.19), channel_id=1, source_target_pairs={{16,0},{32,16},{48,32},{64,48},{80,64},{96,80},{112,96},{17,1},{33... | collective-permute-start | bytes 73736 | tf_op jit(solution)/shard_map/ppermute | solution.py:642
  21.0 1.1 %setup.1 = (f32[22,16,256]{2,1,0:T(8,128)S(1)}, f32[8,1024]{1,0:T(8,128)S(1)}, f32[8,256]{1,0:T(8,128)S(1)}, f32[32,128]{1,0:T(8,128)S(1)}) custom-call(f32[8,128]{1,0:T(8,128)} %bitcast.1, f32[128,8,1024]{2,1,0:T(8,128)} %constant.18.clone.balance_in, f32[8,128]{1,0:T(8,128)} %constant.19.clone.seeds_in, f32[3,8,256]{2,1,0:T(8,128)} %constant.16.clone.north_in.north, ...), custom_call_target="tpu_custom_call" | custom-call | flops 2097152 | bytes 1048576 | tf_op jit(solution)/shard_map/setup/pallas_call | solution.py:587
  22.1 0.0 copy-start
  22.1 0.0 collective-permute-done.south_in
  22.1 0.0 copy-start.2
  22.2 3.0 %collective-permute-done.1.north_in = f32[24,256]{1,0:T(8,128)S(1)} collective-permute-done((f32[24,256]{1,0:T(8,128)}, f32[24,256]{1,0:T(8,128)S(1)}, u32[]{:S(2)}, u32[]{:S(2)}) %collective-permute-start.1) | collective-permute-done | bytes 24608 | tf_op jit(solution)/shard_map/ppermute | solution.py:642
  25.2 0.0 copy-start.3
  25.2 3.5 %all-to-all-done.received = f32[128,8,128]{2,1,0:T(8,128)S(1)} async-done(((f32[128,8,128]{2,1,0:T(8,128)}), f32[128,8,128]{2,1,0:T(8,128)S(1)}, u32[]{:S(2)}, u32[]{:S(2)}) %all-to-all-start) | async-done | bytes 524320 | tf_op jit(solution)/shard_map/all_to_all | solution.py:637
  28.7 0.0 copy-done.1
  28.7 3.9 %legendre.1 = f32[128,8,128]{2,1,0:T(8,128)} custom-call(f32[128,8,128]{2,1,0:T(8,128)S(1)} %all-to-all-done.received, f32[22,16,256]{2,1,0:T(8,128)S(1)} %get-tuple-element.21.gains, f32[8,1024]{1,0:T(8,128)S(1)} %get-tuple-element.22.balance, f32[8,256]{1,0:T(8,128)S(1)} %get-tuple-element.23.start, f32[3,8,256]{2,1,0:T(8,128)S(1)} %copy-done.1), custom_call_target="tpu_custom_call" | custom-call | flops 1610612736 | bytes 9437184 | tf_op jit(solution)/shard_map/legendre/pallas_call | solution.py:587
  32.6 4.9 %all-to-all-start.1 = ((f32[128,8,128]{2,1,0:T(8,128)}), f32[128,8,128]{2,1,0:T(8,128)S(1)}, u32[]{:S(2)}, u32[]{:S(2)}) async-start(f32[128,8,128]{2,1,0:T(8,128)} %legendre.1), calls=%async_computation.1 | async-start | bytes 1048576 | tf_op jit(solution)/shard_map/all_to_all | solution.py:680
  37.5 0.0 copy-done.2
  37.5 0.0 copy-done.3
  37.5 2.1 %columns.1 = (f32[24,128]{1,0:T(8,128)}, f32[24,128]{1,0:T(8,128)}, f32[6,72,256]{2,1,0:T(8,128)}) custom-call(f32[64,256]{1,0:T(8,128)} %height_in.3, f32[64,256]{1,0:T(8,128)} %flux_u_in.3, f32[64,256]{1,0:T(8,128)} %flux_v_in.3, f32[64,256]{1,0:T(8,128)} %depth_in.3, s32[64,256]{1,0:T(8,128)} %mask_in.3, f32[64,256]{1,0:T(8,128)} %flux_in.3, ...), custom_call_target="tpu_custom_call" | custom-call | tf_op jit(solution)/shard_map/columns/pallas_call | solution.py:587
  39.6 1.5 %collective-permute-start.2 = (f32[24,128]{1,0:T(8,128)}, f32[24,128]{1,0:T(8,128)S(1)}, u32[]{:S(2)}, u32[]{:S(2)}) collective-permute-start(f32[24,128]{1,0:T(8,128)} %get-tuple-element.27), channel_id=1, source_target_pairs={{0,1},{1,2},{2,3},{3,4},{4,5},{5,6},{6,7},{7,8},{8,9},{9,10},{10,1... | collective-permute-start | bytes 36872 | tf_op jit(solution)/shard_map/ppermute | solution.py:697
  41.1 3.5 %collective-permute-start.3 = (f32[24,128]{1,0:T(8,128)}, f32[24,128]{1,0:T(8,128)S(1)}, u32[]{:S(2)}, u32[]{:S(2)}) collective-permute-start(f32[24,128]{1,0:T(8,128)} %get-tuple-element.28), channel_id=1, source_target_pairs={{1,0},{2,1},{3,2},{4,3},{5,4},{6,5},{7,6},{8,7},{9,8},{10,9},{11,1... | collective-permute-start | bytes 36872 | tf_op jit(solution)/shard_map/ppermute | solution.py:698
  44.6 3.5 %collective-permute-done.2.west_in = f32[24,128]{1,0:T(8,128)S(1)} collective-permute-done((f32[24,128]{1,0:T(8,128)}, f32[24,128]{1,0:T(8,128)S(1)}, u32[]{:S(2)}, u32[]{:S(2)}) %collective-permute-start.2) | collective-permute-done | bytes 12320 | tf_op jit(solution)/shard_map/ppermute | solution.py:697
  48.2 0.0 collective-permute-done.3.east_in
  48.2 2.7 %all-to-all-done.1.received = f32[128,8,128]{2,1,0:T(8,128)S(1)} async-done(((f32[128,8,128]{2,1,0:T(8,128)}), f32[128,8,128]{2,1,0:T(8,128)S(1)}, u32[]{:S(2)}, u32[]{:S(2)}) %all-to-all-start.1) | async-done | bytes 524320 | tf_op jit(solution)/shard_map/all_to_all | solution.py:680
  50.9 0.0 copy-done
  50.9 3.0 %finish.1 = (f32[64,256]{1,0:T(8,128)}, f32[64,256]{1,0:T(8,128)}, f32[64,256]{1,0:T(8,128)}, f32[64,256]{1,0:T(8,128)}) custom-call(f32[128,8,128]{2,1,0:T(8,128)S(1)} %all-to-all-done.1.received, f32[32,128]{1,0:T(8,128)S(1)} %get-tuple-element.24.phase, f32[24,128]{1,0:T(8,128)S(1)} %collective-permute-done.2.west_in, ...), custom_call_target="tpu_custom_call" | custom-call | tf_op jit(solution)/shard_map/finish/pallas_call | solution.py:587
Async XLA Ops:
  0.6 28.1 %copy-start.1 = (f32[3,8,256]{2,1,0:T(8,128)S(1)}, f32[3,8,256]{2,1,0:T(8,128)}, u32[]{:S(2)}) copy-start(f32[3,8,256]{2,1,0:T(8,128)} %constant.16.clone.north_in.north) | copy-start | bytes 73732
  3.9 24.8 %all-to-all-start = ((f32[128,8,128]{2,1,0:T(8,128)}), f32[128,8,128]{2,1,0:T(8,128)S(1)}, u32[]{:S(2)}, u32[]{:S(2)}) async-start(f32[128,8,128]{2,1,0:T(8,128)} %get-tuple-element.17), calls=%async_computation | async-start | bytes 1048576 | tf_op jit(solution)/shard_map/all_to_all | solution.py:637
  15.4 6.7 %collective-permute-start = (f32[24,256]{1,0:T(8,128)}, f32[24,256]{1,0:T(8,128)S(1)}, u32[]{:S(2)}, u32[]{:S(2)}) collective-permute-start(f32[24,256]{1,0:T(8,128)} %get-tuple-element.18), channel_id=1, source_target_pairs={{0,16},{16,32},{32,48},{48,64},{64,80},{80,96},{96,112},{1,17},{17... | collective-permute-start | bytes 73736 | tf_op jit(solution)/shard_map/ppermute | solution.py:641
  19.1 6.1 %collective-permute-start.1 = (f32[24,256]{1,0:T(8,128)}, f32[24,256]{1,0:T(8,128)S(1)}, u32[]{:S(2)}, u32[]{:S(2)}) collective-permute-start(f32[24,256]{1,0:T(8,128)} %get-tuple-element.19), channel_id=1, source_target_pairs={{16,0},{32,16},{48,32},{64,48},{80,64},{96,80},{112,96},{17,1},{33... | collective-permute-start | bytes 73736 | tf_op jit(solution)/shard_map/ppermute | solution.py:642
  22.1 28.8 %copy-start = (bf16[4,1024,256]{2,1,0:T(8,128)(2,1)S(1)}, bf16[4,1024,256]{2,1,0:T(8,128)(2,1)}, u32[]{:S(2)}) copy-start(bf16[4,1024,256]{2,1,0:T(8,128)(2,1)} %constant.14.clone.wave_in.wave) | copy-start | bytes 6291460
  22.1 15.4 %copy-start.2 = (f32[24,256]{1,0:T(8,128)}, f32[24,256]{1,0:T(8,128)S(1)}, u32[]{:S(2)}) copy-start(f32[24,256]{1,0:T(8,128)S(1)} %collective-permute-done.south_in) | copy-start | bytes 73732
  25.2 12.3 %copy-start.3 = (f32[24,256]{1,0:T(8,128)}, f32[24,256]{1,0:T(8,128)S(1)}, u32[]{:S(2)}) copy-start(f32[24,256]{1,0:T(8,128)S(1)} %collective-permute-done.1.north_in) | copy-start | bytes 73732
  32.6 18.2 %all-to-all-start.1 = ((f32[128,8,128]{2,1,0:T(8,128)}), f32[128,8,128]{2,1,0:T(8,128)S(1)}, u32[]{:S(2)}, u32[]{:S(2)}) async-start(f32[128,8,128]{2,1,0:T(8,128)} %legendre.1), calls=%async_computation.1 | async-start | bytes 1048576 | tf_op jit(solution)/shard_map/all_to_all | solution.py:680
  39.6 8.5 %collective-permute-start.2 = (f32[24,128]{1,0:T(8,128)}, f32[24,128]{1,0:T(8,128)S(1)}, u32[]{:S(2)}, u32[]{:S(2)}) collective-permute-start(f32[24,128]{1,0:T(8,128)} %get-tuple-element.27), channel_id=1, source_target_pairs={{0,1},{1,2},{2,3},{3,4},{4,5},{5,6},{6,7},{7,8},{8,9},{9,10},{10,1... | collective-permute-start | bytes 36872 | tf_op jit(solution)/shard_map/ppermute | solution.py:697
  41.1 7.0 %collective-permute-start.3 = (f32[24,128]{1,0:T(8,128)}, f32[24,128]{1,0:T(8,128)S(1)}, u32[]{:S(2)}, u32[]{:S(2)}) collective-permute-start(f32[24,128]{1,0:T(8,128)} %get-tuple-element.28), channel_id=1, source_target_pairs={{1,0},{2,1},{3,2},{4,3},{5,4},{6,5},{7,6},{8,7},{9,8},{10,9},{11,1... | collective-permute-start | bytes 36872 | tf_op jit(solution)/shard_map/ppermute | solution.py:698

commit v4 on v3

--- a/solution.py
+++ b/solution.py
@@ -28,6 +28,8 @@
 CHUNK = 128
 CHUNKS = DEG // CHUNK
 TILE = 256
+QUARTERS = 4
+QUARTER = DEG // QUARTERS
 
 step_time = 0.5
 sal_ratio = 3.0 * 1035.0 / 5517.0
@@ -37,26 +39,16 @@
 bf16 = jnp.bfloat16
 
 
-def split_table(values):
-    high = values.astype(ml_dtypes.bfloat16)
-    low = (values - high.astype(np.float64)).astype(ml_dtypes.bfloat16)
-    return high, low
-
-
-def wave_tables():
-    order = (np.arange(DEVS)[:, None] + DEVS * np.arange(ORDERS)[None, :]).reshape(-1)
-    angle = (order[:, None] * np.arange(COLS)[None, :] % NLON) * (2.0 * math.pi / NLON)
-    cos_high, cos_low = split_table(np.cos(angle))
-    sin_high, sin_low = split_table(np.sin(angle))
-    return np.stack([cos_high, sin_high, cos_low, sin_low])
-
-
-def phase_tables():
-    angle = np.arange(LONS)[:, None] * np.arange(LONS)[None, :] % LONS * (2.0 * math.pi / LONS)
-    left = np.broadcast_to(np.array([np.cos(angle), -np.sin(angle)])[..., None], (2, LONS, LONS, 64))
-    right = np.broadcast_to(np.array([np.sin(angle), np.cos(angle)])[..., None], (2, LONS, LONS, 64))
-    both = np.concatenate([left, right], axis=-1).transpose(1, 0, 2, 3)
-    return both.reshape(LONS, 2 * LONS, 128).astype(np.float32)
+def turn_tables():
+    column = np.arange(NLON).reshape(LONS, 1, COLS)
+    angle = column * np.arange(DEVS)[None, :, None] % NLON * (2.0 * math.pi / NLON)
+    return np.stack([np.cos(angle), np.sin(angle)], axis=1).astype(np.float32)
+
+
+def step_tables():
+    angle = np.arange(ORDERS)[:, None] * DEVS * np.arange(COLS)[None, :] % NLON
+    angle = angle * (2.0 * math.pi / NLON)
+    return np.stack([np.cos(angle), np.sin(angle)]).astype(np.float32)
 
 
 def balance_table():
@@ -139,16 +131,17 @@
     depth_in,
     mask_in,
     flux_in,
-    wave_in,
-    phase_in,
+    turn_in,
+    step_in,
     area_in,
     message_out,
     north_out,
     south_out,
+    wave,
     tiles,
     mask,
-    wave,
-    phase,
+    turn,
+    step,
     area,
     message,
     strips,
@@ -157,13 +150,12 @@
     strip_sems,
 ):
     lat_index = lax.axis_index("lat")
-    lon_index = lax.axis_index("lon")
     loads = fetch(
         (
             (mask_in, mask),
             (height_in, tiles.at[0]),
-            (wave_in, wave),
-            (phase_in.at[lon_index], phase),
+            (turn_in.at[lax.axis_index("lon")], turn),
+            (step_in, step),
             (flux_in, tiles.at[4]),
             (area_in.at[lat_index], area),
             (flux_u_in, tiles.at[1]),
@@ -172,18 +164,17 @@
         ),
         sems,
     )
-    loads[0].wait()
-    loads[1].wait()
+    for load in loads[:6]:
+        load.wait()
     sea = mask[...].astype(f32)
     mass_high, mass_low = halves(sea * tiles[0])
     both = jnp.concatenate([mass_high, mass_low], axis=1)
     both = dot_nn(row_order(lat_index).astype(bf16), both).astype(bf16)
     mass_high, mass_low = both[:, :COLS], both[:, COLS:]
-    twice = jnp.concatenate([mass_high, mass_high], axis=0)
-    all_parts = jnp.concatenate([twice, mass_low, mass_low], axis=0)
-
-    for load in loads[3:6]:
-        load.wait()
+    zero = jnp.zeros_like(mass_high)
+    for_cos = jnp.concatenate([mass_high, zero, mass_low, zero], axis=0)
+    for_sin = jnp.concatenate([zero, mass_high, zero, mass_low], axis=0)
+
     band = area[...]
     area_cells = sea * jnp.concatenate([band, band], axis=1)
     flux_sum = jnp.sum(area_cells * tiles[4])
@@ -191,31 +182,34 @@
     row = iota((8, 128), 0)
     lane = iota((8, 128), 1)
 
-    loads[2].wait()
+    step_cos, step_sin = step[0], step[1]
+    share = DEVS // QUARTERS
     sends = []
-    share = DEVS // 4
-    for quarter in range(4):
-        place = slice(quarter * share * ORDERS, (quarter + 1) * share * ORDERS)
-        cos_parts = dot_nt(wave[0, place], all_parts)
-        sin_parts = dot_nt(wave[1, place], all_parts)
-        cos_sums = cos_parts[:, :128] + cos_parts[:, 128:] + dot_nt(wave[2, place], twice)
-        sin_sums = sin_parts[:, :128] + sin_parts[:, 128:] + dot_nt(wave[3, place], twice)
+    for quarter in range(QUARTERS):
+        for pair in range(share // 2):
+            cos_rows = []
+            sin_rows = []
+            for device in (quarter * share + 2 * pair, quarter * share + 2 * pair + 1):
+                turn_cos, turn_sin = turn[0, device : device + 1, :], turn[1, device : device + 1, :]
+                cos_rows.append(turn_cos * step_cos - turn_sin * step_sin)
+                sin_rows.append(turn_sin * step_cos + turn_cos * step_sin)
+            rows = slice(2 * ORDERS * pair, 2 * ORDERS * (pair + 1))
+            for slot, parts in enumerate((cos_rows, sin_rows)):
+                high, low = halves(jnp.concatenate(parts, axis=0))
+                wave[quarter, slot, rows, :] = high
+                wave[quarter, 2 + slot, rows, :] = low
+        sums = dot_nt(wave[quarter, 0], for_cos) + dot_nt(wave[quarter, 1], for_sin)
+        sums = sums[:, :128] + sums[:, 128:]
+        sums = sums + dot_nt(wave[quarter, 2], for_cos[:128]) + dot_nt(wave[quarter, 3], for_sin[:128])
         for spot in range(share):
-            device = quarter * share + spot
-            turn = device % LONS
-            rows = slice(spot * ORDERS, (spot + 1) * ORDERS)
-            sent = (
-                phase[turn : turn + 1, :] * cos_sums[rows]
-                + phase[LONS + turn : LONS + turn + 1, :] * sin_sums[rows]
-            )
-            if device == 0:
+            sent = sums[spot * ORDERS : (spot + 1) * ORDERS]
+            if quarter == 0 and spot == 0:
                 sent = jnp.where((row == 0) & (lane >= 64), area_sum, sent)
                 sent = jnp.where((row == 0) & (lane == 64), flux_sum, sent)
-            message[device] = sent
+            message[quarter * share + spot] = sent
         place = pl.ds(quarter * share, share)
         pair = (message.at[place], message_out.at[place])
         sends += fetch((pair,), send_sems.at[pl.ds(quarter, 1)])
-
     for load in loads[6:]:
         load.wait()
     for slot, values in enumerate((tiles[0], tiles[1], tiles[2], tiles[3], sea, tiles[4])):
@@ -226,16 +220,15 @@
         copy.wait()
 
 
-def tiles_of():
+def pairs_of():
     found = []
-    for chunk in range(CHUNKS):
-        kept = 8 if chunk < 4 else 4 if chunk < 6 else 2
-        steps = TILE // kept
-        found += [(chunk, first, steps, kept) for first in range(0, CHUNK, steps)]
+    for first, last, kept in ((0, 512, 8), (512, 768, 4), (768, 1024, 2)):
+        steps = 2 * TILE // kept
+        found += [(start, steps, kept) for start in range(first, last, steps)]
     return found
 
 
-TILES = tiles_of()
+PAIRS = pairs_of()
 
 
 def make_gains(love, balance, device, gains):
@@ -246,25 +239,17 @@
     above = jnp.concatenate([turned[1:], jnp.zeros((1, 128), f32)], axis=0)
     shifted = jnp.where(lane + device < 128, turned, above)
     padded = jnp.concatenate([shifted, jnp.zeros((8, 128), f32)], axis=0)
-    column = iota((ORDERS, TILE), 1)
-    for kept in sorted({kept for _, _, _, kept in TILES}):
-        slots = [slot for slot in range(len(TILES)) if TILES[slot][3] == kept]
-        chunks = sorted({TILES[slot][0] for slot in slots})
+    for pair, (first, steps, kept) in enumerate(PAIRS):
+        chunks = range(first // CHUNK, -(-(first + steps) // CHUNK))
+        width = CHUNK * len(chunks)
         blocks = [padded[c : c + 8] * balance[:, c * CHUNK : (c + 1) * CHUNK] for c in chunks]
-        parts = jnp.concatenate(halves(jnp.concatenate(blocks, axis=0)), axis=0)
-        half = len(chunks) * ORDERS
-        same = column % kept == iota((ORDERS, TILE), 0)
-        even_step = (column // kept) % 2 == 0
-        for begin in sorted({TILES[slot][1] for slot in slots}):
-            spread = iota((CHUNK, TILE), 1) // kept + begin == iota((CHUNK, TILE), 0)
-            wide = dot_nn(parts, spread.astype(f32).astype(bf16))
-            wide = wide[:half] + wide[half:]
-            for spot, chunk in enumerate(chunks):
-                slot = [slot for slot in slots if TILES[slot][:2] == (chunk, begin)][0]
-                here = jnp.where(same, wide[spot * ORDERS : (spot + 1) * ORDERS], 0.0)
-                even = jnp.where(even_step, here, 0.0)
-                gains[slot, 0:8, :] = even
-                gains[slot, 8:16, :] = here - even
+        parts = jnp.concatenate(halves(jnp.concatenate(blocks, axis=1)), axis=0)
+        same = iota((ORDERS, TILE), 1) % kept == iota((ORDERS, TILE), 0)
+        for parity in range(2):
+            step = first % CHUNK + 2 * (iota((width, TILE), 1) // kept) + parity
+            spread = (step == iota((width, TILE), 0)).astype(f32).astype(bf16)
+            wide = dot_nn(parts, spread)
+            gains[2 * pair + parity] = jnp.where(same, wide[:ORDERS] + wide[ORDERS:], 0.0)
 
 
 def setup_kernel(
@@ -272,11 +257,9 @@
     balance_in,
     seeds_in,
     north_in,
-    phase_in,
     gains,
     balance,
     start,
-    phase,
     love,
     seeds,
     north,
@@ -289,7 +272,6 @@
             (north_in, north),
             (balance_in.at[device], balance),
             (love_in, love),
-            (phase_in.at[lax.axis_index("lon")], phase),
         ),
         sems,
     )
@@ -334,69 +316,76 @@
             jnp.concatenate(sin_parts, axis=1) * weight,
         ]
 
-    rows_high, rows_low = halves(jnp.concatenate(arrange(even) + arrange(odd), axis=0))
-    rows_both = jnp.concatenate([rows_high, rows_low], axis=0)
+    lefts = []
+    for parts in (even, odd):
+        rows_high, rows_low = halves(jnp.concatenate(arrange(parts), axis=0))
+        lefts.append(jnp.concatenate([rows_high, rows_low], axis=0))
 
     sine = north[0]
     state = [jnp.zeros((ORDERS, HALF), f32), start[...]]
     wide_row = iota((ORDERS, HALF), 0)
 
-    def extend(slot):
-        chunk, first, steps, kept = TILES[slot]
+    def extend(pair):
+        first, steps, kept = PAIRS[pair]
         share = ORDERS // kept
-        packed = []
-        for step in range(first, first + steps, share):
-            block = None
-            for part in range(share):
-                previous, current = state
-                spot = chunk * CHUNK + step + part
-                if part == 0:
-                    block = current
-                else:
-                    moved = pltpu.roll(current, part * kept, 0)
-                    block = jnp.where(wide_row < part * kept, block, moved)
-                turn = balance[:, spot : spot + 1] * sine
-                state[0], state[1] = current, turn * current - previous
-            packed.append(block)
-            if len(packed) == 2:
-                place = slice(slot * TILE + (step - first) // share * 8 - 8, None)
-                place = slice(place.start, place.start + 16)
-                high[place, :], low[place, :] = halves(jnp.concatenate(packed, axis=0))
-                packed = []
-
-    def analyse(slot):
-        place = slice(slot * TILE, (slot + 1) * TILE)
-        both = dot_nt(rows_both, high[place, :])
-        coefs = both[:32] + both[32:] + dot_nt(rows_high, low[place, :])
-        even, odd = gains[slot, 0:8, :], gains[slot, 8:16, :]
-        coefs_high, coefs_low = halves(coefs * jnp.concatenate([even, even, odd, odd], axis=0))
-        return jnp.concatenate([coefs_high, coefs_low], axis=0)
-
-    def synthesise(slot, coefs):
-        place = slice(slot * TILE, (slot + 1) * TILE)
-        return dot_nn(coefs, high[place, :]), dot_nn(coefs[:32], low[place, :])
-
-    count = len(TILES)
-    total_high = jnp.zeros((64, HALF), f32)
-    total_low = jnp.zeros((32, HALF), f32)
+        block, packed, place = [None, None], [[], []], [2 * pair * TILE, (2 * pair + 1) * TILE]
+        for step in range(steps):
+            parity, part = step % 2, step // 2 % share
+            previous, current = state
+            if part == 0:
+                block[parity] = current
+            else:
+                moved = pltpu.roll(current, part * kept, 0)
+                block[parity] = jnp.where(wide_row < part * kept, block[parity], moved)
+            turn = balance[:, first + step : first + step + 1] * sine
+            state[0], state[1] = current, turn * current - previous
+            if part == share - 1:
+                packed[parity].append(block[parity])
+            if len(packed[parity]) == 2:
+                rows = slice(place[parity], place[parity] + 16)
+                high[rows, :], low[rows, :] = halves(jnp.concatenate(packed[parity], axis=0))
+                packed[parity] = []
+                place[parity] += 16
+
+    def analyse(tile):
+        place = slice(tile * TILE, (tile + 1) * TILE)
+        left_rows = lefts[tile % 2]
+        both = dot_nt(left_rows, high[place, :])
+        found = both[:16] + both[16:] + dot_nt(left_rows[:16], low[place, :])
+        gain = gains[tile]
+        return jnp.concatenate(halves(found * jnp.concatenate([gain, gain], axis=0)), axis=0)
+
+    def synthesise(tile, coefs):
+        place = slice(tile * TILE, (tile + 1) * TILE)
+        return dot_nn(coefs, high[place, :]), dot_nn(coefs[:16], low[place, :])
+
+    count = len(PAIRS)
+    total_high = [jnp.zeros((32, HALF), f32)] * 2
+    total_low = [jnp.zeros((16, HALF), f32)] * 2
     coefs = {}
     for turn in range(count + 2):
         if turn < count:
             extend(turn)
-        if 1 <= turn <= count:
-            coefs[turn - 1] = analyse(turn - 1)
-        if turn >= 2:
-            more_high, more_low = synthesise(turn - 2, coefs.pop(turn - 2))
-            total_high = total_high + more_high
-            total_low = total_low + more_low
-    total = total_high[:32] + total_high[32:] + total_low
+        for parity in range(2):
+            if 1 <= turn <= count:
+                tile = 2 * (turn - 1) + parity
+                coefs[tile] = analyse(tile)
+        for parity in range(2):
+            if turn >= 2:
+                tile = 2 * (turn - 2) + parity
+                more_high, more_low = synthesise(tile, coefs.pop(tile))
+                total_high[parity] = total_high[parity] + more_high
+                total_low[parity] = total_low[parity] + more_low
+    total_even, total_odd = [
+        total_high[parity][:16] + total_high[parity][16:] + total_low[parity] for parity in range(2)
+    ]
 
     flux_sum = jnp.sum(jnp.where((row == 0) & (lane == 64), sums, 0.0))
     area_sum = jnp.sum(jnp.where((row == 0) & (lane == 65), sums, 0.0))
     mean = jnp.full((8, 128), flux_sum, f32) / jnp.full((8, 128), area_sum, f32)
     slot = (device == 0) & (row == 0) & (lane >= 64)
-    cos_even, sin_even = total[0:8, :], total[8:16, :]
-    cos_odd, sin_odd = total[16:24, :], total[24:32, :]
+    cos_even, sin_even = total_even[0:8, :], total_even[8:16, :]
+    cos_odd, sin_odd = total_odd[0:8, :], total_odd[8:16, :]
     copies = []
     for north_side in (True, False):
         if north_side:
@@ -422,44 +411,23 @@
 
 def finish_kernel(
     received,
-    phase,
     west_in,
     east_in,
     wave,
-    blocks_in,
-    bands_in,
+    tiles,
+    bands,
     height_out,
     u_out,
     v_out,
     sal_out,
     blocks,
-    bands,
-    turned_scratch,
     results,
-    sems,
     out_sems,
 ):
     lat_index = lax.axis_index("lat")
-    loads = fetch(
-        (
-            (blocks_in, blocks.at[:, :, pl.ds(0, COLS)]),
-            (bands_in.at[lat_index], bands),
-        ),
-        sems,
-    )
     lane = iota((8, 128), 1)
-    left = lane < 64
-    for device in range(DEVS):
-        turn = device % LONS
-        part = received[device]
-        first, second = phase[turn : turn + 1, :], phase[LONS + turn : LONS + turn + 1, :]
-        cos_turn = jnp.where(left[:1], first, second)
-        sin_turn = -jnp.where(left[:1], second, first)
-        turned_scratch[device * ORDERS : (device + 1) * ORDERS, :] = (
-            cos_turn * part + sin_turn * pltpu.roll(part, 64, 1)
-        )
     mean = jnp.sum(jnp.where((iota((8, 128), 0) == 0) & (lane == 64), received[0], 0.0))
-    turned = turned_scratch[...].T
+    turned = received[...].reshape(DEG, 128).T
     high, low = halves(turned)
     cos_both = jnp.concatenate([high[:64], low[:64]], axis=0)
     sin_both = jnp.concatenate([high[64:], low[64:]], axis=0)
@@ -471,14 +439,17 @@
     for slot in range(FIELDS):
         high_side = pltpu.roll(east, 128 - slot * WIDE, 1) if slot else east
         low_side = pltpu.roll(west, 128 - WIDE - slot * WIDE, 1)
+        blocks[slot, :, :COLS] = tiles[slot]
         blocks[slot, :, COLS:] = jnp.where(
             wide_lane < WIDE, high_side, jnp.where(wide_lane >= 128 - WIDE, low_side, 0.0)
         )
-    for load in loads:
-        load.wait()
-
-    both = dot_nn(cos_both, wave[0]) + dot_nn(sin_both, wave[1])
-    field = both[:64] + both[64:] + dot_nn(high[:64], wave[2]) + dot_nn(high[64:], wave[3])
+    both = jnp.zeros((2 * ROWS, COLS), f32)
+    field = jnp.zeros((ROWS, COLS), f32)
+    for part in range(QUARTERS):
+        place = slice(part * QUARTER, (part + 1) * QUARTER)
+        both += dot_nn(cos_both[:, place], wave[part, 0]) + dot_nn(sin_both[:, place], wave[part, 1])
+        field += dot_nn(high[:64, place], wave[part, 2]) + dot_nn(high[64:, place], wave[part, 3])
+    field = field + both[:64] + both[64:]
     field_high, field_low = halves(field)
     order = row_order(lat_index).astype(bf16)
     field = dot_nn(order, field_high) + dot_nn(order, field_low)
@@ -521,13 +492,14 @@
     flux_in,
     south_in,
     north_in,
+    bands_in,
     west_out,
     east_out,
-    blocks_out,
+    blocks,
+    bands,
     mask,
     strips,
     sides,
-    blocks,
     sems,
     out_sems,
 ):
@@ -542,6 +514,7 @@
             (depth_in, blocks.at[3, own]),
             (mask_in, mask),
             (flux_in, blocks.at[5, own]),
+            (bands_in.at[lax.axis_index("lat")], bands),
         ),
         sems,
     )
@@ -564,15 +537,15 @@
     fill = jnp.zeros((128 - PAD_ROWS, 128), f32)
     sides[0] = jnp.concatenate([west, fill], axis=0).T[:STRIP, :]
     sides[1] = jnp.concatenate([east, fill], axis=0).T[:STRIP, :]
-    pairs = ((sides.at[0], west_out), (sides.at[1], east_out), (blocks, blocks_out))
+    pairs = ((sides.at[0], west_out), (sides.at[1], east_out))
     for copy in fetch(pairs, out_sems):
         copy.wait()
 
 
-def far_call(kernel, name, operands, results, scratch, work=None, here=(), near=(), near_out=False):
+def far_call(kernel, name, operands, results, scratch, work=None, here=(), near=(), near_out=()):
     placed = []
     specs = []
-    out_space = pltpu.VMEM if near_out else pltpu.HBM
+    out_spaces = [pltpu.VMEM if slot in near_out else pltpu.HBM for slot in range(len(results))]
     for slot, operand in enumerate(operands):
         if slot in here:
             space = pltpu.VMEM
@@ -586,9 +559,9 @@
         specs.append(pl.BlockSpec(memory_space=space))
     return pl.pallas_call(
         kernel,
-        out_shape=tuple(out_space(shape, kind) for shape, kind in results),
+        out_shape=tuple(space(*result) for space, result in zip(out_spaces, results)),
         in_specs=specs,
-        out_specs=(pl.BlockSpec(memory_space=out_space),) * len(results),
+        out_specs=tuple(pl.BlockSpec(memory_space=space) for space in out_spaces),
         scratch_shapes=scratch,
         compiler_params=pltpu.CompilerParams(vmem_limit_bytes=32 << 20),
         cost_estimate=work,
@@ -602,8 +575,6 @@
 
 def on_device(sea_height, trans_u, trans_v, depth, sea_mask, freshwater_flux, love_factor):
     both_axes = ("lat", "lon")
-    wave = jnp.asarray(wave_tables())
-    phase = jnp.asarray(phase_tables())
     north = jnp.asarray(north_tables())
     fields = (sea_height, trans_u, trans_v, depth, sea_mask, freshwater_flux)
     vmem = pltpu.VMEM
@@ -615,24 +586,25 @@
     tiles = vmem((FIELDS, ROWS, COLS), f32)
     mask_tile = vmem((ROWS, COLS), jnp.int32)
 
-    message, strip_north, strip_south = far_call(
+    message, strip_north, strip_south, wave = far_call(
         forward_kernel,
         "forward",
-        fields + (wave, phase, jnp.asarray(area_table())),
-        (messages, strip, strip),
+        fields + (jnp.asarray(turn_tables()), jnp.asarray(step_tables()), jnp.asarray(area_table())),
+        (messages, strip, strip, ((QUARTERS, 4, QUARTER, COLS), bf16)),
         [
             tiles,
             mask_tile,
-            vmem((4, DEG, COLS), bf16),
-            vmem((2 * LONS, 128), f32),
+            vmem((2, DEVS, COLS), f32),
+            vmem((2, ORDERS, COLS), f32),
             vmem((ROWS, 128), f32),
             vmem(*messages),
             vmem((2, STRIP, COLS), f32),
             copies((9,)),
-            copies((4,)),
+            copies((QUARTERS,)),
             copies((2,)),
         ],
         work=cost(6 * 2 * 1024 * 256 * 256, 3 << 20),
+        near_out=(3,),
     )
     received = lax.all_to_all(message, both_axes, split_axis=0, concat_axis=0, tiled=True)
 
@@ -641,11 +613,10 @@
     from_south = lax.ppermute(strip_north, "lat", upward)
     from_north = lax.ppermute(strip_south, "lat", downward)
 
-    gain_tiles = ((len(TILES), 16, TILE), f32)
+    gain_tiles = ((2 * len(PAIRS), ORDERS, TILE), f32)
     squares = ((ORDERS, DEG), f32)
     first_rows = ((ORDERS, HALF), f32)
-    turns = ((2 * LONS, 128), f32)
-    gains, balance, start, phase_here = far_call(
+    gains, balance, start = far_call(
         setup_kernel,
         "setup",
         (
@@ -653,20 +624,19 @@
             jnp.asarray(balance_table()),
             jnp.asarray(seed_table()),
             north,
-            phase,
         ),
-        (gain_tiles, squares, first_rows, turns),
+        (gain_tiles, squares, first_rows),
         [
             vmem((8, 128), f32),
             vmem((ORDERS, DEVS), f32),
             vmem((3, 8, HALF), f32),
-            copies((5,)),
+            copies((4,)),
         ],
         work=cost(2 << 20, 1 << 20),
-        near_out=True,
+        near_out=(0, 1, 2),
     )
     received, from_south, from_north = lax.optimization_barrier((received, from_south, from_north))
-    table = ((len(TILES) * TILE, HALF), bf16)
+    table = ((2 * len(PAIRS) * TILE, HALF), bf16)
     (reply,) = far_call(
         legendre_kernel,
         "legendre",
@@ -680,19 +650,19 @@
     answer = lax.all_to_all(reply, both_axes, split_axis=0, concat_axis=0, tiled=True)
 
     padded = ((FIELDS, PAD_ROWS, COLS), f32)
-    to_west, to_east, blocks = far_call(
+    to_west, to_east, blocks, bands = far_call(
         column_kernel,
         "columns",
-        fields + (from_south, from_north),
-        (side, side, padded),
+        fields + (from_south, from_north, jnp.asarray(row_tables())),
+        (side, side, padded, ((2, PAD_ROWS, 128), f32)),
         [
             mask_tile,
             vmem((2, STRIP, COLS), f32),
             vmem((2, STRIP, 128), f32),
-            vmem(*padded),
-            copies((8,)),
-            copies((3,)),
+            copies((9,)),
+            copies((2,)),
         ],
+        near_out=(2, 3),
     )
     from_west = lax.ppermute(to_east, "lon", [(i, (i + 1) % LONS) for i in range(LONS)])
     from_east = lax.ppermute(to_west, "lon", [((i + 1) % LONS, i) for i in range(LONS)])
@@ -700,18 +670,15 @@
     return far_call(
         finish_kernel,
         "finish",
-        (answer, phase_here, from_west, from_east, wave, blocks, jnp.asarray(row_tables())),
+        (answer, from_west, from_east, wave, blocks, bands),
         (tile,) * 4,
         [
             vmem((FIELDS, PAD_ROWS, PAD_COLS), f32),
-            vmem((2, PAD_ROWS, 128), f32),
-            vmem((DEG, 128), f32),
             vmem((4, ROWS, COLS), f32),
-            copies((2,)),
             copies((4,)),
         ],
-        here=(0, 2, 3, 4),
-        near=(1,),
+        here=(0, 1, 2),
+        near=(3, 4, 5),
     )
 
 

time: 54.3 us -> 52.4 us (0.965)
  Pallas kernels: 13.4 us -> 11.6 us
    pallas_call x5, Pallas kernels: 13.4 us -> 11.6 us  [far_call(): pl.pallas_call(kernel, out_shape=tuple((space(*result) for space, result...]
where the time goes in v4:
time: 52.4 us; the launch traced here: 52 us
  starting transfers between devices  26.9 us (51%)
  waiting for transfers between devices  12.7 us (24%)
  Pallas kernels  11.6 us (22%)
  between operations  0.74 us (1%)
    pallas_call x5, Pallas kernels, far_call(): pl.pallas_call(kernel, out_shape=tuple((space(*result) for space, result...  11.6 us
    all_to_all x1, starting transfers between devices, on_device(): lax.all_to_all(message, both_axes, split_axis=0, concat_axis=0, tiled=True)  11.5 us
    all_to_all x1, starting transfers between devices, on_device(): lax.all_to_all(reply, both_axes, split_axis=0, concat_axis=0, tiled=True)  4.87 us
    ppermute x1, starting transfers between devices, on_device(): from_south = lax.ppermute(strip_north, 'lat', upward)  3.66 us
    ppermute x1, waiting for transfers between devices, on_device(): lax.ppermute(to_east, 'lon', [(i, (i + 1) % LONS) for i in range(LONS)])  3.58 us
    all_to_all x1, waiting for transfers between devices, on_device(): lax.all_to_all(message, both_axes, split_axis=0, concat_axis=0, tiled=True)  3.55 us
    ppermute x1, starting transfers between devices, on_device(): lax.ppermute(to_west, 'lon', [((i + 1) % LONS, i) for i in range(LONS)])  3.53 us
    ppermute x1, waiting for transfers between devices, on_device(): from_north = lax.ppermute(strip_south, 'lat', downward)  2.89 us
  transfers between devices with their start and end apart: 6, of which 4 were waited for; matrix products, arithmetic and copies ran while one was open for 0% of the time, Pallas kernels for 6%

profile of v4, /device:TPU:1, one launch (start us, length us, event | category | flops | bytes accessed | tf_op | source)
XLA Modules:
  0.0 52.0 jit_solution(1820269413505439306)
XLA Ops:
  0.6 0.0 copy-start
  0.6 2.7 %forward.1 = (f32[128,8,128]{2,1,0:T(8,128)}, f32[24,256]{1,0:T(8,128)}, f32[24,256]{1,0:T(8,128)}, bf16[4,4,256,256]{3,2,1,0:T(8,128)(2,1)S(1)}) custom-call(f32[64,256]{1,0:T(8,128)} %height_in.3, f32[64,256]{1,0:T(8,128)} %flux_u_in.3, f32[64,256]{1,0:T(8,128)} %flux_v_in.3, f32[64,256]{1,0:T(8,128)} %depth_in.3, s32[64,256]{1,0:T(8,128)} %mask_in.3, ...), custom_call_target="tpu_custom_call" | custom-call | flops 805306368 | bytes 3145728 | tf_op jit(solution)/shard_map/forward/pallas_call | solution.py:560
  3.4 11.5 %all-to-all-start = ((f32[128,8,128]{2,1,0:T(8,128)}), f32[128,8,128]{2,1,0:T(8,128)S(1)}, u32[]{:S(2)}, u32[]{:S(2)}) async-start(f32[128,8,128]{2,1,0:T(8,128)} %get-tuple-element.18), calls=%async_computation | async-start | bytes 1048576 | tf_op jit(solution)/shard_map/all_to_all | solution.py:609
  14.9 3.7 %collective-permute-start = (f32[24,256]{1,0:T(8,128)}, f32[24,256]{1,0:T(8,128)S(1)}, u32[]{:S(2)}, u32[]{:S(2)}) collective-permute-start(f32[24,256]{1,0:T(8,128)} %get-tuple-element.19), channel_id=1, source_target_pairs={{0,16},{16,32},{32,48},{48,64},{64,80},{80,96},{96,112},{1,17},{17... | collective-permute-start | bytes 73736 | tf_op jit(solution)/shard_map/ppermute | solution.py:613
  18.6 1.9 %collective-permute-start.1 = (f32[24,256]{1,0:T(8,128)}, f32[24,256]{1,0:T(8,128)S(1)}, u32[]{:S(2)}, u32[]{:S(2)}) collective-permute-start(f32[24,256]{1,0:T(8,128)} %get-tuple-element.20), channel_id=1, source_target_pairs={{16,0},{32,16},{48,32},{64,48},{80,64},{96,80},{112,96},{17,1},{33... | collective-permute-start | bytes 73736 | tf_op jit(solution)/shard_map/ppermute | solution.py:614
  20.5 1.3 %setup.1 = (f32[22,8,256]{2,1,0:T(8,128)S(1)}, f32[8,1024]{1,0:T(8,128)S(1)}, f32[8,256]{1,0:T(8,128)S(1)}) custom-call(f32[8,128]{1,0:T(8,128)} %bitcast.1, f32[128,8,1024]{2,1,0:T(8,128)} %constant.18.clone.balance_in, f32[8,128]{1,0:T(8,128)} %constant.19.clone.seeds_in, f32[3,8,256]{2,1,0:T(8,128)} %constant.14.clone.north_in.north), custom_call_target="tpu_custom_call" | custom-call | flops 2097152 | bytes 1048576 | tf_op jit(solution)/shard_map/setup/pallas_call | solution.py:560
  21.8 0.0 collective-permute-done.south_in
  21.8 0.0 copy-start.1
  21.8 2.9 %collective-permute-done.1.north_in = f32[24,256]{1,0:T(8,128)S(1)} collective-permute-done((f32[24,256]{1,0:T(8,128)}, f32[24,256]{1,0:T(8,128)S(1)}, u32[]{:S(2)}, u32[]{:S(2)}) %collective-permute-start.1) | collective-permute-done | bytes 24608 | tf_op jit(solution)/shard_map/ppermute | solution.py:614
  24.7 0.0 copy-start.2
  24.7 3.5 %all-to-all-done.received = f32[128,8,128]{2,1,0:T(8,128)S(1)} async-done(((f32[128,8,128]{2,1,0:T(8,128)}), f32[128,8,128]{2,1,0:T(8,128)S(1)}, u32[]{:S(2)}, u32[]{:S(2)}) %all-to-all-start) | async-done | bytes 524320 | tf_op jit(solution)/shard_map/all_to_all | solution.py:609
  28.2 0.0 copy-done
  28.2 3.6 %legendre.1 = f32[128,8,128]{2,1,0:T(8,128)} custom-call(f32[128,8,128]{2,1,0:T(8,128)S(1)} %all-to-all-done.received, f32[22,8,256]{2,1,0:T(8,128)S(1)} %get-tuple-element.22.gains, f32[8,1024]{1,0:T(8,128)S(1)} %get-tuple-element.23.balance, f32[8,256]{1,0:T(8,128)S(1)} %get-tuple-element.24.start, f32[3,8,256]{2,1,0:T(8,128)S(1)} %copy-done), custom_call_target="tpu_custom_call" | custom-call | flops 1610612736 | bytes 9437184 | tf_op jit(solution)/shard_map/legendre/pallas_call | solution.py:560
  31.9 4.9 %all-to-all-start.1 = ((f32[128,8,128]{2,1,0:T(8,128)}), f32[128,8,128]{2,1,0:T(8,128)S(1)}, u32[]{:S(2)}, u32[]{:S(2)}) async-start(f32[128,8,128]{2,1,0:T(8,128)} %legendre.1), calls=%async_computation.1 | async-start | bytes 1048576 | tf_op jit(solution)/shard_map/all_to_all | solution.py:650
  36.8 0.0 copy-done.1
  36.8 0.0 copy-done.2
  36.8 2.0 %columns.1 = (f32[24,128]{1,0:T(8,128)}, f32[24,128]{1,0:T(8,128)}, f32[6,72,256]{2,1,0:T(8,128)S(1)}, f32[2,72,128]{2,1,0:T(8,128)S(1)}) custom-call(f32[64,256]{1,0:T(8,128)} %height_in.3, f32[64,256]{1,0:T(8,128)} %flux_u_in.3, f32[64,256]{1,0:T(8,128)} %flux_v_in.3, f32[64,256]{1,0:T(8,128)} %depth_in.3, s32[64,256]{1,0:T(8,128)} %mask_in.3, ...), custom_call_target="tpu_custom_call" | custom-call | tf_op jit(solution)/shard_map/columns/pallas_call | solution.py:560
  38.8 1.5 %collective-permute-start.2 = (f32[24,128]{1,0:T(8,128)}, f32[24,128]{1,0:T(8,128)S(1)}, u32[]{:S(2)}, u32[]{:S(2)}) collective-permute-start(f32[24,128]{1,0:T(8,128)} %get-tuple-element.27), channel_id=1, source_target_pairs={{0,1},{1,2},{2,3},{3,4},{4,5},{5,6},{6,7},{7,8},{8,9},{9,10},{10,1... | collective-permute-start | bytes 36872 | tf_op jit(solution)/shard_map/ppermute | solution.py:667
  40.3 3.5 %collective-permute-start.3 = (f32[24,128]{1,0:T(8,128)}, f32[24,128]{1,0:T(8,128)S(1)}, u32[]{:S(2)}, u32[]{:S(2)}) collective-permute-start(f32[24,128]{1,0:T(8,128)} %get-tuple-element.28), channel_id=1, source_target_pairs={{1,0},{2,1},{3,2},{4,3},{5,4},{6,5},{7,6},{8,7},{9,8},{10,9},{11,1... | collective-permute-start | bytes 36872 | tf_op jit(solution)/shard_map/ppermute | solution.py:668
  43.8 3.6 %collective-permute-done.2.west_in = f32[24,128]{1,0:T(8,128)S(1)} collective-permute-done((f32[24,128]{1,0:T(8,128)}, f32[24,128]{1,0:T(8,128)S(1)}, u32[]{:S(2)}, u32[]{:S(2)}) %collective-permute-start.2) | collective-permute-done | bytes 12320 | tf_op jit(solution)/shard_map/ppermute | solution.py:667
  47.4 0.0 collective-permute-done.3.east_in
  47.4 2.7 %all-to-all-done.1.received = f32[128,8,128]{2,1,0:T(8,128)S(1)} async-done(((f32[128,8,128]{2,1,0:T(8,128)}), f32[128,8,128]{2,1,0:T(8,128)S(1)}, u32[]{:S(2)}, u32[]{:S(2)}) %all-to-all-start.1) | async-done | bytes 524320 | tf_op jit(solution)/shard_map/all_to_all | solution.py:650
  50.1 1.9 %finish.1 = (f32[64,256]{1,0:T(8,128)}, f32[64,256]{1,0:T(8,128)}, f32[64,256]{1,0:T(8,128)}, f32[64,256]{1,0:T(8,128)}) custom-call(f32[128,8,128]{2,1,0:T(8,128)S(1)} %all-to-all-done.1.received, f32[24,128]{1,0:T(8,128)S(1)} %collective-permute-done.2.west_in, f32[24,128]{1,0:T(8,128)S(1)} %collective-permute-done.3.east_in, ...), custom_call_target="tpu_custom_call" | custom-call | tf_op jit(solution)/shard_map/finish/pallas_call | solution.py:560
Async XLA Ops:
  0.6 27.6 %copy-start = (f32[3,8,256]{2,1,0:T(8,128)S(1)}, f32[3,8,256]{2,1,0:T(8,128)}, u32[]{:S(2)}) copy-start(f32[3,8,256]{2,1,0:T(8,128)} %constant.14.clone.north_in.north) | copy-start | bytes 73732
  3.4 24.8 %all-to-all-start = ((f32[128,8,128]{2,1,0:T(8,128)}), f32[128,8,128]{2,1,0:T(8,128)S(1)}, u32[]{:S(2)}, u32[]{:S(2)}) async-start(f32[128,8,128]{2,1,0:T(8,128)} %get-tuple-element.18), calls=%async_computation | async-start | bytes 1048576 | tf_op jit(solution)/shard_map/all_to_all | solution.py:609
  14.9 6.9 %collective-permute-start = (f32[24,256]{1,0:T(8,128)}, f32[24,256]{1,0:T(8,128)S(1)}, u32[]{:S(2)}, u32[]{:S(2)}) collective-permute-start(f32[24,256]{1,0:T(8,128)} %get-tuple-element.19), channel_id=1, source_target_pairs={{0,16},{16,32},{32,48},{48,64},{64,80},{80,96},{96,112},{1,17},{17... | collective-permute-start | bytes 73736 | tf_op jit(solution)/shard_map/ppermute | solution.py:613
  18.6 6.1 %collective-permute-start.1 = (f32[24,256]{1,0:T(8,128)}, f32[24,256]{1,0:T(8,128)S(1)}, u32[]{:S(2)}, u32[]{:S(2)}) collective-permute-start(f32[24,256]{1,0:T(8,128)} %get-tuple-element.20), channel_id=1, source_target_pairs={{16,0},{32,16},{48,32},{64,48},{80,64},{96,80},{112,96},{17,1},{33... | collective-permute-start | bytes 73736 | tf_op jit(solution)/shard_map/ppermute | solution.py:614
  21.8 15.0 %copy-start.1 = (f32[24,256]{1,0:T(8,128)}, f32[24,256]{1,0:T(8,128)S(1)}, u32[]{:S(2)}) copy-start(f32[24,256]{1,0:T(8,128)S(1)} %collective-permute-done.south_in) | copy-start | bytes 73732
  24.7 12.1 %copy-start.2 = (f32[24,256]{1,0:T(8,128)}, f32[24,256]{1,0:T(8,128)S(1)}, u32[]{:S(2)}) copy-start(f32[24,256]{1,0:T(8,128)S(1)} %collective-permute-done.1.north_in) | copy-start | bytes 73732
  31.9 18.2 %all-to-all-start.1 = ((f32[128,8,128]{2,1,0:T(8,128)}), f32[128,8,128]{2,1,0:T(8,128)S(1)}, u32[]{:S(2)}, u32[]{:S(2)}) async-start(f32[128,8,128]{2,1,0:T(8,128)} %legendre.1), calls=%async_computation.1 | async-start | bytes 1048576 | tf_op jit(solution)/shard_map/all_to_all | solution.py:650
  38.8 8.6 %collective-permute-start.2 = (f32[24,128]{1,0:T(8,128)}, f32[24,128]{1,0:T(8,128)S(1)}, u32[]{:S(2)}, u32[]{:S(2)}) collective-permute-start(f32[24,128]{1,0:T(8,128)} %get-tuple-element.27), channel_id=1, source_target_pairs={{0,1},{1,2},{2,3},{3,4},{4,5},{5,6},{6,7},{7,8},{8,9},{9,10},{10,1... | collective-permute-start | bytes 36872 | tf_op jit(solution)/shard_map/ppermute | solution.py:667
  40.3 7.1 %collective-permute-start.3 = (f32[24,128]{1,0:T(8,128)}, f32[24,128]{1,0:T(8,128)S(1)}, u32[]{:S(2)}, u32[]{:S(2)}) collective-permute-start(f32[24,128]{1,0:T(8,128)} %get-tuple-element.28), channel_id=1, source_target_pairs={{1,0},{2,1},{3,2},{4,3},{5,4},{6,5},{7,6},{8,7},{9,8},{10,9},{11,1... | collective-permute-start | bytes 36872 | tf_op jit(solution)/shard_map/ppermute | solution.py:668

commit v5 on v4

--- a/solution.py
+++ b/solution.py
@@ -90,6 +90,23 @@
     order = np.arange(1, DEG)
     grown = 0.5 * math.log(2.0) + 0.5 * np.cumsum(np.log((2.0 * order + 1.0) / (2.0 * order)))
     return np.concatenate([[0.0], grown]).reshape(ORDERS, DEVS).astype(np.float32)
+
+
+def position(lat, lon):
+    return (lat % 2 * (LATS // 2) + lat // 2) * LONS + (lon + 4) % LONS
+
+
+def exchange(messages):
+    mesh_order = [(position(lat, lon), lat * LONS + lon) for lat in range(LATS) for lon in range(LONS)]
+    group = [place for _, place in sorted(mesh_order)]
+    return lax.all_to_all(
+        messages,
+        ("lat", "lon"),
+        split_axis=0,
+        concat_axis=0,
+        tiled=True,
+        axis_index_groups=[group],
+    )
 
 
 def iota(shape, dim):
@@ -253,6 +270,13 @@
 
 
 def setup_kernel(
+    height_in,
+    flux_u_in,
+    flux_v_in,
+    depth_in,
+    mask_in,
+    flux_in,
+    bands_in,
     love_in,
     balance_in,
     seeds_in,
@@ -260,23 +284,34 @@
     gains,
     balance,
     start,
+    own,
+    bands,
+    mask,
     love,
     seeds,
     north,
     sems,
 ):
-    device = lax.axis_index("lat") * LONS + lax.axis_index("lon")
+    device = position(lax.axis_index("lat"), lax.axis_index("lon"))
     loads = fetch(
         (
             (seeds_in, seeds),
             (north_in, north),
             (balance_in.at[device], balance),
             (love_in, love),
+            (height_in, own.at[0]),
+            (flux_u_in, own.at[1]),
+            (flux_v_in, own.at[2]),
+            (depth_in, own.at[3]),
+            (mask_in, mask),
+            (flux_in, own.at[5]),
+            (bands_in.at[lax.axis_index("lat")], bands),
         ),
         sems,
     )
     for load in loads:
         load.wait()
+    own[4] = mask[...].astype(f32)
     lane = iota((8, 128), 1)
     seed_log = jnp.sum(jnp.where(lane == device, seeds[...], 0.0), axis=1, keepdims=True)
     order = (device + DEVS * iota((8, 128), 0)).astype(f32)[:, :1]
@@ -287,16 +322,16 @@
 def legendre_kernel(
     received, gains, balance, start, north, message_out, high, low, message, out_sems
 ):
-    device = lax.axis_index("lat") * LONS + lax.axis_index("lon")
+    device = position(lax.axis_index("lat"), lax.axis_index("lon"))
     lane = iota((8, 128), 1)
     row = iota((8, 128), 0)
     left = lane < 64
 
     bands = []
     for lat in range(LATS):
-        band = received[lat * LONS]
+        band = received[position(lat, 0)]
         for lon in range(1, LONS):
-            band = band + received[lat * LONS + lon]
+            band = band + received[position(lat, lon)]
         bands.append(band)
     sums = bands[0]
     for band in bands[1:]:
@@ -402,8 +437,8 @@
             sent = jnp.where(slot, mean, sent)
             lat = 4 + part if north_side else 3 - part
             for lon in range(LONS):
-                message[lat * LONS + lon] = sent
-            part_place = pl.ds(lat * LONS, LONS)
+                message[position(lat, lon)] = sent
+            part_place = pl.ds(position(lat, 0) // LONS * LONS, LONS)
             copies += fetch(((message.at[part_place], message_out.at[part_place]),), out_sems.at[pl.ds(lat, 1)])
     for copy in copies:
         copy.wait()
@@ -414,7 +449,8 @@
     west_in,
     east_in,
     wave,
-    tiles,
+    own,
+    edges,
     bands,
     height_out,
     u_out,
@@ -439,7 +475,8 @@
     for slot in range(FIELDS):
         high_side = pltpu.roll(east, 128 - slot * WIDE, 1) if slot else east
         low_side = pltpu.roll(west, 128 - WIDE - slot * WIDE, 1)
-        blocks[slot, :, :COLS] = tiles[slot]
+        blocks[slot, :ROWS, :COLS] = own[slot]
+        blocks[slot, ROWS:, :COLS] = edges[slot]
         blocks[slot, :, COLS:] = jnp.where(
             wide_lane < WIDE, high_side, jnp.where(wide_lane >= 128 - WIDE, low_side, 0.0)
         )
@@ -483,53 +520,18 @@
         copy.wait()
 
 
-def column_kernel(
-    height_in,
-    flux_u_in,
-    flux_v_in,
-    depth_in,
-    mask_in,
-    flux_in,
-    south_in,
-    north_in,
-    bands_in,
-    west_out,
-    east_out,
-    blocks,
-    bands,
-    mask,
-    strips,
-    sides,
-    sems,
-    out_sems,
-):
-    own = pl.ds(0, ROWS)
-    loads = fetch(
-        (
-            (south_in, strips.at[0]),
-            (north_in, strips.at[1]),
-            (height_in, blocks.at[0, own]),
-            (flux_u_in, blocks.at[1, own]),
-            (flux_v_in, blocks.at[2, own]),
-            (depth_in, blocks.at[3, own]),
-            (mask_in, mask),
-            (flux_in, blocks.at[5, own]),
-            (bands_in.at[lax.axis_index("lat")], bands),
-        ),
-        sems,
-    )
+def column_kernel(from_south, from_north, own, west_out, east_out, edges, sides, out_sems):
     lane = iota((PAD_ROWS, 128), 1)
     west = jnp.zeros((PAD_ROWS, 128), f32)
     east = jnp.zeros((PAD_ROWS, 128), f32)
-    for load in loads:
-        load.wait()
-    blocks[4, 0:ROWS, :] = mask[...].astype(f32)
     for slot in range(FIELDS):
-        blocks[slot, ROWS : ROWS + WIDE, :] = strips[1, slot * WIDE : (slot + 1) * WIDE, :]
-        blocks[slot, ROWS + WIDE : PAD_ROWS, :] = strips[0, slot * WIDE : (slot + 1) * WIDE, :]
+        rows = slice(slot * WIDE, (slot + 1) * WIDE)
+        edges[slot, 0:WIDE, :] = from_north[rows, :]
+        edges[slot, WIDE : 2 * WIDE, :] = from_south[rows, :]
         here = (lane >= slot * WIDE) & (lane < (slot + 1) * WIDE)
-        west_part = blocks[slot, :, 0:128]
-        east_part = pltpu.roll(blocks[slot, :, COLS - 128 : COLS], (WIDE + slot * WIDE) % 128, 1)
+        west_part = jnp.concatenate([own[slot, :, 0:128], edges[slot, :, 0:128]], axis=0)
+        east_part = jnp.concatenate([own[slot, :, COLS - 128 :], edges[slot, :, COLS - 128 :]], axis=0)
+        east_part = pltpu.roll(east_part, (WIDE + slot * WIDE) % 128, 1)
         if slot:
             west_part = pltpu.roll(west_part, slot * WIDE, 1)
         west = jnp.where(here, west_part, west)
@@ -537,8 +539,7 @@
     fill = jnp.zeros((128 - PAD_ROWS, 128), f32)
     sides[0] = jnp.concatenate([west, fill], axis=0).T[:STRIP, :]
     sides[1] = jnp.concatenate([east, fill], axis=0).T[:STRIP, :]
-    pairs = ((sides.at[0], west_out), (sides.at[1], east_out))
-    for copy in fetch(pairs, out_sems):
+    for copy in fetch(((sides.at[0], west_out), (sides.at[1], east_out)), out_sems):
         copy.wait()
 
 
@@ -574,7 +575,6 @@
 
 
 def on_device(sea_height, trans_u, trans_v, depth, sea_mask, freshwater_flux, love_factor):
-    both_axes = ("lat", "lon")
     north = jnp.asarray(north_tables())
     fields = (sea_height, trans_u, trans_v, depth, sea_mask, freshwater_flux)
     vmem = pltpu.VMEM
@@ -606,7 +606,7 @@
         work=cost(6 * 2 * 1024 * 256 * 256, 3 << 20),
         near_out=(3,),
     )
-    received = lax.all_to_all(message, both_axes, split_axis=0, concat_axis=0, tiled=True)
+    received = exchange(message)
 
     upward = [(i, i + 1) for i in range(LATS - 1)]
     downward = [(i + 1, i) for i in range(LATS - 1)]
@@ -616,24 +616,28 @@
     gain_tiles = ((2 * len(PAIRS), ORDERS, TILE), f32)
     squares = ((ORDERS, DEG), f32)
     first_rows = ((ORDERS, HALF), f32)
-    gains, balance, start = far_call(
+    own_fields = ((FIELDS, ROWS, COLS), f32)
+    gains, balance, start, own, bands = far_call(
         setup_kernel,
         "setup",
-        (
+        fields
+        + (
+            jnp.asarray(row_tables()),
             love_factor.reshape(8, 128),
             jnp.asarray(balance_table()),
             jnp.asarray(seed_table()),
             north,
         ),
-        (gain_tiles, squares, first_rows),
+        (gain_tiles, squares, first_rows, own_fields, ((2, PAD_ROWS, 128), f32)),
         [
+            mask_tile,
             vmem((8, 128), f32),
             vmem((ORDERS, DEVS), f32),
             vmem((3, 8, HALF), f32),
-            copies((4,)),
+            copies((11,)),
         ],
         work=cost(2 << 20, 1 << 20),
-        near_out=(0, 1, 2),
+        near_out=(0, 1, 2, 3, 4),
     )
     received, from_south, from_north = lax.optimization_barrier((received, from_south, from_north))
     table = ((2 * len(PAIRS) * TILE, HALF), bf16)
@@ -647,22 +651,17 @@
         here=(0, 4),
         near=(1, 2, 3),
     )
-    answer = lax.all_to_all(reply, both_axes, split_axis=0, concat_axis=0, tiled=True)
-
-    padded = ((FIELDS, PAD_ROWS, COLS), f32)
-    to_west, to_east, blocks, bands = far_call(
+    answer = exchange(reply)
+
+    to_west, to_east, edges = far_call(
         column_kernel,
         "columns",
-        fields + (from_south, from_north, jnp.asarray(row_tables())),
-        (side, side, padded, ((2, PAD_ROWS, 128), f32)),
-        [
-            mask_tile,
-            vmem((2, STRIP, COLS), f32),
-            vmem((2, STRIP, 128), f32),
-            copies((9,)),
-            copies((2,)),
-        ],
-        near_out=(2, 3),
+        (from_south, from_north, own),
+        (side, side, ((FIELDS, 2 * WIDE, COLS), f32)),
+        [vmem((2, STRIP, 128), f32), copies((2,))],
+        here=(0, 1),
+        near=(2,),
+        near_out=(2,),
     )
     from_west = lax.ppermute(to_east, "lon", [(i, (i + 1) % LONS) for i in range(LONS)])
     from_east = lax.ppermute(to_west, "lon", [((i + 1) % LONS, i) for i in range(LONS)])
@@ -670,7 +669,7 @@
     return far_call(
         finish_kernel,
         "finish",
-        (answer, from_west, from_east, wave, blocks, bands),
+        (answer, from_west, from_east, wave, own, edges, bands),
         (tile,) * 4,
         [
             vmem((FIELDS, PAD_ROWS, PAD_COLS), f32),
@@ -678,7 +677,7 @@
             copies((4,)),
         ],
         here=(0, 1, 2),
-        near=(3, 4, 5),
+        near=(3, 4, 5, 6),
     )
 
 

time: 52.4 us -> 50.9 us (0.971)
  waiting for transfers between devices: 12.7 us -> 10.8 us
  starting transfers between devices: 26.9 us -> 28.3 us
  Pallas kernels: 11.6 us -> 10.8 us
    all_to_all x2, waiting for transfers between devices: 6.27 us -> 1.91 us  [exchange(): lax.all_to_all(messages, ('lat', 'lon'), split_axis=0, concat_axis=0, til...]
    all_to_all x2, starting transfers between devices: 16.4 us -> 17.8 us  [exchange(): lax.all_to_all(messages, ('lat', 'lon'), split_axis=0, concat_axis=0, til...]
    ppermute x1, waiting for transfers between devices: 3.58 us -> 4.79 us  [on_device(): lax.ppermute(to_east, 'lon', [(i, (i + 1) % LONS) for i in range(LONS)])]
    ppermute x1, waiting for transfers between devices: 2.89 us -> 4.06 us  [on_device(): from_north = lax.ppermute(strip_south, 'lat', downward)]
    pallas_call x5, Pallas kernels: 11.6 us -> 10.8 us  [far_call(): pl.pallas_call(kernel, out_shape=tuple((space(*result) for space, result...]
  transfers between devices with their start and end apart: 6 -> 6, of which waited for: 4 -> 4; matrix products, arithmetic and copies ran while one was open for 0% -> 0% of each run, Pallas kernels for 6% -> 5%
where the time goes in v5:
time: 50.9 us; the launch traced here: 50.6 us
  starting transfers between devices  28.3 us (56%)
  Pallas kernels  10.8 us (21%)
  waiting for transfers between devices  10.8 us (21%)
  between operations  0.71 us (1%)
    all_to_all x2, starting transfers between devices, exchange(): lax.all_to_all(messages, ('lat', 'lon'), split_axis=0, concat_axis=0, til...  17.8 us
    pallas_call x5, Pallas kernels, far_call(): pl.pallas_call(kernel, out_shape=tuple((space(*result) for space, result...  10.8 us
    ppermute x1, waiting for transfers between devices, on_device(): lax.ppermute(to_east, 'lon', [(i, (i + 1) % LONS) for i in range(LONS)])  4.79 us
    ppermute x1, waiting for transfers between devices, on_device(): from_north = lax.ppermute(strip_south, 'lat', downward)  4.06 us
    ppermute x1, starting transfers between devices, on_device(): from_south = lax.ppermute(strip_north, 'lat', upward)  3.66 us
    ppermute x1, starting transfers between devices, on_device(): lax.ppermute(to_west, 'lon', [((i + 1) % LONS, i) for i in range(LONS)])  3.5 us
    ppermute x1, starting transfers between devices, on_device(): from_north = lax.ppermute(strip_south, 'lat', downward)  1.92 us
    all_to_all x2, waiting for transfers between devices, exchange(): lax.all_to_all(messages, ('lat', 'lon'), split_axis=0, concat_axis=0, til...  1.91 us
  transfers between devices with their start and end apart: 6, of which 4 were waited for; matrix products, arithmetic and copies ran while one was open for 0% of the time, Pallas kernels for 5%

profile of v5, /device:TPU:1, one launch (start us, length us, event | category | flops | bytes accessed | tf_op | source)
XLA Modules:
  0.0 50.6 jit_solution(14400212100578292343)
XLA Ops:
  0.6 2.7 %forward.1 = (f32[128,8,128]{2,1,0:T(8,128)}, f32[24,256]{1,0:T(8,128)}, f32[24,256]{1,0:T(8,128)}, bf16[4,4,256,256]{3,2,1,0:T(8,128)(2,1)S(1)}) custom-call(f32[64,256]{1,0:T(8,128)} %height_in.3, f32[64,256]{1,0:T(8,128)} %flux_u_in.3, f32[64,256]{1,0:T(8,128)} %flux_v_in.3, f32[64,256]{1,0:T(8,128)} %depth_in.3, s32[64,256]{1,0:T(8,128)} %mask_in.3, ...), custom_call_target="tpu_custom_call" | custom-call | flops 805306368 | bytes 3145728 | tf_op jit(solution)/shard_map/forward/pallas_call | solution.py:561
  3.4 0.0 copy-start
  3.4 11.5 %all-to-all-start = ((f32[128,8,128]{2,1,0:T(8,128)}), f32[128,8,128]{2,1,0:T(8,128)S(1)}, u32[]{:S(2)}, u32[]{:S(2)}) async-start(f32[128,8,128]{2,1,0:T(8,128)} %get-tuple-element.19), calls=%async_computation | async-start | bytes 1048576 | tf_op jit(solution)/shard_map/all_to_all | solution.py:102
  14.9 3.7 %collective-permute-start = (f32[24,256]{1,0:T(8,128)}, f32[24,256]{1,0:T(8,128)S(1)}, u32[]{:S(2)}, u32[]{:S(2)}) collective-permute-start(f32[24,256]{1,0:T(8,128)} %get-tuple-element.20), channel_id=1, source_target_pairs={{0,16},{16,32},{32,48},{48,64},{64,80},{80,96},{96,112},{1,17},{17... | collective-permute-start | bytes 73736 | tf_op jit(solution)/shard_map/ppermute | solution.py:613
  18.6 1.9 %collective-permute-start.1 = (f32[24,256]{1,0:T(8,128)}, f32[24,256]{1,0:T(8,128)S(1)}, u32[]{:S(2)}, u32[]{:S(2)}) collective-permute-start(f32[24,256]{1,0:T(8,128)} %get-tuple-element.21), channel_id=1, source_target_pairs={{16,0},{32,16},{48,32},{64,48},{80,64},{96,80},{112,96},{17,1},{33... | collective-permute-start | bytes 73736 | tf_op jit(solution)/shard_map/ppermute | solution.py:614
  20.5 1.7 %setup.1 = (f32[22,8,256]{2,1,0:T(8,128)S(1)}, f32[8,1024]{1,0:T(8,128)S(1)}, f32[8,256]{1,0:T(8,128)S(1)}, f32[6,64,256]{2,1,0:T(8,128)S(1)}, f32[2,72,128]{2,1,0:T(8,128)S(1)}) custom-call(f32[64,256]{1,0:T(8,128)} %height_in.3, f32[64,256]{1,0:T(8,128)} %flux_u_in.3, f32[64,256]{1,0:T(8,128)} %flux_v_in.3, f32[64,256]{1,0:T(8,128)} %depth_in.3, ...), custom_call_target="tpu_custom_call" | custom-call | flops 2097152 | bytes 1048576 | tf_op jit(solution)/shard_map/setup/pallas_call | solution.py:561
  22.2 0.0 collective-permute-done.from_south
  22.2 4.1 %collective-permute-done.1.from_north = f32[24,256]{1,0:T(8,128)S(1)} collective-permute-done((f32[24,256]{1,0:T(8,128)}, f32[24,256]{1,0:T(8,128)S(1)}, u32[]{:S(2)}, u32[]{:S(2)}) %collective-permute-start.1) | collective-permute-done | bytes 24608 | tf_op jit(solution)/shard_map/ppermute | solution.py:614
  26.2 0.6 %all-to-all-done.received = f32[128,8,128]{2,1,0:T(8,128)S(1)} async-done(((f32[128,8,128]{2,1,0:T(8,128)}), f32[128,8,128]{2,1,0:T(8,128)S(1)}, u32[]{:S(2)}, u32[]{:S(2)}) %all-to-all-start) | async-done | bytes 524320 | tf_op jit(solution)/shard_map/all_to_all | solution.py:102
  26.8 0.0 copy-done
  26.8 3.7 %legendre.1 = f32[128,8,128]{2,1,0:T(8,128)} custom-call(f32[128,8,128]{2,1,0:T(8,128)S(1)} %all-to-all-done.received, f32[22,8,256]{2,1,0:T(8,128)S(1)} %get-tuple-element.23.gains, f32[8,1024]{1,0:T(8,128)S(1)} %get-tuple-element.24.balance, f32[8,256]{1,0:T(8,128)S(1)} %get-tuple-element.25.start, f32[3,8,256]{2,1,0:T(8,128)S(1)} %copy-done), custom_call_target="tpu_custom_call" | custom-call | flops 1610612736 | bytes 9437184 | tf_op jit(solution)/shard_map/legendre/pallas_call | solution.py:561
  30.5 6.3 %all-to-all-start.1 = ((f32[128,8,128]{2,1,0:T(8,128)}), f32[128,8,128]{2,1,0:T(8,128)S(1)}, u32[]{:S(2)}, u32[]{:S(2)}) async-start(f32[128,8,128]{2,1,0:T(8,128)} %legendre.1), calls=%async_computation.1 | async-start | bytes 1048576 | tf_op jit(solution)/shard_map/all_to_all | solution.py:102
  36.8 0.9 %columns.1 = (f32[24,128]{1,0:T(8,128)}, f32[24,128]{1,0:T(8,128)}, f32[6,8,256]{2,1,0:T(8,128)S(1)}) custom-call(f32[24,256]{1,0:T(8,128)S(1)} %collective-permute-done.from_south, f32[24,256]{1,0:T(8,128)S(1)} %collective-permute-done.1.from_north, f32[6,64,256]{2,1,0:T(8,128)S(1)} %get-tuple-element.28.own), custom_call_target="tpu_custom_call" | custom-call | tf_op jit(solution)/shard_map/columns/pallas_call | solution.py:561
  37.6 1.5 %collective-permute-start.2 = (f32[24,128]{1,0:T(8,128)}, f32[24,128]{1,0:T(8,128)S(1)}, u32[]{:S(2)}, u32[]{:S(2)}) collective-permute-start(f32[24,128]{1,0:T(8,128)} %get-tuple-element.29), channel_id=1, source_target_pairs={{0,1},{1,2},{2,3},{3,4},{4,5},{5,6},{6,7},{7,8},{8,9},{9,10},{10,1... | collective-permute-start | bytes 36872 | tf_op jit(solution)/shard_map/ppermute | solution.py:666
  39.1 3.5 %collective-permute-start.3 = (f32[24,128]{1,0:T(8,128)}, f32[24,128]{1,0:T(8,128)S(1)}, u32[]{:S(2)}, u32[]{:S(2)}) collective-permute-start(f32[24,128]{1,0:T(8,128)} %get-tuple-element.30), channel_id=1, source_target_pairs={{1,0},{2,1},{3,2},{4,3},{5,4},{6,5},{7,6},{8,7},{9,8},{10,9},{11,1... | collective-permute-start | bytes 36872 | tf_op jit(solution)/shard_map/ppermute | solution.py:667
  42.6 4.8 %collective-permute-done.2.west_in = f32[24,128]{1,0:T(8,128)S(1)} collective-permute-done((f32[24,128]{1,0:T(8,128)}, f32[24,128]{1,0:T(8,128)S(1)}, u32[]{:S(2)}, u32[]{:S(2)}) %collective-permute-start.2) | collective-permute-done | bytes 12320 | tf_op jit(solution)/shard_map/ppermute | solution.py:666
  47.4 0.0 collective-permute-done.3.east_in
  47.4 1.3 %all-to-all-done.1.received = f32[128,8,128]{2,1,0:T(8,128)S(1)} async-done(((f32[128,8,128]{2,1,0:T(8,128)}), f32[128,8,128]{2,1,0:T(8,128)S(1)}, u32[]{:S(2)}, u32[]{:S(2)}) %all-to-all-start.1) | async-done | bytes 524320 | tf_op jit(solution)/shard_map/all_to_all | solution.py:102
  48.7 1.9 %finish.1 = (f32[64,256]{1,0:T(8,128)}, f32[64,256]{1,0:T(8,128)}, f32[64,256]{1,0:T(8,128)}, f32[64,256]{1,0:T(8,128)}) custom-call(f32[128,8,128]{2,1,0:T(8,128)S(1)} %all-to-all-done.1.received, f32[24,128]{1,0:T(8,128)S(1)} %collective-permute-done.2.west_in, f32[24,128]{1,0:T(8,128)S(1)} %collective-permute-done.3.east_in, ...), custom_call_target="tpu_custom_call" | custom-call | tf_op jit(solution)/shard_map/finish/pallas_call | solution.py:561
Async XLA Ops:
  3.4 23.5 %copy-start = (f32[3,8,256]{2,1,0:T(8,128)S(1)}, f32[3,8,256]{2,1,0:T(8,128)}, u32[]{:S(2)}) copy-start(f32[3,8,256]{2,1,0:T(8,128)} %constant.14.clone.north_in.north) | copy-start | bytes 73732
  3.4 23.5 %all-to-all-start = ((f32[128,8,128]{2,1,0:T(8,128)}), f32[128,8,128]{2,1,0:T(8,128)S(1)}, u32[]{:S(2)}, u32[]{:S(2)}) async-start(f32[128,8,128]{2,1,0:T(8,128)} %get-tuple-element.19), calls=%async_computation | async-start | bytes 1048576 | tf_op jit(solution)/shard_map/all_to_all | solution.py:102
  14.9 7.3 %collective-permute-start = (f32[24,256]{1,0:T(8,128)}, f32[24,256]{1,0:T(8,128)S(1)}, u32[]{:S(2)}, u32[]{:S(2)}) collective-permute-start(f32[24,256]{1,0:T(8,128)} %get-tuple-element.20), channel_id=1, source_target_pairs={{0,16},{16,32},{32,48},{48,64},{64,80},{80,96},{96,112},{1,17},{17... | collective-permute-start | bytes 73736 | tf_op jit(solution)/shard_map/ppermute | solution.py:613
  18.6 7.7 %collective-permute-start.1 = (f32[24,256]{1,0:T(8,128)}, f32[24,256]{1,0:T(8,128)S(1)}, u32[]{:S(2)}, u32[]{:S(2)}) collective-permute-start(f32[24,256]{1,0:T(8,128)} %get-tuple-element.21), channel_id=1, source_target_pairs={{16,0},{32,16},{48,32},{64,48},{80,64},{96,80},{112,96},{17,1},{33... | collective-permute-start | bytes 73736 | tf_op jit(solution)/shard_map/ppermute | solution.py:614
  30.5 18.2 %all-to-all-start.1 = ((f32[128,8,128]{2,1,0:T(8,128)}), f32[128,8,128]{2,1,0:T(8,128)S(1)}, u32[]{:S(2)}, u32[]{:S(2)}) async-start(f32[128,8,128]{2,1,0:T(8,128)} %legendre.1), calls=%async_computation.1 | async-start | bytes 1048576 | tf_op jit(solution)/shard_map/all_to_all | solution.py:102
  37.6 9.8 %collective-permute-start.2 = (f32[24,128]{1,0:T(8,128)}, f32[24,128]{1,0:T(8,128)S(1)}, u32[]{:S(2)}, u32[]{:S(2)}) collective-permute-start(f32[24,128]{1,0:T(8,128)} %get-tuple-element.29), channel_id=1, source_target_pairs={{0,1},{1,2},{2,3},{3,4},{4,5},{5,6},{6,7},{7,8},{8,9},{9,10},{10,1... | collective-permute-start | bytes 36872 | tf_op jit(solution)/shard_map/ppermute | solution.py:666
  39.1 8.3 %collective-permute-start.3 = (f32[24,128]{1,0:T(8,128)}, f32[24,128]{1,0:T(8,128)S(1)}, u32[]{:S(2)}, u32[]{:S(2)}) collective-permute-start(f32[24,128]{1,0:T(8,128)} %get-tuple-element.30), channel_id=1, source_target_pairs={{1,0},{2,1},{3,2},{4,3},{5,4},{6,5},{7,6},{8,7},{9,8},{10,9},{11,1... | collective-permute-start | bytes 36872 | tf_op jit(solution)/shard_map/ppermute | solution.py:667

commit v6 on v5

--- a/solution.py
+++ b/solution.py
@@ -152,8 +152,8 @@
     step_in,
     area_in,
     message_out,
-    north_out,
-    south_out,
+    near_out,
+    far_out,
     wave,
     tiles,
     mask,
@@ -232,7 +232,8 @@
     for slot, values in enumerate((tiles[0], tiles[1], tiles[2], tiles[3], sea, tiles[4])):
         strips[0, slot * WIDE : (slot + 1) * WIDE, :] = values[ROWS - WIDE :, :]
         strips[1, slot * WIDE : (slot + 1) * WIDE, :] = values[:WIDE, :]
-    sends += fetch(((strips.at[0], north_out), (strips.at[1], south_out)), strip_sems)
+    odd = lat_index % 2
+    sends += fetch(((strips.at[odd], near_out), (strips.at[1 - odd], far_out)), strip_sems)
     for copy in sends:
         copy.wait()
 
@@ -446,8 +447,8 @@
 
 def finish_kernel(
     received,
-    west_in,
-    east_in,
+    from_near,
+    from_far,
     wave,
     own,
     edges,
@@ -462,16 +463,22 @@
 ):
     lat_index = lax.axis_index("lat")
     lane = iota((8, 128), 1)
-    mean = jnp.sum(jnp.where((iota((8, 128), 0) == 0) & (lane == 64), received[0], 0.0))
-    turned = received[...].reshape(DEG, 128).T
+    first_row = iota((8, 128), 0) == 0
+    mean = jnp.sum(jnp.where(first_row & (lane == 64), received[0], 0.0))
+    first = jnp.where(first_row & (lane >= 64), 0.0, received[0])
+    others = received[1:].reshape(DEG - ORDERS, 128)
+    turned = jnp.concatenate([first, others], axis=0).T
     high, low = halves(turned)
     cos_both = jnp.concatenate([high[:64], low[:64]], axis=0)
     sin_both = jnp.concatenate([high[64:], low[64:]], axis=0)
 
     wide_lane = iota((PAD_ROWS, 128), 1)
     fill = jnp.zeros((128 - STRIP, 128), f32)
-    west = jnp.concatenate([west_in[...], fill], axis=0).T[:PAD_ROWS, :]
-    east = jnp.concatenate([east_in[...], fill], axis=0).T[:PAD_ROWS, :]
+    odd_lon = lax.axis_index("lon") % 2 == 1
+    west_in = jnp.where(odd_lon, from_near[...], from_far[...])
+    east_in = jnp.where(odd_lon, from_far[...], from_near[...])
+    west = jnp.concatenate([west_in, fill], axis=0).T[:PAD_ROWS, :]
+    east = jnp.concatenate([east_in, fill], axis=0).T[:PAD_ROWS, :]
     for slot in range(FIELDS):
         high_side = pltpu.roll(east, 128 - slot * WIDE, 1) if slot else east
         low_side = pltpu.roll(west, 128 - WIDE - slot * WIDE, 1)
@@ -520,14 +527,17 @@
         copy.wait()
 
 
-def column_kernel(from_south, from_north, own, west_out, east_out, edges, sides, out_sems):
+def column_kernel(from_near, from_far, own, near_out, far_out, edges, sides, out_sems):
+    odd_lat = lax.axis_index("lat") % 2 == 1
+    odd = lax.axis_index("lon") % 2
     lane = iota((PAD_ROWS, 128), 1)
     west = jnp.zeros((PAD_ROWS, 128), f32)
     east = jnp.zeros((PAD_ROWS, 128), f32)
     for slot in range(FIELDS):
         rows = slice(slot * WIDE, (slot + 1) * WIDE)
-        edges[slot, 0:WIDE, :] = from_north[rows, :]
-        edges[slot, WIDE : 2 * WIDE, :] = from_south[rows, :]
+        one, other = from_near[rows, :], from_far[rows, :]
+        edges[slot, 0:WIDE, :] = jnp.where(odd_lat, other, one)
+        edges[slot, WIDE : 2 * WIDE, :] = jnp.where(odd_lat, one, other)
         here = (lane >= slot * WIDE) & (lane < (slot + 1) * WIDE)
         west_part = jnp.concatenate([own[slot, :, 0:128], edges[slot, :, 0:128]], axis=0)
         east_part = jnp.concatenate([own[slot, :, COLS - 128 :], edges[slot, :, COLS - 128 :]], axis=0)
@@ -537,9 +547,9 @@
         west = jnp.where(here, west_part, west)
         east = jnp.where(here, east_part, east)
     fill = jnp.zeros((128 - PAD_ROWS, 128), f32)
-    sides[0] = jnp.concatenate([west, fill], axis=0).T[:STRIP, :]
-    sides[1] = jnp.concatenate([east, fill], axis=0).T[:STRIP, :]
-    for copy in fetch(((sides.at[0], west_out), (sides.at[1], east_out)), out_sems):
+    sides[1] = jnp.concatenate([west, fill], axis=0).T[:STRIP, :]
+    sides[0] = jnp.concatenate([east, fill], axis=0).T[:STRIP, :]
+    for copy in fetch(((sides.at[odd], near_out), (sides.at[1 - odd], far_out)), out_sems):
         copy.wait()
 
 
@@ -586,7 +596,7 @@
     tiles = vmem((FIELDS, ROWS, COLS), f32)
     mask_tile = vmem((ROWS, COLS), jnp.int32)
 
-    message, strip_north, strip_south, wave = far_call(
+    message, strip_near, strip_far, wave = far_call(
         forward_kernel,
         "forward",
         fields + (jnp.asarray(turn_tables()), jnp.asarray(step_tables()), jnp.asarray(area_table())),
@@ -608,10 +618,10 @@
     )
     received = exchange(message)
 
-    upward = [(i, i + 1) for i in range(LATS - 1)]
-    downward = [(i + 1, i) for i in range(LATS - 1)]
-    from_south = lax.ppermute(strip_north, "lat", upward)
-    from_north = lax.ppermute(strip_south, "lat", downward)
+    near_pairs = [(i, i ^ 1) for i in range(LATS)]
+    far_pairs = [(i, ((i + 1) ^ 1) - 1) for i in range(1, LATS - 1)]
+    from_near = lax.ppermute(strip_near, "lat", near_pairs)
+    from_far = lax.ppermute(strip_far, "lat", far_pairs)
 
     gain_tiles = ((2 * len(PAIRS), ORDERS, TILE), f32)
     squares = ((ORDERS, DEG), f32)
@@ -639,7 +649,7 @@
         work=cost(2 << 20, 1 << 20),
         near_out=(0, 1, 2, 3, 4),
     )
-    received, from_south, from_north = lax.optimization_barrier((received, from_south, from_north))
+    received, from_near, from_far = lax.optimization_barrier((received, from_near, from_far))
     table = ((2 * len(PAIRS) * TILE, HALF), bf16)
     (reply,) = far_call(
         legendre_kernel,
@@ -653,23 +663,25 @@
     )
     answer = exchange(reply)
 
-    to_west, to_east, edges = far_call(
+    to_near, to_far, edges = far_call(
         column_kernel,
         "columns",
-        (from_south, from_north, own),
+        (from_near, from_far, own),
         (side, side, ((FIELDS, 2 * WIDE, COLS), f32)),
         [vmem((2, STRIP, 128), f32), copies((2,))],
         here=(0, 1),
         near=(2,),
         near_out=(2,),
     )
-    from_west = lax.ppermute(to_east, "lon", [(i, (i + 1) % LONS) for i in range(LONS)])
-    from_east = lax.ppermute(to_west, "lon", [((i + 1) % LONS, i) for i in range(LONS)])
+    near_lons = [(i, i ^ 1) for i in range(LONS)]
+    far_lons = [(i, (((i + 1) ^ 1) - 1) % LONS) for i in range(LONS)]
+    side_near = lax.ppermute(to_near, "lon", near_lons)
+    side_far = lax.ppermute(to_far, "lon", far_lons)
 
     return far_call(
         finish_kernel,
         "finish",
-        (answer, from_west, from_east, wave, own, edges, bands),
+        (answer, side_near, side_far, wave, own, edges, bands),
         (tile,) * 4,
         [
             vmem((FIELDS, PAD_ROWS, PAD_COLS), f32),

time: 50.9 us -> 50.5 us (level)
  starting transfers between devices: 28.3 us -> 26.6 us
  waiting for transfers between devices: 10.8 us -> 12 us
    all_to_all x2, waiting for transfers between devices: 1.91 us -> 6.45 us  [exchange(): lax.all_to_all(messages, ('lat', 'lon'), split_axis=0, concat_axis=0, til...]
    ppermute x4, waiting for transfers between devices: 8.86 us -> 5.6 us  [the longest x1 4.35 us: on_device(): side_far = lax.ppermute(to_far, 'lon', far_lons)]
    ppermute x4, starting transfers between devices: 10.5 us -> 9.28 us  [the longest x1 3.93 us: on_device(): side_far = lax.ppermute(to_far, 'lon', far_lons)]
where the time goes in v6:
time: 50.5 us; the launch traced here: 50.2 us
  starting transfers between devices  26.6 us (53%)
  waiting for transfers between devices  12 us (24%)
  Pallas kernels  10.8 us (21%)
  between operations  0.71 us (1%)
    all_to_all x2, starting transfers between devices, exchange(): lax.all_to_all(messages, ('lat', 'lon'), split_axis=0, concat_axis=0, til...  17.4 us
    pallas_call x5, Pallas kernels, far_call(): pl.pallas_call(kernel, out_shape=tuple((space(*result) for space, result...  10.8 us
    all_to_all x2, waiting for transfers between devices, exchange(): lax.all_to_all(messages, ('lat', 'lon'), split_axis=0, concat_axis=0, til...  6.45 us
    ppermute x1, waiting for transfers between devices, on_device(): side_far = lax.ppermute(to_far, 'lon', far_lons)  4.35 us
    ppermute x1, starting transfers between devices, on_device(): side_far = lax.ppermute(to_far, 'lon', far_lons)  3.93 us
    ppermute x1, starting transfers between devices, on_device(): from_far = lax.ppermute(strip_far, 'lat', far_pairs)  2.73 us
    ppermute x1, starting transfers between devices, on_device(): side_near = lax.ppermute(to_near, 'lon', near_lons)  1.47 us
    ppermute x1, waiting for transfers between devices, on_device(): from_far = lax.ppermute(strip_far, 'lat', far_pairs)  1.24 us
  transfers between devices with their start and end apart: 6, of which 4 were waited for; matrix products, arithmetic and copies ran while one was open for 0% of the time, Pallas kernels for 5%

profile of v6, /device:TPU:1, one launch (start us, length us, event | category | flops | bytes accessed | tf_op | source)
XLA Modules:
  0.0 50.2 jit_solution(17225863760279927583)
XLA Ops:
  0.6 2.7 %forward.1 = (f32[128,8,128]{2,1,0:T(8,128)}, f32[24,256]{1,0:T(8,128)}, f32[24,256]{1,0:T(8,128)}, bf16[4,4,256,256]{3,2,1,0:T(8,128)(2,1)S(1)}) custom-call(f32[64,256]{1,0:T(8,128)} %height_in.3, f32[64,256]{1,0:T(8,128)} %flux_u_in.3, f32[64,256]{1,0:T(8,128)} %flux_v_in.3, f32[64,256]{1,0:T(8,128)} %depth_in.3, s32[64,256]{1,0:T(8,128)} %mask_in.3, ...), custom_call_target="tpu_custom_call" | custom-call | flops 805306368 | bytes 3145728 | tf_op jit(solution)/shard_map/forward/pallas_call | solution.py:571
  3.4 0.0 copy-start
  3.4 11.5 %all-to-all-start = ((f32[128,8,128]{2,1,0:T(8,128)}), f32[128,8,128]{2,1,0:T(8,128)S(1)}, u32[]{:S(2)}, u32[]{:S(2)}) async-start(f32[128,8,128]{2,1,0:T(8,128)} %get-tuple-element.19), calls=%async_computation | async-start | bytes 1048576 | tf_op jit(solution)/shard_map/all_to_all | solution.py:102
  14.9 1.1 %collective-permute-start = (f32[24,256]{1,0:T(8,128)}, f32[24,256]{1,0:T(8,128)S(1)}, u32[]{:S(2)}, u32[]{:S(2)}) collective-permute-start(f32[24,256]{1,0:T(8,128)} %get-tuple-element.20), channel_id=1, source_target_pairs={{0,16},{16,0},{32,48},{48,32},{64,80},{80,64},{96,112},{112,96},{1... | collective-permute-start | bytes 73736 | tf_op jit(solution)/shard_map/ppermute | solution.py:623
  16.0 2.7 %collective-permute-start.1 = (f32[24,256]{1,0:T(8,128)}, f32[24,256]{1,0:T(8,128)S(1)}, u32[]{:S(2)}, u32[]{:S(2)}) collective-permute-start(f32[24,256]{1,0:T(8,128)} %get-tuple-element.21), channel_id=1, source_target_pairs={{16,32},{32,16},{48,64},{64,48},{80,96},{96,80},{17,33},{33,17},{4... | collective-permute-start | bytes 73736 | tf_op jit(solution)/shard_map/ppermute | solution.py:624
  18.8 1.7 %setup.1 = (f32[22,8,256]{2,1,0:T(8,128)S(1)}, f32[8,1024]{1,0:T(8,128)S(1)}, f32[8,256]{1,0:T(8,128)S(1)}, f32[6,64,256]{2,1,0:T(8,128)S(1)}, f32[2,72,128]{2,1,0:T(8,128)S(1)}) custom-call(f32[64,256]{1,0:T(8,128)} %height_in.3, f32[64,256]{1,0:T(8,128)} %flux_u_in.3, f32[64,256]{1,0:T(8,128)} %flux_v_in.3, f32[64,256]{1,0:T(8,128)} %depth_in.3, ...), custom_call_target="tpu_custom_call" | custom-call | flops 2097152 | bytes 1048576 | tf_op jit(solution)/shard_map/setup/pallas_call | solution.py:571
  20.5 0.0 collective-permute-done.from_near
  20.5 1.2 %collective-permute-done.1.from_far = f32[24,256]{1,0:T(8,128)S(1)} collective-permute-done((f32[24,256]{1,0:T(8,128)}, f32[24,256]{1,0:T(8,128)S(1)}, u32[]{:S(2)}, u32[]{:S(2)}) %collective-permute-start.1) | collective-permute-done | bytes 24608 | tf_op jit(solution)/shard_map/ppermute | solution.py:624
  21.7 5.1 %all-to-all-done.received = f32[128,8,128]{2,1,0:T(8,128)S(1)} async-done(((f32[128,8,128]{2,1,0:T(8,128)}), f32[128,8,128]{2,1,0:T(8,128)S(1)}, u32[]{:S(2)}, u32[]{:S(2)}) %all-to-all-start) | async-done | bytes 524320 | tf_op jit(solution)/shard_map/all_to_all | solution.py:102
  26.8 0.0 copy-done
  26.8 3.7 %legendre.1 = f32[128,8,128]{2,1,0:T(8,128)} custom-call(f32[128,8,128]{2,1,0:T(8,128)S(1)} %all-to-all-done.received, f32[22,8,256]{2,1,0:T(8,128)S(1)} %get-tuple-element.23.gains, f32[8,1024]{1,0:T(8,128)S(1)} %get-tuple-element.24.balance, f32[8,256]{1,0:T(8,128)S(1)} %get-tuple-element.25.start, f32[3,8,256]{2,1,0:T(8,128)S(1)} %copy-done), custom_call_target="tpu_custom_call" | custom-call | flops 1610612736 | bytes 9437184 | tf_op jit(solution)/shard_map/legendre/pallas_call | solution.py:571
  30.5 5.9 %all-to-all-start.1 = ((f32[128,8,128]{2,1,0:T(8,128)}), f32[128,8,128]{2,1,0:T(8,128)S(1)}, u32[]{:S(2)}, u32[]{:S(2)}) async-start(f32[128,8,128]{2,1,0:T(8,128)} %legendre.1), calls=%async_computation.1 | async-start | bytes 1048576 | tf_op jit(solution)/shard_map/all_to_all | solution.py:102
  36.4 0.9 %columns.1 = (f32[24,128]{1,0:T(8,128)}, f32[24,128]{1,0:T(8,128)}, f32[6,8,256]{2,1,0:T(8,128)S(1)}) custom-call(f32[24,256]{1,0:T(8,128)S(1)} %collective-permute-done.from_near, f32[24,256]{1,0:T(8,128)S(1)} %collective-permute-done.1.from_far, f32[6,64,256]{2,1,0:T(8,128)S(1)} %get-tuple-element.28.own), custom_call_target="tpu_custom_call" | custom-call | tf_op jit(solution)/shard_map/columns/pallas_call | solution.py:571
  37.2 1.5 %collective-permute-start.2 = (f32[24,128]{1,0:T(8,128)}, f32[24,128]{1,0:T(8,128)S(1)}, u32[]{:S(2)}, u32[]{:S(2)}) collective-permute-start(f32[24,128]{1,0:T(8,128)} %get-tuple-element.29), channel_id=1, source_target_pairs={{0,1},{1,0},{2,3},{3,2},{4,5},{5,4},{6,7},{7,6},{8,9},{9,8},{10,11... | collective-permute-start | bytes 36872 | tf_op jit(solution)/shard_map/ppermute | solution.py:678
  38.7 3.9 %collective-permute-start.3 = (f32[24,128]{1,0:T(8,128)}, f32[24,128]{1,0:T(8,128)S(1)}, u32[]{:S(2)}, u32[]{:S(2)}) collective-permute-start(f32[24,128]{1,0:T(8,128)} %get-tuple-element.30), channel_id=1, source_target_pairs={{0,15},{1,2},{2,1},{3,4},{4,3},{5,6},{6,5},{7,8},{8,7},{9,10},{10,... | collective-permute-start | bytes 36872 | tf_op jit(solution)/shard_map/ppermute | solution.py:679
  42.6 0.0 collective-permute-done.2.from_near
  42.6 4.4 %collective-permute-done.3.from_far = f32[24,128]{1,0:T(8,128)S(1)} collective-permute-done((f32[24,128]{1,0:T(8,128)}, f32[24,128]{1,0:T(8,128)S(1)}, u32[]{:S(2)}, u32[]{:S(2)}) %collective-permute-start.3) | collective-permute-done | bytes 12320 | tf_op jit(solution)/shard_map/ppermute | solution.py:679
  47.0 1.3 %all-to-all-done.1.received = f32[128,8,128]{2,1,0:T(8,128)S(1)} async-done(((f32[128,8,128]{2,1,0:T(8,128)}), f32[128,8,128]{2,1,0:T(8,128)S(1)}, u32[]{:S(2)}, u32[]{:S(2)}) %all-to-all-start.1) | async-done | bytes 524320 | tf_op jit(solution)/shard_map/all_to_all | solution.py:102
  48.3 1.9 %finish.1 = (f32[64,256]{1,0:T(8,128)}, f32[64,256]{1,0:T(8,128)}, f32[64,256]{1,0:T(8,128)}, f32[64,256]{1,0:T(8,128)}) custom-call(f32[128,8,128]{2,1,0:T(8,128)S(1)} %all-to-all-done.1.received, f32[24,128]{1,0:T(8,128)S(1)} %collective-permute-done.2.from_near, f32[24,128]{1,0:T(8,128)S(1)} %collective-permute-done.3.from_far, ...), custom_call_target="tpu_custom_call" | custom-call | tf_op jit(solution)/shard_map/finish/pallas_call | solution.py:571
Async XLA Ops:
  3.4 23.5 %copy-start = (f32[3,8,256]{2,1,0:T(8,128)S(1)}, f32[3,8,256]{2,1,0:T(8,128)}, u32[]{:S(2)}) copy-start(f32[3,8,256]{2,1,0:T(8,128)} %constant.14.clone.north_in.north) | copy-start | bytes 73732
  3.4 23.5 %all-to-all-start = ((f32[128,8,128]{2,1,0:T(8,128)}), f32[128,8,128]{2,1,0:T(8,128)S(1)}, u32[]{:S(2)}, u32[]{:S(2)}) async-start(f32[128,8,128]{2,1,0:T(8,128)} %get-tuple-element.19), calls=%async_computation | async-start | bytes 1048576 | tf_op jit(solution)/shard_map/all_to_all | solution.py:102
  14.9 5.6 %collective-permute-start = (f32[24,256]{1,0:T(8,128)}, f32[24,256]{1,0:T(8,128)S(1)}, u32[]{:S(2)}, u32[]{:S(2)}) collective-permute-start(f32[24,256]{1,0:T(8,128)} %get-tuple-element.20), channel_id=1, source_target_pairs={{0,16},{16,0},{32,48},{48,32},{64,80},{80,64},{96,112},{112,96},{1... | collective-permute-start | bytes 73736 | tf_op jit(solution)/shard_map/ppermute | solution.py:623
  16.0 5.7 %collective-permute-start.1 = (f32[24,256]{1,0:T(8,128)}, f32[24,256]{1,0:T(8,128)S(1)}, u32[]{:S(2)}, u32[]{:S(2)}) collective-permute-start(f32[24,256]{1,0:T(8,128)} %get-tuple-element.21), channel_id=1, source_target_pairs={{16,32},{32,16},{48,64},{64,48},{80,96},{96,80},{17,33},{33,17},{4... | collective-permute-start | bytes 73736 | tf_op jit(solution)/shard_map/ppermute | solution.py:624
  30.5 17.8 %all-to-all-start.1 = ((f32[128,8,128]{2,1,0:T(8,128)}), f32[128,8,128]{2,1,0:T(8,128)S(1)}, u32[]{:S(2)}, u32[]{:S(2)}) async-start(f32[128,8,128]{2,1,0:T(8,128)} %legendre.1), calls=%async_computation.1 | async-start | bytes 1048576 | tf_op jit(solution)/shard_map/all_to_all | solution.py:102
  37.2 5.4 %collective-permute-start.2 = (f32[24,128]{1,0:T(8,128)}, f32[24,128]{1,0:T(8,128)S(1)}, u32[]{:S(2)}, u32[]{:S(2)}) collective-permute-start(f32[24,128]{1,0:T(8,128)} %get-tuple-element.29), channel_id=1, source_target_pairs={{0,1},{1,0},{2,3},{3,2},{4,5},{5,4},{6,7},{7,6},{8,9},{9,8},{10,11... | collective-permute-start | bytes 36872 | tf_op jit(solution)/shard_map/ppermute | solution.py:678
  38.7 8.3 %collective-permute-start.3 = (f32[24,128]{1,0:T(8,128)}, f32[24,128]{1,0:T(8,128)S(1)}, u32[]{:S(2)}, u32[]{:S(2)}) collective-permute-start(f32[24,128]{1,0:T(8,128)} %get-tuple-element.30), channel_id=1, source_target_pairs={{0,15},{1,2},{2,1},{3,4},{4,3},{5,6},{6,5},{7,8},{8,7},{9,10},{10,... | collective-permute-start | bytes 36872 | tf_op jit(solution)/shard_map/ppermute | solution.py:679

commit v7 on v6

--- a/solution.py
+++ b/solution.py
@@ -649,7 +649,17 @@
         work=cost(2 << 20, 1 << 20),
         near_out=(0, 1, 2, 3, 4),
     )
-    received, from_near, from_far = lax.optimization_barrier((received, from_near, from_far))
+    to_near, to_far, edges = far_call(
+        column_kernel,
+        "columns",
+        (from_near, from_far, own),
+        (side, side, ((FIELDS, 2 * WIDE, COLS), f32)),
+        [vmem((2, STRIP, 128), f32), copies((2,))],
+        here=(0, 1),
+        near=(2,),
+        near_out=(2,),
+    )
+    received, to_near, to_far = lax.optimization_barrier((received, to_near, to_far))
     table = ((2 * len(PAIRS) * TILE, HALF), bf16)
     (reply,) = far_call(
         legendre_kernel,
@@ -663,16 +673,6 @@
     )
     answer = exchange(reply)
 
-    to_near, to_far, edges = far_call(
-        column_kernel,
-        "columns",
-        (from_near, from_far, own),
-        (side, side, ((FIELDS, 2 * WIDE, COLS), f32)),
-        [vmem((2, STRIP, 128), f32), copies((2,))],
-        here=(0, 1),
-        near=(2,),
-        near_out=(2,),
-    )
     near_lons = [(i, i ^ 1) for i in range(LONS)]
     far_lons = [(i, (((i + 1) ^ 1) - 1) % LONS) for i in range(LONS)]
     side_near = lax.ppermute(to_near, "lon", near_lons)

time: 50.5 us -> 50.6 us (level)
    all_to_all x2, waiting for transfers between devices: 6.45 us -> 5.57 us  [exchange(): lax.all_to_all(messages, ('lat', 'lon'), split_axis=0, concat_axis=0, til...]
    ppermute x1, waiting for transfers between devices: 4.35 us -> 5.2 us  [on_device(): side_far = lax.ppermute(to_far, 'lon', far_lons)]
where the time goes in v7:
time: 50.6 us; the launch traced here: 50.2 us
  starting transfers between devices  26.7 us (53%)
  waiting for transfers between devices  12 us (24%)
  Pallas kernels  10.8 us (21%)
  between operations  0.73 us (1%)
    all_to_all x2, starting transfers between devices, exchange(): lax.all_to_all(messages, ('lat', 'lon'), split_axis=0, concat_axis=0, til...  17.4 us
    pallas_call x5, Pallas kernels, far_call(): pl.pallas_call(kernel, out_shape=tuple((space(*result) for space, result...  10.8 us
    all_to_all x2, waiting for transfers between devices, exchange(): lax.all_to_all(messages, ('lat', 'lon'), split_axis=0, concat_axis=0, til...  5.57 us
    ppermute x1, waiting for transfers between devices, on_device(): side_far = lax.ppermute(to_far, 'lon', far_lons)  5.2 us
    ppermute x1, starting transfers between devices, on_device(): side_far = lax.ppermute(to_far, 'lon', far_lons)  3.93 us
    ppermute x1, starting transfers between devices, on_device(): from_far = lax.ppermute(strip_far, 'lat', far_pairs)  2.73 us
    ppermute x1, starting transfers between devices, on_device(): side_near = lax.ppermute(to_near, 'lon', near_lons)  1.47 us
    ppermute x1, waiting for transfers between devices, on_device(): from_far = lax.ppermute(strip_far, 'lat', far_pairs)  1.24 us
  transfers between devices with their start and end apart: 6, of which 4 were waited for; matrix products, arithmetic and copies ran while one was open for 0% of the time, Pallas kernels for 5%

profile of v7, /device:TPU:1, one launch (start us, length us, event | category | flops | bytes accessed | tf_op | source)
XLA Modules:
  0.0 50.2 jit_solution(10079433293721170926)
XLA Ops:
  0.6 2.7 %forward.1 = (f32[128,8,128]{2,1,0:T(8,128)}, f32[24,256]{1,0:T(8,128)}, f32[24,256]{1,0:T(8,128)}, bf16[4,4,256,256]{3,2,1,0:T(8,128)(2,1)S(1)}) custom-call(f32[64,256]{1,0:T(8,128)} %height_in.3, f32[64,256]{1,0:T(8,128)} %flux_u_in.3, f32[64,256]{1,0:T(8,128)} %flux_v_in.3, f32[64,256]{1,0:T(8,128)} %depth_in.3, s32[64,256]{1,0:T(8,128)} %mask_in.3, ...), custom_call_target="tpu_custom_call" | custom-call | flops 805306368 | bytes 3145728 | tf_op jit(solution)/shard_map/forward/pallas_call | solution.py:571
  3.4 0.0 copy-start
  3.4 11.5 %all-to-all-start = ((f32[128,8,128]{2,1,0:T(8,128)}), f32[128,8,128]{2,1,0:T(8,128)S(1)}, u32[]{:S(2)}, u32[]{:S(2)}) async-start(f32[128,8,128]{2,1,0:T(8,128)} %get-tuple-element.19), calls=%async_computation | async-start | bytes 1048576 | tf_op jit(solution)/shard_map/all_to_all | solution.py:102
  14.9 1.1 %collective-permute-start = (f32[24,256]{1,0:T(8,128)}, f32[24,256]{1,0:T(8,128)S(1)}, u32[]{:S(2)}, u32[]{:S(2)}) collective-permute-start(f32[24,256]{1,0:T(8,128)} %get-tuple-element.20), channel_id=1, source_target_pairs={{0,16},{16,0},{32,48},{48,32},{64,80},{80,64},{96,112},{112,96},{1... | collective-permute-start | bytes 73736 | tf_op jit(solution)/shard_map/ppermute | solution.py:623
  16.0 2.7 %collective-permute-start.1 = (f32[24,256]{1,0:T(8,128)}, f32[24,256]{1,0:T(8,128)S(1)}, u32[]{:S(2)}, u32[]{:S(2)}) collective-permute-start(f32[24,256]{1,0:T(8,128)} %get-tuple-element.21), channel_id=1, source_target_pairs={{16,32},{32,16},{48,64},{64,48},{80,96},{96,80},{17,33},{33,17},{4... | collective-permute-start | bytes 73736 | tf_op jit(solution)/shard_map/ppermute | solution.py:624
  18.8 1.7 %setup.1 = (f32[22,8,256]{2,1,0:T(8,128)S(1)}, f32[8,1024]{1,0:T(8,128)S(1)}, f32[8,256]{1,0:T(8,128)S(1)}, f32[6,64,256]{2,1,0:T(8,128)S(1)}, f32[2,72,128]{2,1,0:T(8,128)S(1)}) custom-call(f32[64,256]{1,0:T(8,128)} %height_in.3, f32[64,256]{1,0:T(8,128)} %flux_u_in.3, f32[64,256]{1,0:T(8,128)} %flux_v_in.3, f32[64,256]{1,0:T(8,128)} %depth_in.3, ...), custom_call_target="tpu_custom_call" | custom-call | flops 2097152 | bytes 1048576 | tf_op jit(solution)/shard_map/setup/pallas_call | solution.py:571
  20.5 0.0 collective-permute-done.from_near
  20.5 1.2 %collective-permute-done.1.from_far = f32[24,256]{1,0:T(8,128)S(1)} collective-permute-done((f32[24,256]{1,0:T(8,128)}, f32[24,256]{1,0:T(8,128)S(1)}, u32[]{:S(2)}, u32[]{:S(2)}) %collective-permute-start.1) | collective-permute-done | bytes 24608 | tf_op jit(solution)/shard_map/ppermute | solution.py:624
  21.7 0.8 %columns.1 = (f32[24,128]{1,0:T(8,128)}, f32[24,128]{1,0:T(8,128)}, f32[6,8,256]{2,1,0:T(8,128)S(1)}) custom-call(f32[24,256]{1,0:T(8,128)S(1)} %collective-permute-done.from_near, f32[24,256]{1,0:T(8,128)S(1)} %collective-permute-done.1.from_far, f32[6,64,256]{2,1,0:T(8,128)S(1)} %get-tuple-element.22.own), custom_call_target="tpu_custom_call" | custom-call | tf_op jit(solution)/shard_map/columns/pallas_call | solution.py:571
  22.6 0.0 copy-start.2
  22.6 0.0 copy-start.1
  22.6 4.2 %all-to-all-done.received = f32[128,8,128]{2,1,0:T(8,128)S(1)} async-done(((f32[128,8,128]{2,1,0:T(8,128)}), f32[128,8,128]{2,1,0:T(8,128)S(1)}, u32[]{:S(2)}, u32[]{:S(2)}) %all-to-all-start) | async-done | bytes 524320 | tf_op jit(solution)/shard_map/all_to_all | solution.py:102
  26.8 0.0 copy-done
  26.8 3.7 %legendre.1 = f32[128,8,128]{2,1,0:T(8,128)} custom-call(f32[128,8,128]{2,1,0:T(8,128)S(1)} %all-to-all-done.received, f32[22,8,256]{2,1,0:T(8,128)S(1)} %get-tuple-element.26.gains, f32[8,1024]{1,0:T(8,128)S(1)} %get-tuple-element.27.balance, f32[8,256]{1,0:T(8,128)S(1)} %get-tuple-element.28.start, f32[3,8,256]{2,1,0:T(8,128)S(1)} %copy-done), custom_call_target="tpu_custom_call" | custom-call | flops 1610612736 | bytes 9437184 | tf_op jit(solution)/shard_map/legendre/pallas_call | solution.py:571
  30.5 5.9 %all-to-all-start.1 = ((f32[128,8,128]{2,1,0:T(8,128)}), f32[128,8,128]{2,1,0:T(8,128)S(1)}, u32[]{:S(2)}, u32[]{:S(2)}) async-start(f32[128,8,128]{2,1,0:T(8,128)} %legendre.1), calls=%async_computation.1 | async-start | bytes 1048576 | tf_op jit(solution)/shard_map/all_to_all | solution.py:102
  36.4 0.0 copy-done.2
  36.4 1.5 %collective-permute-start.2 = (f32[24,128]{1,0:T(8,128)S(1)}, f32[24,128]{1,0:T(8,128)S(1)}, u32[]{:S(2)}, u32[]{:S(2)}) collective-permute-start(f32[24,128]{1,0:T(8,128)S(1)} %copy-done.2), channel_id=1, source_target_pairs={{0,1},{1,0},{2,3},{3,2},{4,5},{5,4},{6,7},{7,6},{8,9},{9,8},{10,11... | collective-permute-start | bytes 36872 | tf_op jit(solution)/shard_map/ppermute | solution.py:678
  37.9 0.0 copy-done.1
  37.9 3.9 %collective-permute-start.3 = (f32[24,128]{1,0:T(8,128)S(1)}, f32[24,128]{1,0:T(8,128)S(1)}, u32[]{:S(2)}, u32[]{:S(2)}) collective-permute-start(f32[24,128]{1,0:T(8,128)S(1)} %copy-done.1), channel_id=1, source_target_pairs={{0,15},{1,2},{2,1},{3,4},{4,3},{5,6},{6,5},{7,8},{8,7},{9,10},{10,... | collective-permute-start | bytes 36872 | tf_op jit(solution)/shard_map/ppermute | solution.py:679
  41.8 0.0 collective-permute-done.2.from_near
  41.8 5.2 %collective-permute-done.3.from_far = f32[24,128]{1,0:T(8,128)S(1)} collective-permute-done((f32[24,128]{1,0:T(8,128)S(1)}, f32[24,128]{1,0:T(8,128)S(1)}, u32[]{:S(2)}, u32[]{:S(2)}) %collective-permute-start.3) | collective-permute-done | bytes 12320 | tf_op jit(solution)/shard_map/ppermute | solution.py:679
  47.0 1.3 %all-to-all-done.1.received = f32[128,8,128]{2,1,0:T(8,128)S(1)} async-done(((f32[128,8,128]{2,1,0:T(8,128)}), f32[128,8,128]{2,1,0:T(8,128)S(1)}, u32[]{:S(2)}, u32[]{:S(2)}) %all-to-all-start.1) | async-done | bytes 524320 | tf_op jit(solution)/shard_map/all_to_all | solution.py:102
  48.4 1.9 %finish.1 = (f32[64,256]{1,0:T(8,128)}, f32[64,256]{1,0:T(8,128)}, f32[64,256]{1,0:T(8,128)}, f32[64,256]{1,0:T(8,128)}) custom-call(f32[128,8,128]{2,1,0:T(8,128)S(1)} %all-to-all-done.1.received, f32[24,128]{1,0:T(8,128)S(1)} %collective-permute-done.2.from_near, f32[24,128]{1,0:T(8,128)S(1)} %collective-permute-done.3.from_far, ...), custom_call_target="tpu_custom_call" | custom-call | tf_op jit(solution)/shard_map/finish/pallas_call | solution.py:571
Async XLA Ops:
  3.4 23.5 %copy-start = (f32[3,8,256]{2,1,0:T(8,128)S(1)}, f32[3,8,256]{2,1,0:T(8,128)}, u32[]{:S(2)}) copy-start(f32[3,8,256]{2,1,0:T(8,128)} %constant.14.clone.north_in.north) | copy-start | bytes 73732
  3.4 23.5 %all-to-all-start = ((f32[128,8,128]{2,1,0:T(8,128)}), f32[128,8,128]{2,1,0:T(8,128)S(1)}, u32[]{:S(2)}, u32[]{:S(2)}) async-start(f32[128,8,128]{2,1,0:T(8,128)} %get-tuple-element.19), calls=%async_computation | async-start | bytes 1048576 | tf_op jit(solution)/shard_map/all_to_all | solution.py:102
  14.9 5.6 %collective-permute-start = (f32[24,256]{1,0:T(8,128)}, f32[24,256]{1,0:T(8,128)S(1)}, u32[]{:S(2)}, u32[]{:S(2)}) collective-permute-start(f32[24,256]{1,0:T(8,128)} %get-tuple-element.20), channel_id=1, source_target_pairs={{0,16},{16,0},{32,48},{48,32},{64,80},{80,64},{96,112},{112,96},{1... | collective-permute-start | bytes 73736 | tf_op jit(solution)/shard_map/ppermute | solution.py:623
  16.0 5.7 %collective-permute-start.1 = (f32[24,256]{1,0:T(8,128)}, f32[24,256]{1,0:T(8,128)S(1)}, u32[]{:S(2)}, u32[]{:S(2)}) collective-permute-start(f32[24,256]{1,0:T(8,128)} %get-tuple-element.21), channel_id=1, source_target_pairs={{16,32},{32,16},{48,64},{64,48},{80,96},{96,80},{17,33},{33,17},{4... | collective-permute-start | bytes 73736 | tf_op jit(solution)/shard_map/ppermute | solution.py:624
  22.6 13.9 %copy-start.2 = (f32[24,128]{1,0:T(8,128)S(1)}, f32[24,128]{1,0:T(8,128)}, u32[]{:S(2)}) copy-start(f32[24,128]{1,0:T(8,128)} %get-tuple-element.29) | copy-start | bytes 36868
  22.6 15.3 %copy-start.1 = (f32[24,128]{1,0:T(8,128)S(1)}, f32[24,128]{1,0:T(8,128)}, u32[]{:S(2)}) copy-start(f32[24,128]{1,0:T(8,128)} %get-tuple-element.30) | copy-start | bytes 36868
  30.5 17.9 %all-to-all-start.1 = ((f32[128,8,128]{2,1,0:T(8,128)}), f32[128,8,128]{2,1,0:T(8,128)S(1)}, u32[]{:S(2)}, u32[]{:S(2)}) async-start(f32[128,8,128]{2,1,0:T(8,128)} %legendre.1), calls=%async_computation.1 | async-start | bytes 1048576 | tf_op jit(solution)/shard_map/all_to_all | solution.py:102
  36.4 5.4 %collective-permute-start.2 = (f32[24,128]{1,0:T(8,128)S(1)}, f32[24,128]{1,0:T(8,128)S(1)}, u32[]{:S(2)}, u32[]{:S(2)}) collective-permute-start(f32[24,128]{1,0:T(8,128)S(1)} %copy-done.2), channel_id=1, source_target_pairs={{0,1},{1,0},{2,3},{3,2},{4,5},{5,4},{6,7},{7,6},{8,9},{9,8},{10,11... | collective-permute-start | bytes 36872 | tf_op jit(solution)/shard_map/ppermute | solution.py:678
  37.9 9.1 %collective-permute-start.3 = (f32[24,128]{1,0:T(8,128)S(1)}, f32[24,128]{1,0:T(8,128)S(1)}, u32[]{:S(2)}, u32[]{:S(2)}) collective-permute-start(f32[24,128]{1,0:T(8,128)S(1)} %copy-done.1), channel_id=1, source_target_pairs={{0,15},{1,2},{2,1},{3,4},{4,3},{5,6},{6,5},{7,8},{8,7},{9,10},{10,... | collective-permute-start | bytes 36872 | tf_op jit(solution)/shard_map/ppermute | solution.py:679

commit v8 on v7

--- a/solution.py
+++ b/solution.py
@@ -494,9 +494,6 @@
         both += dot_nn(cos_both[:, place], wave[part, 0]) + dot_nn(sin_both[:, place], wave[part, 1])
         field += dot_nn(high[:64, place], wave[part, 2]) + dot_nn(high[64:, place], wave[part, 3])
     field = field + both[:64] + both[64:]
-    field_high, field_low = halves(field)
-    order = row_order(lat_index).astype(bf16)
-    field = dot_nn(order, field_high) + dot_nn(order, field_low)
 
     def eastward(values):
         return pltpu.roll(values, PAD_COLS - 1, 1)
@@ -521,9 +518,14 @@
         v_now = open_v * v_now - pull_v * (northward(height_now) - height_now)
     for slot, values in enumerate((height_now, u_now, v_now)):
         results[slot] = values[:ROWS, :COLS]
+    pairs = zip((results.at[0], results.at[1], results.at[2]), (height_out, u_out, v_out))
+    sends = fetch(pairs, out_sems)
+    field_high, field_low = halves(field)
+    order = row_order(lat_index).astype(bf16)
+    field = dot_nn(order, field_high) + dot_nn(order, field_low)
     results[3] = field * sea[:ROWS, :COLS]
-    outs = (height_out, u_out, v_out, sal_out)
-    for copy in fetch([(results.at[slot], out) for slot, out in enumerate(outs)], out_sems):
+    sends += fetch(((results.at[3], sal_out),), out_sems.at[pl.ds(3, 1)])
+    for copy in sends:
         copy.wait()
 
 

time: 50.6 us -> 50.6 us (level)
  no operation moved by 1% of the time
where the time goes in v8:
time: 50.6 us; the launch traced here: 50.2 us
  starting transfers between devices  26.7 us (53%)
  waiting for transfers between devices  12 us (24%)
  Pallas kernels  10.8 us (21%)
  between operations  0.73 us (1%)
    all_to_all x2, starting transfers between devices, exchange(): lax.all_to_all(messages, ('lat', 'lon'), split_axis=0, concat_axis=0, til...  17.4 us
    pallas_call x5, Pallas kernels, far_call(): pl.pallas_call(kernel, out_shape=tuple((space(*result) for space, result...  10.8 us
    all_to_all x2, waiting for transfers between devices, exchange(): lax.all_to_all(messages, ('lat', 'lon'), split_axis=0, concat_axis=0, til...  5.57 us
    ppermute x1, waiting for transfers between devices, on_device(): side_far = lax.ppermute(to_far, 'lon', far_lons)  5.2 us
    ppermute x1, starting transfers between devices, on_device(): side_far = lax.ppermute(to_far, 'lon', far_lons)  3.93 us
    ppermute x1, starting transfers between devices, on_device(): from_far = lax.ppermute(strip_far, 'lat', far_pairs)  2.73 us
    ppermute x1, starting transfers between devices, on_device(): side_near = lax.ppermute(to_near, 'lon', near_lons)  1.47 us
    ppermute x1, waiting for transfers between devices, on_device(): from_far = lax.ppermute(strip_far, 'lat', far_pairs)  1.24 us
  transfers between devices with their start and end apart: 6, of which 4 were waited for; matrix products, arithmetic and copies ran while one was open for 0% of the time, Pallas kernels for 5%

profile of v8, /device:TPU:1, one launch (start us, length us, event | category | flops | bytes accessed | tf_op | source)
XLA Modules:
  0.0 50.2 jit_solution(17556844428953335793)
XLA Ops:
  0.6 2.7 %forward.1 = (f32[128,8,128]{2,1,0:T(8,128)}, f32[24,256]{1,0:T(8,128)}, f32[24,256]{1,0:T(8,128)}, bf16[4,4,256,256]{3,2,1,0:T(8,128)(2,1)S(1)}) custom-call(f32[64,256]{1,0:T(8,128)} %height_in.3, f32[64,256]{1,0:T(8,128)} %flux_u_in.3, f32[64,256]{1,0:T(8,128)} %flux_v_in.3, f32[64,256]{1,0:T(8,128)} %depth_in.3, s32[64,256]{1,0:T(8,128)} %mask_in.3, ...), custom_call_target="tpu_custom_call" | custom-call | flops 805306368 | bytes 3145728 | tf_op jit(solution)/shard_map/forward/pallas_call | solution.py:573
  3.4 0.0 copy-start
  3.4 11.5 %all-to-all-start = ((f32[128,8,128]{2,1,0:T(8,128)}), f32[128,8,128]{2,1,0:T(8,128)S(1)}, u32[]{:S(2)}, u32[]{:S(2)}) async-start(f32[128,8,128]{2,1,0:T(8,128)} %get-tuple-element.19), calls=%async_computation | async-start | bytes 1048576 | tf_op jit(solution)/shard_map/all_to_all | solution.py:102
  14.9 1.1 %collective-permute-start = (f32[24,256]{1,0:T(8,128)}, f32[24,256]{1,0:T(8,128)S(1)}, u32[]{:S(2)}, u32[]{:S(2)}) collective-permute-start(f32[24,256]{1,0:T(8,128)} %get-tuple-element.20), channel_id=1, source_target_pairs={{0,16},{16,0},{32,48},{48,32},{64,80},{80,64},{96,112},{112,96},{1... | collective-permute-start | bytes 73736 | tf_op jit(solution)/shard_map/ppermute | solution.py:625
  16.0 2.7 %collective-permute-start.1 = (f32[24,256]{1,0:T(8,128)}, f32[24,256]{1,0:T(8,128)S(1)}, u32[]{:S(2)}, u32[]{:S(2)}) collective-permute-start(f32[24,256]{1,0:T(8,128)} %get-tuple-element.21), channel_id=1, source_target_pairs={{16,32},{32,16},{48,64},{64,48},{80,96},{96,80},{17,33},{33,17},{4... | collective-permute-start | bytes 73736 | tf_op jit(solution)/shard_map/ppermute | solution.py:626
  18.8 1.7 %setup.1 = (f32[22,8,256]{2,1,0:T(8,128)S(1)}, f32[8,1024]{1,0:T(8,128)S(1)}, f32[8,256]{1,0:T(8,128)S(1)}, f32[6,64,256]{2,1,0:T(8,128)S(1)}, f32[2,72,128]{2,1,0:T(8,128)S(1)}) custom-call(f32[64,256]{1,0:T(8,128)} %height_in.3, f32[64,256]{1,0:T(8,128)} %flux_u_in.3, f32[64,256]{1,0:T(8,128)} %flux_v_in.3, f32[64,256]{1,0:T(8,128)} %depth_in.3, ...), custom_call_target="tpu_custom_call" | custom-call | flops 2097152 | bytes 1048576 | tf_op jit(solution)/shard_map/setup/pallas_call | solution.py:573
  20.5 0.0 collective-permute-done.from_near
  20.5 1.2 %collective-permute-done.1.from_far = f32[24,256]{1,0:T(8,128)S(1)} collective-permute-done((f32[24,256]{1,0:T(8,128)}, f32[24,256]{1,0:T(8,128)S(1)}, u32[]{:S(2)}, u32[]{:S(2)}) %collective-permute-start.1) | collective-permute-done | bytes 24608 | tf_op jit(solution)/shard_map/ppermute | solution.py:626
  21.7 0.8 %columns.1 = (f32[24,128]{1,0:T(8,128)}, f32[24,128]{1,0:T(8,128)}, f32[6,8,256]{2,1,0:T(8,128)S(1)}) custom-call(f32[24,256]{1,0:T(8,128)S(1)} %collective-permute-done.from_near, f32[24,256]{1,0:T(8,128)S(1)} %collective-permute-done.1.from_far, f32[6,64,256]{2,1,0:T(8,128)S(1)} %get-tuple-element.22.own), custom_call_target="tpu_custom_call" | custom-call | tf_op jit(solution)/shard_map/columns/pallas_call | solution.py:573
  22.6 0.0 copy-start.2
  22.6 0.0 copy-start.1
  22.6 4.2 %all-to-all-done.received = f32[128,8,128]{2,1,0:T(8,128)S(1)} async-done(((f32[128,8,128]{2,1,0:T(8,128)}), f32[128,8,128]{2,1,0:T(8,128)S(1)}, u32[]{:S(2)}, u32[]{:S(2)}) %all-to-all-start) | async-done | bytes 524320 | tf_op jit(solution)/shard_map/all_to_all | solution.py:102
  26.8 0.0 copy-done
  26.8 3.7 %legendre.1 = f32[128,8,128]{2,1,0:T(8,128)} custom-call(f32[128,8,128]{2,1,0:T(8,128)S(1)} %all-to-all-done.received, f32[22,8,256]{2,1,0:T(8,128)S(1)} %get-tuple-element.26.gains, f32[8,1024]{1,0:T(8,128)S(1)} %get-tuple-element.27.balance, f32[8,256]{1,0:T(8,128)S(1)} %get-tuple-element.28.start, f32[3,8,256]{2,1,0:T(8,128)S(1)} %copy-done), custom_call_target="tpu_custom_call" | custom-call | flops 1610612736 | bytes 9437184 | tf_op jit(solution)/shard_map/legendre/pallas_call | solution.py:573
  30.5 5.9 %all-to-all-start.1 = ((f32[128,8,128]{2,1,0:T(8,128)}), f32[128,8,128]{2,1,0:T(8,128)S(1)}, u32[]{:S(2)}, u32[]{:S(2)}) async-start(f32[128,8,128]{2,1,0:T(8,128)} %legendre.1), calls=%async_computation.1 | async-start | bytes 1048576 | tf_op jit(solution)/shard_map/all_to_all | solution.py:102
  36.4 0.0 copy-done.2
  36.4 1.5 %collective-permute-start.2 = (f32[24,128]{1,0:T(8,128)S(1)}, f32[24,128]{1,0:T(8,128)S(1)}, u32[]{:S(2)}, u32[]{:S(2)}) collective-permute-start(f32[24,128]{1,0:T(8,128)S(1)} %copy-done.2), channel_id=1, source_target_pairs={{0,1},{1,0},{2,3},{3,2},{4,5},{5,4},{6,7},{7,6},{8,9},{9,8},{10,11... | collective-permute-start | bytes 36872 | tf_op jit(solution)/shard_map/ppermute | solution.py:680
  37.9 0.0 copy-done.1
  37.9 3.9 %collective-permute-start.3 = (f32[24,128]{1,0:T(8,128)S(1)}, f32[24,128]{1,0:T(8,128)S(1)}, u32[]{:S(2)}, u32[]{:S(2)}) collective-permute-start(f32[24,128]{1,0:T(8,128)S(1)} %copy-done.1), channel_id=1, source_target_pairs={{0,15},{1,2},{2,1},{3,4},{4,3},{5,6},{6,5},{7,8},{8,7},{9,10},{10,... | collective-permute-start | bytes 36872 | tf_op jit(solution)/shard_map/ppermute | solution.py:681
  41.8 0.0 collective-permute-done.2.from_near
  41.8 5.2 %collective-permute-done.3.from_far = f32[24,128]{1,0:T(8,128)S(1)} collective-permute-done((f32[24,128]{1,0:T(8,128)S(1)}, f32[24,128]{1,0:T(8,128)S(1)}, u32[]{:S(2)}, u32[]{:S(2)}) %collective-permute-start.3) | collective-permute-done | bytes 12320 | tf_op jit(solution)/shard_map/ppermute | solution.py:681
  47.0 1.3 %all-to-all-done.1.received = f32[128,8,128]{2,1,0:T(8,128)S(1)} async-done(((f32[128,8,128]{2,1,0:T(8,128)}), f32[128,8,128]{2,1,0:T(8,128)S(1)}, u32[]{:S(2)}, u32[]{:S(2)}) %all-to-all-start.1) | async-done | bytes 524320 | tf_op jit(solution)/shard_map/all_to_all | solution.py:102
  48.4 1.9 %finish.1 = (f32[64,256]{1,0:T(8,128)}, f32[64,256]{1,0:T(8,128)}, f32[64,256]{1,0:T(8,128)}, f32[64,256]{1,0:T(8,128)}) custom-call(f32[128,8,128]{2,1,0:T(8,128)S(1)} %all-to-all-done.1.received, f32[24,128]{1,0:T(8,128)S(1)} %collective-permute-done.2.from_near, f32[24,128]{1,0:T(8,128)S(1)} %collective-permute-done.3.from_far, ...), custom_call_target="tpu_custom_call" | custom-call | tf_op jit(solution)/shard_map/finish/pallas_call | solution.py:573
Async XLA Ops:
  3.4 23.5 %copy-start = (f32[3,8,256]{2,1,0:T(8,128)S(1)}, f32[3,8,256]{2,1,0:T(8,128)}, u32[]{:S(2)}) copy-start(f32[3,8,256]{2,1,0:T(8,128)} %constant.14.clone.north_in.north) | copy-start | bytes 73732
  3.4 23.5 %all-to-all-start = ((f32[128,8,128]{2,1,0:T(8,128)}), f32[128,8,128]{2,1,0:T(8,128)S(1)}, u32[]{:S(2)}, u32[]{:S(2)}) async-start(f32[128,8,128]{2,1,0:T(8,128)} %get-tuple-element.19), calls=%async_computation | async-start | bytes 1048576 | tf_op jit(solution)/shard_map/all_to_all | solution.py:102
  14.9 5.6 %collective-permute-start = (f32[24,256]{1,0:T(8,128)}, f32[24,256]{1,0:T(8,128)S(1)}, u32[]{:S(2)}, u32[]{:S(2)}) collective-permute-start(f32[24,256]{1,0:T(8,128)} %get-tuple-element.20), channel_id=1, source_target_pairs={{0,16},{16,0},{32,48},{48,32},{64,80},{80,64},{96,112},{112,96},{1... | collective-permute-start | bytes 73736 | tf_op jit(solution)/shard_map/ppermute | solution.py:625
  16.0 5.7 %collective-permute-start.1 = (f32[24,256]{1,0:T(8,128)}, f32[24,256]{1,0:T(8,128)S(1)}, u32[]{:S(2)}, u32[]{:S(2)}) collective-permute-start(f32[24,256]{1,0:T(8,128)} %get-tuple-element.21), channel_id=1, source_target_pairs={{16,32},{32,16},{48,64},{64,48},{80,96},{96,80},{17,33},{33,17},{4... | collective-permute-start | bytes 73736 | tf_op jit(solution)/shard_map/ppermute | solution.py:626
  22.6 13.9 %copy-start.2 = (f32[24,128]{1,0:T(8,128)S(1)}, f32[24,128]{1,0:T(8,128)}, u32[]{:S(2)}) copy-start(f32[24,128]{1,0:T(8,128)} %get-tuple-element.29) | copy-start | bytes 36868
  22.6 15.3 %copy-start.1 = (f32[24,128]{1,0:T(8,128)S(1)}, f32[24,128]{1,0:T(8,128)}, u32[]{:S(2)}) copy-start(f32[24,128]{1,0:T(8,128)} %get-tuple-element.30) | copy-start | bytes 36868
  30.5 17.9 %all-to-all-start.1 = ((f32[128,8,128]{2,1,0:T(8,128)}), f32[128,8,128]{2,1,0:T(8,128)S(1)}, u32[]{:S(2)}, u32[]{:S(2)}) async-start(f32[128,8,128]{2,1,0:T(8,128)} %legendre.1), calls=%async_computation.1 | async-start | bytes 1048576 | tf_op jit(solution)/shard_map/all_to_all | solution.py:102
  36.4 5.4 %collective-permute-start.2 = (f32[24,128]{1,0:T(8,128)S(1)}, f32[24,128]{1,0:T(8,128)S(1)}, u32[]{:S(2)}, u32[]{:S(2)}) collective-permute-start(f32[24,128]{1,0:T(8,128)S(1)} %copy-done.2), channel_id=1, source_target_pairs={{0,1},{1,0},{2,3},{3,2},{4,5},{5,4},{6,7},{7,6},{8,9},{9,8},{10,11... | collective-permute-start | bytes 36872 | tf_op jit(solution)/shard_map/ppermute | solution.py:680
  37.9 9.1 %collective-permute-start.3 = (f32[24,128]{1,0:T(8,128)S(1)}, f32[24,128]{1,0:T(8,128)S(1)}, u32[]{:S(2)}, u32[]{:S(2)}) collective-permute-start(f32[24,128]{1,0:T(8,128)S(1)} %copy-done.1), channel_id=1, source_target_pairs={{0,15},{1,2},{2,1},{3,4},{4,3},{5,6},{6,5},{7,8},{8,7},{9,10},{10,... | collective-permute-start | bytes 36872 | tf_op jit(solution)/shard_map/ppermute | solution.py:681
